TPU v7x, 32 devices: a whole 2x2x4 slice. The times are simulated.
32 devices in a mesh: section: 2 (over core), dp: 4 (over y, x), ctx: 4 (over z).
Axes of the slice: x: 2, y: 2, z: 4, core: 2. Of those that a mesh axis runs over, the one named last changes fastest.
Arguments:
- ends: bfloat16 [2, 8, 1024, 768], P('section', 'dp', 'ctx'), may hold values from -6 to 6
- segment_ids: int32 [8, 1024], P('dp', 'ctx'), may hold values from 0 to 3, as said below
- ln1_gain: float32 [2, 768], P('section'), may hold values from 0.5 to 1.5
- ln1_bias: float32 [2, 768], P('section'), may hold values from -1.5 to 1.5
- qkv_weight: bfloat16 [2, 768, 1920], P('section'), may hold values from -0.21875 to 0.21875
- out_weight: bfloat16 [2, 768, 768], P('section'), may hold values from -0.875 to 0.875
- ln2_gain: float32 [2, 768], P('section'), may hold values from 0.5 to 1.5
- ln2_bias: float32 [2, 768], P('section'), may hold values from -1.5 to 1.5
- fc_weight: bfloat16 [2, 768, 3072], P('section'), may hold values from -0.21875 to 0.21875
- fc_bias: float32 [2, 3072], P('section'), may hold values from -2.5 to 2.5
- proj_weight: bfloat16 [2, 3072, 768], P('section'), may hold values from -0.109375 to 0.109375
- shared_weight: bfloat16 [768, 384], replicated, may hold values from -0.21875 to 0.21875
Outputs:
- block_ends: float32 [2, 8, 1024, 768], P('section', 'dp', 'ctx')
- qkv_grad: float32 [2, 768, 1920], P('section', ('dp', 'ctx'))
- out_grad: float32 [2, 768, 768], P('section', ('dp', 'ctx'))
- fc_grad: float32 [2, 768, 3072], P('section', ('dp', 'ctx'))
- fc_bias_grad: float32 [2, 3072], P('section', ('dp', 'ctx'))
- proj_grad: float32 [2, 3072, 768], P('section', ('dp', 'ctx'))
- shared_grad: float32 [768, 384], P(('dp', 'ctx'))
- ln1_gain_grad: float32 [2, 768], P('section', ('dp', 'ctx'))
- ln1_bias_grad: float32 [2, 768], P('section', ('dp', 'ctx'))
- ln2_gain_grad: float32 [2, 768], P('section', ('dp', 'ctx'))
- ln2_bias_grad: float32 [2, 768], P('section', ('dp', 'ctx'))
Inputs may be any that keep to these rules, and one draw needn't show every extreme that they name: `segment_ids`: along each row the ids start at 0 and rise by 0 or 1 from one position to the next; each row holds either one document or exactly 4; in each aligned block of 2 rows exactly one row holds a single document.
All inputs are finite; a program needn't handle non-finite values.
Results may differ from a plain program's by a relative error of at most 0.024.
Values may be sent and summed in bfloat16 or wider, within the bound.
A program may use at most 256 MiB of HBM per device.

v0:
```python
import jax
import jax.numpy as jnp
from jax import lax
from jax.sharding import PartitionSpec as P

HEADS = 12
HEAD = 64


EPSILON = 1e-05
MASKED = -1000000000.0


def passed_along(block, axis, distance):
    devices = range(lax.axis_size(axis))
    route = [(i - distance, i) for i in devices if i - distance in devices]
    return lax.ppermute(block, axis, route)


def layer_norm(values, gain, bias):
    row_mean = jnp.mean(values, axis=-1, keepdims=True)
    centred = values - row_mean
    spread = jnp.mean(centred * centred, axis=-1, keepdims=True)
    return centred * lax.rsqrt(spread + EPSILON) * gain + bias


def gelu_tanh(inputs):
    return (
        0.5
        * inputs
        * (1.0 + jnp.tanh(0.7978845608028654 * (inputs + 0.044715 * inputs * inputs * inputs)))
    )


def product(left, right):
    return jnp.dot(left, right, preferred_element_type=jnp.float32)


def transposed(left, right):
    return lax.dot_general(
        left, right, (((1,), (1,)), ((), ())), preferred_element_type=jnp.float32
    )


def inner_rows(left, right):
    return lax.dot_general(
        left, right, (((0,), (0,)), ((), ())), preferred_element_type=jnp.float32
    )


def gather_keys(parts):
    return (
        lax.all_gather(parts[0], "ctx", axis=0, tiled=True),
        lax.all_gather(parts[1], "ctx", axis=0, tiled=True),
        lax.all_gather(parts[2], "ctx", axis=0, tiled=True),
    )


def masked_scores(queries, all_keys, segment, all_segments):
    span_rows = queries.shape[0]
    length = all_keys.shape[0]
    query_place = lax.axis_index("ctx") * span_rows + jnp.arange(span_rows)
    allowed = (jnp.arange(length)[None, :] <= query_place[:, None]) & (
        all_segments[None, :] == segment[:, None]
    )
    scores = jnp.einsum(
        "qhd,khd->hqk",
        queries.reshape(span_rows, HEADS, HEAD),
        all_keys.reshape(length, HEADS, HEAD),
        preferred_element_type=jnp.float32,
    ) * HEAD ** (-0.5)
    return jnp.where(allowed[None], scores, MASKED)


def forward(resid, source_in, is_first, segment, weights, collect):
    gain1, bias1, qkv_w, out_w, gain2, bias2, fc_w, fc_b, proj_w, shared_w = weights
    span_rows, model_width = resid.shape
    normed = layer_norm(resid, gain1, bias1).astype(jnp.bfloat16)
    source = jnp.where(is_first, normed, source_in)
    packed = product(normed, qkv_w).astype(jnp.bfloat16)
    reused = product(source, shared_w).astype(jnp.bfloat16)
    queries = packed[:, :model_width]
    keys_local = packed[:, model_width : 2 * model_width]
    values = jnp.concatenate([reused, packed[:, 2 * model_width :]], axis=1)
    all_keys, all_values, all_segments = collect((keys_local, values, segment))
    length = all_keys.shape[0]
    scores = masked_scores(queries, all_keys, segment, all_segments)
    row_top = jnp.max(scores, axis=-1, keepdims=True)
    exponent = jnp.exp(scores - row_top)
    row_total = jnp.sum(exponent, axis=-1, keepdims=True)
    attn_probs = (exponent / row_total).astype(jnp.bfloat16)
    logsum = row_top + jnp.log(row_total)
    attended = jnp.einsum(
        "hqk,khd->qhd",
        attn_probs,
        all_values.reshape(length, HEADS, HEAD),
        preferred_element_type=jnp.float32,
    )
    attended = attended.reshape(span_rows, model_width).astype(jnp.bfloat16)
    hidden = resid + product(attended, out_w)
    normed2 = layer_norm(hidden, gain2, bias2).astype(jnp.bfloat16)
    up_proj = product(normed2, fc_w) + fc_b
    activated = gelu_tanh(up_proj).astype(jnp.bfloat16)
    result = hidden + product(activated, proj_w)
    stored = dict(
        resid=resid,
        normed=normed,
        source=source,
        queries=queries,
        all_keys=all_keys,
        all_values=all_values,
        all_segments=all_segments,
        segment=segment,
        logsum=logsum,
        attended=attended,
        hidden=hidden,
        normed2=normed2,
        up_proj=up_proj,
        activated=activated,
    )
    return (result, normed, stored)


def backward(stored, grad_out, weights):
    gain1, bias1, qkv_w, out_w, gain2, bias2, fc_w, fc_b, proj_w, shared_w = weights
    span_rows, model_width = grad_out.shape
    half_width = model_width // 2
    scale = HEAD ** (-0.5)
    grad_mlp = grad_out.astype(jnp.bfloat16)
    grad_act = transposed(grad_mlp, proj_w)
    grad_up = jax.vjp(gelu_tanh, stored["up_proj"])[1](grad_act)[0].astype(jnp.bfloat16)
    grad_normed2 = transposed(grad_up, fc_w)
    norm_back = jax.vjp(layer_norm, stored["hidden"], gain2, bias2)[1]
    grad_hidden_norm, grad_gain2, grad_bias2 = norm_back(grad_normed2)
    grad_hidden = grad_out + grad_hidden_norm
    grad_branch = grad_hidden.astype(jnp.bfloat16)
    grad_attended = transposed(grad_branch, out_w).astype(jnp.bfloat16)
    length = stored["all_keys"].shape[0]
    query_heads = stored["queries"].reshape(span_rows, HEADS, HEAD)
    key_heads = stored["all_keys"].reshape(length, HEADS, HEAD)
    value_heads = stored["all_values"].reshape(length, HEADS, HEAD)
    grad_heads = grad_attended.reshape(span_rows, HEADS, HEAD)
    scores = masked_scores(
        stored["queries"], stored["all_keys"], stored["segment"], stored["all_segments"]
    )
    attn_probs = jnp.exp(scores - stored["logsum"])
    grad_probs = jnp.einsum(
        "qhd,khd->hqk", grad_heads, value_heads, preferred_element_type=jnp.float32
    )
    row_delta = jnp.sum(attn_probs * grad_probs, axis=-1, keepdims=True)
    grad_scores = (attn_probs * (grad_probs - row_delta)).astype(jnp.bfloat16)
    grad_queries = (
        jnp.einsum("hqk,khd->qhd", grad_scores, key_heads, preferred_element_type=jnp.float32)
        * scale
    )
    probs_low = attn_probs.astype(jnp.bfloat16)
    grad_values_all = jnp.einsum(
        "hqk,qhd->khd", probs_low, grad_heads, preferred_element_type=jnp.float32
    )
    grad_keys_all = (
        jnp.einsum("hqk,qhd->khd", grad_scores, query_heads, preferred_element_type=jnp.float32)
        * scale
    )
    grad_keys, grad_values = (
        lax.psum_scatter(
            grad_keys_all.reshape(length, model_width).astype(jnp.bfloat16),
            "ctx",
            scatter_dimension=0,
            tiled=True,
        ).astype(jnp.float32),
        lax.psum_scatter(
            grad_values_all.reshape(length, model_width).astype(jnp.bfloat16),
            "ctx",
            scatter_dimension=0,
            tiled=True,
        ).astype(jnp.float32),
    )
    grad_packed = jnp.concatenate(
        [grad_queries.reshape(span_rows, model_width), grad_keys, grad_values[:, half_width:]],
        axis=1,
    ).astype(jnp.bfloat16)
    grad_reused = grad_values[:, :half_width].astype(jnp.bfloat16)
    grad_normed = transposed(grad_packed, qkv_w)
    grad_source = transposed(grad_reused, shared_w)
    operands = (
        (stored["normed"], grad_packed),
        (stored["source"], grad_reused),
        (stored["attended"], grad_branch),
        (stored["normed2"], grad_up),
        (stored["activated"], grad_mlp),
    )
    small = (grad_gain2, grad_bias2, jnp.sum(grad_up.astype(jnp.float32), axis=0))
    return (grad_hidden, grad_normed, grad_source, operands, small)


def shards(
    ends,
    segment_ids,
    ln1_gain,
    ln1_bias,
    qkv_weight,
    out_weight,
    ln2_gain,
    ln2_bias,
    fc_weight,
    fc_bias,
    proj_weight,
    shared_weight,
):
    weights = (
        ln1_gain[0],
        ln1_bias[0],
        qkv_weight[0],
        out_weight[0],
        ln2_gain[0],
        ln2_bias[0],
        fc_weight[0],
        fc_bias[0],
        proj_weight[0],
        shared_weight,
    )
    section_index = lax.axis_index("section")
    is_first = section_index == 0
    is_last = section_index == 1
    micros = ends.shape[1]
    span_rows = ends.shape[2]
    model_width = ends.shape[3]
    local_ends = ends[0]
    slots = jnp.arange(micros)
    recv_resid = jnp.zeros((span_rows, model_width), jnp.bfloat16)
    recv_source = jnp.zeros((span_rows, model_width), jnp.bfloat16)
    back_resid = jnp.zeros((span_rows, model_width), jnp.float32)
    back_source = jnp.zeros((span_rows, model_width), jnp.float32)
    block_out = jnp.zeros((micros, span_rows, model_width), jnp.float32)
    small_sums = (
        jnp.zeros((model_width,), jnp.float32),
        jnp.zeros((model_width,), jnp.float32),
        jnp.zeros((model_width,), jnp.float32),
        jnp.zeros((model_width,), jnp.float32),
        jnp.zeros(fc_bias.shape[1:], jnp.float32),
    )
    input_log = []
    stored_log = []
    operand_log = []

    def pick(later_value, early_value):
        return jnp.where(is_last, later_value, early_value)

    for moment in range(micros + 2):
        if moment <= micros:
            fwd_micro = moment - section_index
            fwd_valid = (fwd_micro >= 0) & (fwd_micro < micros)
            fwd_index = jnp.clip(fwd_micro, 0, micros - 1)
            own_input = lax.dynamic_index_in_dim(local_ends, fwd_index, 0, keepdims=False).astype(
                jnp.float32
            )
            resid = jnp.where(is_first, own_input, recv_resid.astype(jnp.float32))
            segment = lax.dynamic_index_in_dim(segment_ids, fwd_index, 0, keepdims=False)
            result, normed, stored = forward(
                resid, recv_source, is_first, segment, weights, gather_keys
            )
            input_log.append((resid, recv_source, segment))
            stored_log.append(stored)
            write_mask = ((slots == fwd_index) & fwd_valid & is_last).astype(jnp.float32)
            block_out = block_out + write_mask[:, None, None] * result[None]
            if moment < micros:
                recv_resid, recv_source = passed_along(
                    (result.astype(jnp.bfloat16), normed), "section", 1
                )
        if moment >= 1:
            back_micro = moment - 2 + section_index
            back_valid = (back_micro >= 0) & (back_micro < micros)
            back_index = jnp.clip(back_micro, 0, micros - 1)
            current = min(moment, micros)
            earlier = max(moment - 2, 0)
            stored = jax.tree.map(pick, stored_log[current], stored_log[earlier])
            own_grad = lax.dynamic_index_in_dim(local_ends, back_index, 0, keepdims=False).astype(
                jnp.float32
            )
            grad_out = jnp.where(is_first, back_resid, own_grad)
            grad_hidden, grad_normed, grad_source, operands, small = backward(
                stored, grad_out, weights
            )
            normed_total = grad_normed + jnp.where(is_first, grad_source + back_source, 0.0)
            norm_back = jax.vjp(layer_norm, stored["resid"], weights[0], weights[1])[1]
            grad_resid, grad_gain1, grad_bias1 = norm_back(normed_total)
            grad_input = grad_hidden + grad_resid
            if moment <= micros:
                back_resid, back_source = passed_along((grad_input, grad_source), "section", -1)
            write_mask = ((slots == back_index) & back_valid & is_first).astype(jnp.float32)
            block_out = block_out + write_mask[:, None, None] * grad_input[None]
            valid_low = back_valid.astype(jnp.bfloat16)
            valid_wide = back_valid.astype(jnp.float32)
            operand_log.append(
                tuple(((left_side, right_side * valid_low) for left_side, right_side in operands))
            )
            additions = (grad_gain1, grad_bias1, small[0], small[1], small[2])
            small_sums = tuple(
                (total + valid_wide * extra for total, extra in zip(small_sums, additions))
            )

    def weight_grad(slot):
        lefts = jnp.concatenate([logged[slot][0] for logged in operand_log], axis=0)
        rights = jnp.concatenate([logged[slot][1] for logged in operand_log], axis=0)
        return inner_rows(lefts, rights)

    qkv_part = weight_grad(0)
    shared_part = weight_grad(1)
    out_part = weight_grad(2)
    fc_part = weight_grad(3)
    proj_part = weight_grad(4)
    (
        qkv_sum,
        out_sum,
        fc_sum,
        proj_sum,
        shared_sum,
        fcb_sum,
        gain1_sum,
        bias1_sum,
        gain2_sum,
        bias2_sum,
    ) = (
        lax.psum_scatter(qkv_part[None], ("dp", "ctx"), scatter_dimension=1, tiled=True),
        lax.psum_scatter(out_part[None], ("dp", "ctx"), scatter_dimension=1, tiled=True),
        lax.psum_scatter(fc_part[None], ("dp", "ctx"), scatter_dimension=1, tiled=True),
        lax.psum_scatter(proj_part[None], ("dp", "ctx"), scatter_dimension=1, tiled=True),
        lax.psum_scatter(shared_part[None], ("dp", "ctx"), scatter_dimension=1, tiled=True),
        lax.psum_scatter(small_sums[4][None], ("dp", "ctx"), scatter_dimension=1, tiled=True),
        lax.psum_scatter(small_sums[0][None], ("dp", "ctx"), scatter_dimension=1, tiled=True),
        lax.psum_scatter(small_sums[1][None], ("dp", "ctx"), scatter_dimension=1, tiled=True),
        lax.psum_scatter(small_sums[2][None], ("dp", "ctx"), scatter_dimension=1, tiled=True),
        lax.psum_scatter(small_sums[3][None], ("dp", "ctx"), scatter_dimension=1, tiled=True),
    )
    shared_total = lax.psum(shared_sum[0], "section")
    return (
        block_out[None],
        qkv_sum,
        out_sum,
        fc_sum,
        fcb_sum,
        proj_sum,
        shared_total,
        gain1_sum,
        bias1_sum,
        gain2_sum,
        bias2_sum,
    )


def solution(mesh):
    placed = (
        P("section", "dp", "ctx", None),
        P("dp", "ctx"),
        P("section", None),
        P("section", None),
        P("section", None, None),
        P("section", None, None),
        P("section", None),
        P("section", None),
        P("section", None, None),
        P("section", None),
        P("section", None, None),
        P(),
    )
    return jax.shard_map(
        shards,
        mesh=mesh,
        in_specs=placed,
        out_specs=(
            P("section", "dp", "ctx", None),
            P("section", ("dp", "ctx"), None),
            P("section", ("dp", "ctx"), None),
            P("section", ("dp", "ctx"), None),
            P("section", ("dp", "ctx")),
            P("section", ("dp", "ctx"), None),
            P(("dp", "ctx"), None),
            P("section", ("dp", "ctx")),
            P("section", ("dp", "ctx")),
            P("section", ("dp", "ctx")),
            P("section", ("dp", "ctx")),
        ),
        check_vma=False,
    )
```

profile of v0, /device:TPU:1, one launch (start us, length us, event | category | flops | bytes accessed | tf_op | source)
XLA Modules:
  0.0 2044.7 jit_solution(15728449928628770912)
XLA Ops:
  20.4 10.4 all-gather.2
  30.8 6.5 all-gather.1
  37.3 8.4 all-gather
  57.3 3.9 fusion
  61.2 4.6 copy-done.11
  65.9 4.1 fusion.3
  70.0 22.8 %all-gather.10.cloned.1.call-done = bf16[1024,768]{1,0:T(8,128)(2,1)} async-done(((bf16[256,768]{1,0:T(8,128)(2,1)}), bf16[1024,768]{1,0:T(8,128)(2,1)}) %all-gather.10.cloned.1.call-update) | async-done | bytes 1572880 | tf_op jit(solution)/shard_map/all_gather | solution.py:54
  95.4 7.1 fusion.157
  104.0 4.0 fusion.55
  124.8 30.6 %all-gather.16.cloned.1.call-done = bf16[1024,768]{1,0:T(8,128)(2,1)} async-done(((bf16[256,768]{1,0:T(8,128)(2,1)}), bf16[1024,768]{1,0:T(8,128)(2,1)}) %all-gather.16.cloned.1.call-update) | async-done | bytes 1572880 | tf_op jit(solution)/shard_map/all_gather | solution.py:53
  158.0 3.9 fusion.1
  161.9 4.6 copy-done.12
  166.6 4.1 fusion.4
  170.7 22.1 %all-gather.14.cloned.1.call-done = bf16[1024,768]{1,0:T(8,128)(2,1)} async-done(((bf16[256,768]{1,0:T(8,128)(2,1)}), bf16[1024,768]{1,0:T(8,128)(2,1)}) %all-gather.14.cloned.1.call-update) | async-done | bytes 1572880 | tf_op jit(solution)/shard_map/all_gather | solution.py:54
  195.4 7.1 fusion.156
  224.9 8.7 broadcast_multiply_fusion.2
  240.0 17.8 all-gather.20.cloned.1.call-done
  260.6 3.9 fusion.2
  264.6 3.5 fusion.5
  270.5 24.8 %all-gather.18.cloned.1.call-done = bf16[1024,768]{1,0:T(8,128)(2,1)} async-done(((bf16[256,768]{1,0:T(8,128)(2,1)}), bf16[1024,768]{1,0:T(8,128)(2,1)}) %all-gather.18.cloned.1.call-update) | async-done | bytes 1572880 | tf_op jit(solution)/shard_map/all_gather | solution.py:54
  297.9 8.1 broadcast_select_fusion.11
  310.3 4.5 multiply_reduce_fusion.5
  319.5 4.7 broadcast_select_fusion.1
  330.5 5.0 fusion.129
  335.6 4.7 broadcast_select_fusion
  343.1 12.1 multiply_reduce_fusion.2
  356.5 6.8 multiply_convert_fusion.2
  378.8 5.7 fusion.152
  384.6 9.3 broadcast_select_fusion.8
  397.9 8.5 reduce-scatter.27.cloned.1.call-done
  406.5 3.4 multiply_reduce_fusion.8
  413.7 7.6 fusion.296
  422.2 5.1 broadcast_multiply_fusion.1
  434.9 9.0 fusion.132
  446.8 12.4 multiply_reduce_fusion.1
  460.4 6.8 multiply_convert_fusion.1
  479.2 6.1 fusion.153
  489.3 24.8 %reduce-scatter.31.cloned.1.call-done = bf16[256,768]{0,1:T(8,128)(2,1)} async-done(((bf16[1024,768]{0,1:T(8,128)(2,1)}), bf16[256,768]{0,1:T(8,128)(2,1)}) %reduce-scatter.31.cloned.1.call-update) | async-done | bytes 393232 | tf_op jit(solution)/shard_map/reduce_scatter | solution.py:165
  514.1 3.9 multiply_reduce_fusion.7
  521.6 7.9 fusion.297
  530.4 4.8 broadcast_multiply_fusion
  542.8 9.0 fusion.135
  554.9 12.4 multiply_reduce_fusion
  568.5 6.8 multiply_convert_fusion
  580.4 5.2 reduce-scatter.37.cloned.1.call-done
  596.9 3.6 collective-permute-start.7
  610.0 6.1 fusion.154
  616.1 5.9 reduce-scatter.35.cloned.1.call-done
  629.7 4.1 convolution_bitcast_fusion.3
  641.3 107.3 %reduce-scatter.47.cloned.1.call-done = f32[1,48,384]{2,1,0:T(8,128)} async-done(((f32[1,768,384]{2,1,0:T(8,128)}), f32[1,48,384]{2,1,0:T(8,128)}) %reduce-scatter.47.cloned.1.call-update) | async-done | bytes 73744 | tf_op jit(solution)/shard_map/reduce_scatter | solution.py:328
  748.7 7.2 convolution_bitcast_fusion.2
  758.0 10.2 convolution_bitcast_fusion.1
  769.2 10.0 convolution_bitcast_fusion
  779.3 6.3 fusion.149
  785.7 88.2 %reduce-scatter.55.cloned.1.call-done = f32[48,1]{1,0:T(8,128)} async-done(((f32[768,1]{1,0:T(8,128)}), f32[48,1]{1,0:T(8,128)}) %reduce-scatter.55.cloned.1.call-update) | async-done | bytes 208
  875.2 124.6 %reduce-scatter.57.cloned.1.call-done = f32[48,1]{1,0:T(8,128)} async-done(((f32[768,1]{1,0:T(8,128)}), f32[48,1]{1,0:T(8,128)}) %reduce-scatter.57.cloned.1.call-update) | async-done | bytes 208
  1001.2 126.9 %reduce-scatter.49.cloned.1.call-done = f32[192,1]{1,0:T(8,128)} async-done(((f32[3072,1]{1,0:T(8,128)}), f32[192,1]{1,0:T(8,128)}) %reduce-scatter.49.cloned.1.call-update) | async-done | bytes 784
  1134.7 118.7 %reduce-scatter.51.cloned.1.call-done = f32[48,1]{1,0:T(8,128)} async-done(((f32[768,1]{1,0:T(8,128)}), f32[48,1]{1,0:T(8,128)}) %reduce-scatter.51.cloned.1.call-update) | async-done | bytes 208
  1254.7 124.6 %reduce-scatter.53.cloned.1.call-done = f32[48,1]{1,0:T(8,128)} async-done(((f32[768,1]{1,0:T(8,128)}), f32[48,1]{1,0:T(8,128)}) %reduce-scatter.53.cloned.1.call-update) | async-done | bytes 208
  1380.6 130.9 %reduce-scatter.41.cloned.1.call-done = f32[1,48,768]{2,1,0:T(8,128)} async-done(((f32[1,768,768]{2,1,0:T(8,128)}), f32[1,48,768]{2,1,0:T(8,128)}) %reduce-scatter.41.cloned.1.call-update) | async-done | bytes 147472 | tf_op jit(solution)/shard_map/reduce_scatter | solution.py:325
  1511.5 21.1 %all-reduce.2.cloned.1.call-done = f32[48,384]{1,0:T(8,128)} async-done(((f32[48,384]{1,0:T(8,128)}), f32[48,384]{1,0:T(8,128)}) %all-reduce.2.cloned.1.call-update) | async-done | bytes 73744 | tf_op jit(solution)/shard_map/psum | solution.py:335
  1532.6 149.9 %reduce-scatter.39.cloned.1.call-done = f32[1,48,1920]{2,1,0:T(8,128)} async-done(((f32[1,768,1920]{2,1,0:T(8,128)}), f32[1,48,1920]{2,1,0:T(8,128)}) %reduce-scatter.39.cloned.1.call-update) | async-done | bytes 368656 | tf_op jit(solution)/shard_map/reduce_scatter | solution.py:324
  1682.5 177.7 %reduce-scatter.43.cloned.1.call-done = f32[1,48,3072]{2,1,0:T(8,128)} async-done(((f32[1,768,3072]{2,1,0:T(8,128)}), f32[1,48,3072]{2,1,0:T(8,128)}) %reduce-scatter.43.cloned.1.call-update) | async-done | bytes 589840 | tf_op jit(solution)/shard_map/reduce_scatter | solution.py:326
  1860.2 176.2 %reduce-scatter.45.cloned.1.call-done = f32[1,192,768]{2,1,0:T(8,128)} async-done(((f32[1,3072,768]{2,1,0:T(8,128)}), f32[1,192,768]{2,1,0:T(8,128)}) %reduce-scatter.45.cloned.1.call-update) | async-done | bytes 589840 | tf_op jit(solution)/shard_map/reduce_scatter | solution.py:327
  (600 shorter events, 230.7 us)
Async XLA Ops:
  7.2 47.5 %all-gather.12.cloned.1.call-start = ((), (), s32[]{:S(2)}) async-start(), calls=%async_computation.17 | async-start | bytes 1966080 | tf_op jit(solution)/shard_map/all_gather | solution.py:53
  8.1 207.4 %copy-start.98 = (f32[768]{0:T(1024)}, f32[768]{0:T(1024)S(1)}, u32[]{:S(2)}) copy-start(f32[768]{0:T(1024)S(1)} %reduce.2) | copy-start | bytes 9220
  15.3 77.5 %all-gather.10.cloned.1.call-start = ((), (), s32[]{:S(2)}) async-start(), calls=%async_computation.16 | async-start | bytes 1966080 | tf_op jit(solution)/shard_map/all_gather | solution.py:54
  19.5 135.9 %all-gather.16.cloned.1.call-start = ((), (), s32[]{:S(2)}) async-start(), calls=%async_computation.19 | async-start | bytes 1966080 | tf_op jit(solution)/shard_map/all_gather | solution.py:53
  20.4 10.5 copy-start.119
  20.4 16.9 copy-start.118
  20.4 27.8 %copy-start.117 = (s32[1,256]{1,0:T(1,128)}, s32[1,256]{1,0:T(1,128)S(1)}, u32[]{:S(2)}) copy-start(s32[1,256]{1,0:T(1,128)S(1)} %get-tuple-element.120) | copy-start | bytes 3076
  111.0 3.6 collective-permute-start
  112.3 3.6 collective-permute-start.1
  119.6 73.2 %all-gather.14.cloned.1.call-start = ((), (), s32[]{:S(2)}) async-start(), calls=%async_computation.18 | async-start | bytes 1966080 | tf_op jit(solution)/shard_map/all_gather | solution.py:54
  122.8 135.1 %all-gather.20.cloned.1.call-start = ((), (), s32[]{:S(2)}) async-start(), calls=%async_computation.23 | async-start | bytes 1966080 | tf_op jit(solution)/shard_map/all_gather | solution.py:53
  209.3 3.7 collective-permute-start.2
  210.8 4.7 collective-permute-start.3
  221.6 73.6 %all-gather.18.cloned.1.call-start = ((), (), s32[]{:S(2)}) async-start(), calls=%async_computation.22 | async-start | bytes 1966080 | tf_op jit(solution)/shard_map/all_gather | solution.py:54
  224.8 169.0 %reduce-scatter.29.cloned.1.call-start = ((), (), s32[]{:S(2)}) async-start(), calls=%async_computation.21 | async-start | bytes 1966080 | tf_op jit(solution)/shard_map/reduce_scatter | solution.py:171
  238.1 26.4 %copy-start.126 = (f32[256]{0:T(256)}, f32[256]{0:T(256)S(1)}, u32[]{:S(2)}) copy-start(f32[256]{0:T(256)S(1)} %broadcast_multiply_fusion.17) | copy-start | bytes 3076
  335.6 70.9 %reduce-scatter.27.cloned.1.call-start = ((), (), s32[]{:S(2)}) async-start(), calls=%async_computation.20 | async-start | bytes 1966080 | tf_op jit(solution)/shard_map/reduce_scatter | solution.py:165
  343.1 12.2 slice-start.6
  343.1 12.2 slice-start.7
  343.1 13.4 slice-start.8
  343.1 13.4 copy-start.60
  343.1 13.4 copy-start.96
  366.5 118.8 %reduce-scatter.33.cloned.1.call-start = ((), (), s32[]{:S(2)}) async-start(), calls=%async_computation.25 | async-start | bytes 1966080 | tf_op jit(solution)/shard_map/reduce_scatter | solution.py:171
  384.6 21.8 %copy-start.127 = (f32[256]{0:T(256)S(1)}, f32[256]{0:T(256)}, u32[]{:S(2)}) copy-start(f32[256]{0:T(256)} %copy-done.126) | copy-start | bytes 3076
  384.6 21.8 %copy-start.139 = (f32[256]{0:T(256)S(1)}, f32[256]{0:T(256)}, u32[]{:S(2)}) copy-start(f32[256]{0:T(256)} %fusion.241) | copy-start | bytes 3076
  406.5 15.7 slice-start.19
  410.6 10.7 copy-start.50
  410.6 10.7 collective-permute-start.4
  413.7 13.6 slice-start.11
  444.0 70.2 %reduce-scatter.31.cloned.1.call-start = ((), (), s32[]{:S(2)}) async-start(), calls=%async_computation.24 | async-start | bytes 1966080 | tf_op jit(solution)/shard_map/reduce_scatter | solution.py:165
  446.8 12.5 slice-start.3
  446.8 12.5 slice-start.4
  446.8 13.6 slice-start.5
  446.8 13.6 copy-start.58
  446.8 13.6 copy-start.90
  470.5 115.1 %reduce-scatter.37.cloned.1.call-start = ((), (), s32[]{:S(2)}) async-start(), calls=%async_computation.27 | async-start | bytes 1966080 | tf_op jit(solution)/shard_map/reduce_scatter | solution.py:171
  477.0 12.3 collective-permute-start.5
  514.1 16.2 slice-start.21
  518.6 10.8 copy-start.52
  518.6 10.8 collective-permute-start.6
  521.5 13.7 slice-start.13
  551.8 70.2 %reduce-scatter.35.cloned.1.call-start = ((), (), s32[]{:S(2)}) async-start(), calls=%async_computation.26 | async-start | bytes 1966080 | tf_op jit(solution)/shard_map/reduce_scatter | solution.py:165
  554.9 12.5 slice-start
  554.9 12.5 slice-start.1
  554.9 13.6 slice-start.2
  554.9 13.6 copy-start.57
  554.9 13.6 copy-start.89
  578.5 170.1 %reduce-scatter.47.cloned.1.call-start = ((), (), s32[]{:S(2)}) async-start(), calls=%async_computation.32 | async-start | bytes 1253376 | tf_op jit(solution)/shard_map/reduce_scatter | solution.py:328
  590.5 283.4 %reduce-scatter.55.cloned.1.call-start = ((), (), s32[]{:S(2)}) async-start(), calls=%async_computation.37 | async-start | bytes 417792
  596.9 27.5 %collective-permute-start.7 = (f32[256,768]{1,0:T(8,128)}, f32[256,768]{1,0:T(8,128)}, u32[]{:S(2)}, u32[]{:S(2)}) collective-permute-start(f32[256,768]{1,0:T(8,128)} %fusion.233), channel_id=1, source_target_pairs={{16,0},{17,1},{18,2},{19,3},{20,4},{21,5},{22,6},{23,7},{24,8},{25... | collective-permute-start | bytes 2359304 | tf_op jit(solution)/shard_map/ppermute | solution.py:17
  604.5 395.4 %reduce-scatter.57.cloned.1.call-start = ((), (), s32[]{:S(2)}) async-start(), calls=%async_computation.38 | async-start | bytes 417792
  606.2 521.9 %reduce-scatter.49.cloned.1.call-start = ((), (), s32[]{:S(2)}) async-start(), calls=%async_computation.34 | async-start | bytes 1671168
  610.0 643.4 %reduce-scatter.51.cloned.1.call-start = ((), (), s32[]{:S(2)}) async-start(), calls=%async_computation.35 | async-start | bytes 417792
  628.6 750.7 %reduce-scatter.53.cloned.1.call-start = ((), (), s32[]{:S(2)}) async-start(), calls=%async_computation.36 | async-start | bytes 417792
  629.6 881.9 %reduce-scatter.41.cloned.1.call-start = ((), (), s32[]{:S(2)}) async-start(), calls=%async_computation.29 | async-start | bytes 2506752 | tf_op jit(solution)/shard_map/reduce_scatter | solution.py:325
  633.9 898.8 %all-reduce.2.cloned.1.call-start = ((), (), s32[]{:S(2)}) async-start(), calls=%async_computation.33 | async-start | bytes 147456 | tf_op jit(solution)/shard_map/psum | solution.py:335
  636.6 112.1 %copy-start.86 = (bf16[256,768]{1,0:T(8,128)(2,1)S(1)}, bf16[256,768]{1,0:T(8,128)(2,1)}, u32[]{:S(2)}) copy-start(bf16[256,768]{1,0:T(8,128)(2,1)} %get-tuple-element.112) | copy-start | bytes 1179652
  748.7 933.9 %reduce-scatter.39.cloned.1.call-start = ((), (), s32[]{:S(2)}) async-start(), calls=%async_computation.28 | async-start | bytes 6266880 | tf_op jit(solution)/shard_map/reduce_scatter | solution.py:324
  756.0 1104.2 %reduce-scatter.43.cloned.1.call-start = ((), (), s32[]{:S(2)}) async-start(), calls=%async_computation.30 | async-start | bytes 10027008 | tf_op jit(solution)/shard_map/reduce_scatter | solution.py:326
  768.2 1268.2 %reduce-scatter.45.cloned.1.call-start = ((), (), s32[]{:S(2)}) async-start(), calls=%async_computation.31 | async-start | bytes 10027008 | tf_op jit(solution)/shard_map/reduce_scatter | solution.py:327
  779.3 350.4 %copy-start.134 = (f32[256]{0:T(256)S(1)}, f32[256]{0:T(256)}, u32[]{:S(2)}) copy-start(f32[256]{0:T(256)} %copy-done.133) | copy-start | bytes 3076
  779.3 350.4 %copy-start.138 = (f32[256]{0:T(256)S(1)}, f32[256]{0:T(256)}, u32[]{:S(2)}) copy-start(f32[256]{0:T(256)} %get-tuple-element.22) | copy-start | bytes 3076
  779.3 350.4 %copy-start.116 = (f32[256]{0:T(256)S(1)}, f32[256]{0:T(256)}, u32[]{:S(2)}) copy-start(f32[256]{0:T(256)} %copy-done.114) | copy-start | bytes 3076
  779.3 350.4 %copy-start.123 = (f32[256]{0:T(256)S(1)}, f32[256]{0:T(256)}, u32[]{:S(2)}) copy-start(f32[256]{0:T(256)} %fusion.245) | copy-start | bytes 3076
  (148 other events, 651.4 us)
Sparse Core Ops, SparseCore 0:
  15.4 39.2 all-gather.11
  56.8 35.9 all-gather.9
  119.7 35.5 all-gather.15
  156.8 35.9 all-gather.13
  221.7 36.0 all-gather.19
  259.3 35.9 all-gather.17
  335.7 34.1 reduce-scatter.28
  372.1 34.2 reduce-scatter.26
  444.1 33.5 reduce-scatter.32
  479.8 34.2 reduce-scatter.30
  551.9 33.5 reduce-scatter.36
  587.7 34.2 reduce-scatter.34
  626.8 121.8 reduce-scatter.46
  753.2 120.6 reduce-scatter.54
  879.1 120.7 reduce-scatter.56
  1004.5 123.5 reduce-scatter.48
  1132.6 120.7 reduce-scatter.50
  1258.6 120.6 reduce-scatter.52
  1384.8 126.6 reduce-scatter.40
  1513.7 18.8 all-reduce.1
  1539.4 143.1 reduce-scatter.38
  1689.7 170.4 reduce-scatter.42
  1866.5 169.9 reduce-scatter.44
where the time goes:
time: 2050 us; the launch traced here: 2040 us
  waiting for transfers between devices  1510 us (74%)
  matrix products  259 us (13%)
  other arithmetic  118 us (6%)
  local copies, waits for them, and re-layouts  94.7 us (5%)
  blocking collectives  25.3 us (1%)
    unnamed x28, waiting for transfers between devices  583 us
    reduce_scatter x1, waiting for transfers between devices, shards(): lax.psum_scatter(fc_part[None], ('dp', 'ctx'), scatter_dimension=1, tiled...  178 us
    reduce_scatter x1, waiting for transfers between devices, shards(): lax.psum_scatter(proj_part[None], ('dp', 'ctx'), scatter_dimension=1, til...  176 us
    reduce_scatter x1, waiting for transfers between devices, shards(): lax.psum_scatter(qkv_part[None], ('dp', 'ctx'), scatter_dimension=1, tile...  150 us
    reduce_scatter x1, waiting for transfers between devices, shards(): lax.psum_scatter(out_part[None], ('dp', 'ctx'), scatter_dimension=1, tile...  131 us
    reduce_scatter x1, waiting for transfers between devices, shards(): lax.psum_scatter(shared_part[None], ('dp', 'ctx'), scatter_dimension=1, t...  107 us
    all_gather x3, waiting for transfers between devices, gather_keys(): lax.all_gather(parts[1], 'ctx', axis=0, tiled=True)  69.7 us
    all_gather x3, waiting for transfers between devices, gather_keys(): lax.all_gather(parts[0], 'ctx', axis=0, tiled=True)  49.3 us
  transfers between devices with their start and end apart: 31, of which 24 were waited for; matrix products, arithmetic and copies ran while one was open for 15% of the time, Pallas kernels for 0%

commit v1 on v0

v1 whole, which is shorter than its diff:
```python
import functools

import jax
import jax.numpy as jnp
from jax import lax
from jax.experimental import pallas as pl
from jax.experimental.pallas import tpu as pltpu
from jax.sharding import PartitionSpec as P

HEAD = 64
EPSILON = 1e-05
MASKED = -1000000000.0
F32 = jnp.float32
BF16 = jnp.bfloat16
VMEM_LIMIT = 56 * 2**20


def mm(left, right):
    return jnp.dot(left, right, preferred_element_type=F32)


def mm_nt(left, right):
    return lax.dot_general(left, right, (((1,), (1,)), ((), ())), preferred_element_type=F32)


def mm_tn(left, right):
    return lax.dot_general(left, right, (((0,), (0,)), ((), ())), preferred_element_type=F32)


def norm_parts(values):
    mean = jnp.mean(values, axis=-1, keepdims=True)
    centred = values - mean
    spread = jnp.mean(centred * centred, axis=-1, keepdims=True)
    rstd = lax.rsqrt(spread + EPSILON)
    return centred * rstd, rstd


def layer_norm(values, gain, bias):
    return norm_parts(values)[0] * gain + bias


def norm_back(values, gain, grad):
    unit, rstd = norm_parts(values)
    scaled = grad * gain
    m1 = jnp.mean(scaled, axis=-1, keepdims=True)
    m2 = jnp.mean(scaled * unit, axis=-1, keepdims=True)
    return rstd * (scaled - m1 - unit * m2), jnp.sum(grad * unit, axis=0), jnp.sum(grad, axis=0)


def gelu(u):
    return 0.5 * u * (1.0 + jnp.tanh(0.7978845608028654 * (u + 0.044715 * u * u * u)))


def gelu_grad(u):
    t = jnp.tanh(0.7978845608028654 * (u + 0.044715 * u * u * u))
    return 0.5 * (1.0 + t) + 0.5 * u * (1.0 - t * t) * 0.7978845608028654 * (1.0 + 3 * 0.044715 * u * u)


def swap(x):
    return lax.ppermute(x, "section", [(0, 1), (1, 0)])


def fwd_attention_kernel(T, q_ref, k_ref, v_ref, qpos_ref, qseg_ref, kseg_ref, o_ref, lse_ref, bias):
    L = k_ref.shape[0]

    @pl.when(pl.program_id(0) == 0)
    def _():
        kpos = lax.broadcasted_iota(jnp.int32, (2 * T, L), 1)
        allowed = (kpos <= qpos_ref[...]) & (kseg_ref[...] == qseg_ref[...])
        bias[...] = jnp.where(allowed, 0.0, MASKED)

    lane = lax.broadcasted_iota(jnp.int32, (T, 128), 1)
    for part in range(2):
        rows = slice(part * T, (part + 1) * T)
        keys = L // 2 if part == 0 else L
        q2 = q_ref[rows, :]
        outs, lses = [], []
        for h in range(2):
            qh = jnp.where((lane >= 64) == (h == 1), q2, jnp.zeros_like(q2)) * jnp.asarray(HEAD**-0.5, BF16)
            s = mm_nt(qh, k_ref[:keys, :]) + bias[rows, :keys]
            top = jnp.max(s, axis=-1, keepdims=True)
            e = jnp.exp(s - top)
            total = jnp.sum(e, axis=-1, keepdims=True)
            prob = (e * (1.0 / total)).astype(BF16)
            outs.append(mm(prob, v_ref[:keys, :]))
            lses.append(top + jnp.log(total))
        o_ref[rows, :] = jnp.where(lane < 64, outs[0], outs[1]).astype(BF16)
        lse_ref[0, rows, :] = jnp.where(lane < 64, lses[0], lses[1])


def fwd_attention(q, k, v, qpos, qseg, kseg):
    rows, width = q.shape
    T, L = rows // 2, k.shape[0]
    pairs = width // 128
    col = lambda n: pl.BlockSpec((n, 128), lambda i: (0, i))
    full = lambda a: pl.BlockSpec(a.shape, lambda i: (0, 0))
    return pl.pallas_call(
        functools.partial(fwd_attention_kernel, T),
        grid=(pairs,),
        in_specs=[col(rows), col(L), col(L), full(qpos), full(qseg), full(kseg)],
        out_specs=[col(rows), pl.BlockSpec((1, rows, 128), lambda i: (i, 0, 0))],
        out_shape=[jax.ShapeDtypeStruct((rows, width), BF16), jax.ShapeDtypeStruct((pairs, rows, 128), F32)],
        scratch_shapes=[pltpu.VMEM((rows, L), F32)],
        compiler_params=pltpu.CompilerParams(vmem_limit_bytes=VMEM_LIMIT),
        name="attention_forward",
    )(q, k, v, qpos, qseg, kseg)


def bwd_attention_kernel(T, q_ref, k_ref, v_ref, go_ref, o_ref, lse_ref, qpos_ref, qseg_ref, kseg_ref,
                         dq_ref, dk_ref, dv_ref, bias):
    L = k_ref.shape[0]

    @pl.when(pl.program_id(0) == 0)
    def _():
        kpos = lax.broadcasted_iota(jnp.int32, (2 * T, L), 1)
        allowed = (kpos <= qpos_ref[...]) & (kseg_ref[...] == qseg_ref[...])
        bias[...] = jnp.where(allowed, 0.0, MASKED)

    lane = lax.broadcasted_iota(jnp.int32, (T, 128), 1)
    lane_k = lax.broadcasted_iota(jnp.int32, (L, 128), 1)
    scale = jnp.asarray(HEAD**-0.5, BF16)
    for part in (1, 0):
        rows = slice(part * T, (part + 1) * T)
        keys = L // 2 if part == 0 else L
        q2 = q_ref[rows, :]
        go2 = go_ref[rows, :]
        prod = go2.astype(F32) * o_ref[rows, :].astype(F32)
        lse2 = lse_ref[0, rows, :]
        dqs, dks, dvs = [], [], []
        for h in range(2):
            sel = (lane >= 64) == (h == 1)
            qh = jnp.where(sel, q2, jnp.zeros_like(q2)) * scale
            goh = jnp.where(sel, go2, jnp.zeros_like(go2))
            delta = jnp.sum(jnp.where(sel, prod, 0.0), axis=-1, keepdims=True)
            s = mm_nt(qh, k_ref[:keys, :]) + bias[rows, :keys]
            prob = jnp.exp(s - lse2[:, 64 * h : 64 * h + 1])
            gp = mm_nt(goh, v_ref[:keys, :])
            gs = (prob * (gp - delta)).astype(BF16)
            dqs.append(mm(gs, k_ref[:keys, :]))
            dks.append(mm_tn(gs, qh))
            dvs.append(mm_tn(prob.astype(BF16), goh))
        dq_ref[rows, :] = (jnp.where(lane < 64, dqs[0], dqs[1]) * HEAD**-0.5).astype(BF16)
        dk = dks[0] + dks[1]
        dv = dvs[0] + dvs[1]
        if part == 1:
            dk_ref[...] = dk
            dv_ref[...] = dv
        else:
            dk_ref[:keys, :] += dk
            dv_ref[:keys, :] += dv


def bwd_attention(q, k, v, go, o, lse, qpos, qseg, kseg):
    rows, width = q.shape
    T, L = rows // 2, k.shape[0]
    pairs = width // 128
    col = lambda n: pl.BlockSpec((n, 128), lambda i: (0, i))
    full = lambda a: pl.BlockSpec(a.shape, lambda i: (0, 0))
    return pl.pallas_call(
        functools.partial(bwd_attention_kernel, T),
        grid=(pairs,),
        in_specs=[col(rows), col(L), col(L), col(rows), col(rows), pl.BlockSpec((1, rows, 128), lambda i: (i, 0, 0)),
                  full(qpos), full(qseg), full(kseg)],
        out_specs=[col(rows), col(L), col(L)],
        out_shape=[jax.ShapeDtypeStruct((rows, width), BF16), jax.ShapeDtypeStruct((L, width), F32),
                   jax.ShapeDtypeStruct((L, width), F32)],
        scratch_shapes=[pltpu.VMEM((rows, L), F32)],
        compiler_params=pltpu.CompilerParams(vmem_limit_bytes=VMEM_LIMIT),
        name="attention_backward",
    )(q, k, v, go, o, lse, qpos, qseg, kseg)


def xor_route(size, bit):
    return [(i, i ^ (1 << bit)) for i in range(size)]


def halve(grad, axis_name, bit, at):
    mine = (lax.axis_index(axis_name) >> bit) & 1
    keep = lax.dynamic_index_in_dim(grad, mine, at, keepdims=False)
    send = lax.dynamic_index_in_dim(grad, 1 - mine, at, keepdims=False)
    got = lax.ppermute(send, axis_name, xor_route(lax.axis_size(axis_name), bit))
    return (keep.astype(F32) + got.astype(F32)).astype(grad.dtype)


def bits_of(axis_name):
    return lax.axis_size(axis_name).bit_length() - 1


def scatter_sum(grad, order, skip_first=False):
    dims = [("dp", b) for b in reversed(range(bits_of("dp")))] + [("ctx", b) for b in reversed(range(bits_of("ctx")))]
    if skip_first:
        dims = dims[1:]
    parts = len(dims)
    rows, cols = grad.shape
    grad = grad.reshape((2,) * parts + (rows >> parts, cols))
    for item in order:
        at = dims.index(item)
        grad = halve(grad, item[0], item[1], at)
        dims.pop(at)
    return grad


def shards(ends, segment_ids, ln1_gain, ln1_bias, qkv_weight, out_weight, ln2_gain, ln2_bias, fc_weight, fc_bias,
           proj_weight, shared_weight):
    core = lax.axis_index("section")
    place = lax.axis_index("ctx")
    C = lax.axis_size("ctx")
    N = C // 2
    micros, T, D = ends.shape[1:]
    L = T * C
    half = D // 2
    F = fc_weight.shape[2]
    FH = F // 2
    upper = place >= N
    row = upper.astype(jnp.int32)
    reverse = [(i, C - 1 - i) for i in range(C)]
    first = core == 0

    mine = lax.dynamic_index_in_dim(ends[0], row, 0, keepdims=False)
    other = lax.dynamic_index_in_dim(ends[0], 1 - row, 0, keepdims=False)
    got = lax.ppermute(other, "ctx", reverse)
    both = jnp.where(upper, jnp.concatenate([got, mine], 0), jnp.concatenate([mine, got], 0))
    both_other = swap(both)
    x_in = jnp.where(first, both, both_other)
    g_out = jnp.where(first, both_other, both)

    lo = jnp.minimum(place, C - 1 - place)
    hi = C - 1 - lo
    seg_pieces = [(place, segment_ids)]
    for k in range(1, C):
        seg_pieces.append((lax.rem(place + C - k, C), lax.ppermute(segment_ids, "ctx", [(i, (i + k) % C) for i in range(C)])))
    seg_row = jnp.zeros((C, T), jnp.int32)
    for at, piece in seg_pieces:
        seg_row = lax.dynamic_update_slice(seg_row, lax.dynamic_index_in_dim(piece, row, 0, keepdims=True), (at, 0))
    kseg = seg_row.reshape(1, L)
    qseg = jnp.concatenate([lax.dynamic_index_in_dim(seg_row, lo, 0, keepdims=False),
                            lax.dynamic_index_in_dim(seg_row, hi, 0, keepdims=False)]).reshape(2 * T, 1)
    qpos = jnp.concatenate([lo * T + jnp.arange(T), hi * T + jnp.arange(T)]).astype(jnp.int32).reshape(2 * T, 1)

    def qkv_half(c):
        wq = lax.dynamic_slice_in_dim(qkv_weight[0], c * half, half, 1)
        wk = lax.dynamic_slice_in_dim(qkv_weight[0], D + c * half, half, 1)
        wv = jnp.where(c == 0, shared_weight, qkv_weight[0][:, 2 * D :])
        return jnp.concatenate([wq, wk, wv], axis=1)

    def halves(c):
        return (qkv_half(c), lax.dynamic_slice_in_dim(out_weight[0], c * half, half, 0),
                lax.dynamic_slice_in_dim(fc_weight[0], c * FH, FH, 1), lax.dynamic_slice_in_dim(proj_weight[0], c * FH, FH, 0))

    own_half = halves(core)
    got_half = tuple(swap(w) for w in halves(1 - core))
    small = jnp.concatenate([ln1_gain[0], ln1_bias[0], ln2_gain[0], ln2_bias[0], fc_bias[0]])
    small_other = swap(small)

    def layer_weights(l):
        is_own = core == l
        ws = tuple(jnp.where(is_own, a, b) for a, b in zip(own_half, got_half))
        sm = jnp.where(is_own, small, small_other)
        norms = tuple(sm[i * D : (i + 1) * D] for i in range(4))
        return ws + (norms, lax.dynamic_slice_in_dim(sm, 4 * D + core * FH, FH, 0))

    weights = [layer_weights(0), layer_weights(1)]

    def to_group(blocks):
        send = jnp.where(first, blocks[:T], blocks[T:])
        out = jnp.zeros((C, T, D), blocks.dtype)
        out = lax.dynamic_update_slice(out, blocks[:T][None], (lo, 0, 0))
        out = lax.dynamic_update_slice(out, blocks[T:][None], (hi, 0, 0))
        base = jnp.where(upper, N, 0)
        for k in range(1, N):
            route = [(g * N + i, g * N + (i + k) % N) for g in range(2) for i in range(N)]
            piece = lax.ppermute(send, "ctx", route)
            other_piece = swap(piece)
            src = base + lax.rem(place - base + N - k, N)
            slo = jnp.minimum(src, C - 1 - src)
            a = jnp.where(first, piece, other_piece)
            b = jnp.where(first, other_piece, piece)
            out = lax.dynamic_update_slice(out, a[None], (slo, 0, 0))
            out = lax.dynamic_update_slice(out, b[None], (C - 1 - slo, 0, 0))
        return out.reshape(L, D)

    def from_group(parts):
        parts = parts.reshape(C, T, D)
        base = jnp.where(upper, N, 0)
        own = jnp.concatenate([lax.dynamic_index_in_dim(parts, lo, 0, keepdims=False),
                               lax.dynamic_index_in_dim(parts, hi, 0, keepdims=False)], 0)
        sums = None
        for k in range(1, N):
            dst = base + lax.rem(place - base + k, N)
            dlo = jnp.minimum(dst, C - 1 - dst)
            plo = lax.dynamic_index_in_dim(parts, dlo, 0, keepdims=False)
            phi = lax.dynamic_index_in_dim(parts, C - 1 - dlo, 0, keepdims=False)
            keep = jnp.where(first, plo, phi)
            give = jnp.where(first, phi, plo).astype(BF16)
            pair = (keep + swap(give).astype(F32)).astype(BF16)
            route = [(g * N + i, g * N + (i + k) % N) for g in range(2) for i in range(N)]
            come = lax.ppermute(pair, "ctx", route).astype(F32)
            sums = come if sums is None else sums + come
        zero = jnp.zeros_like(own[:T])
        extra = jnp.where(first, jnp.concatenate([sums, zero], 0), jnp.concatenate([zero, sums], 0))
        own = own + extra
        return own + swap(own.astype(BF16)).astype(F32)

    def pair_sum(x):
        return x + swap(x.astype(BF16)).astype(F32)

    def forward(l, resid, first_all):
        wqkv, wout, wfc, wproj, (g1, b1, g2, b2), fcb = weights[l]
        normed = layer_norm(resid, g1, b1).astype(BF16)
        normed_all = to_group(normed)
        source_all = normed_all if l == 0 else first_all
        value_in = jnp.where(first, source_all, normed_all)
        q = mm(normed, wqkv[:, :half]).astype(BF16)
        k = mm(normed_all, wqkv[:, half : 2 * half]).astype(BF16)
        v = mm(value_in, wqkv[:, 2 * half :]).astype(BF16)
        o, lse = fwd_attention(q, k, v, qpos, qseg, kseg)
        hidden = resid + pair_sum(mm(o, wout))
        normed2 = layer_norm(hidden, g2, b2).astype(BF16)
        up = mm(normed2, wfc) + fcb
        act = gelu(up).astype(BF16)
        out = hidden + pair_sum(mm(act, wproj))
        return out, dict(resid=resid, normed=normed, normed_all=normed_all, value_in=value_in, q=q, k=k, v=v, o=o,
                         lse=lse, hidden=hidden, normed2=normed2, up=up, act=act)

    def backward(l, st, grad_out, source_part):
        wqkv, wout, wfc, wproj, (g1, b1, g2, b2), fcb = weights[l]
        gm = grad_out.astype(BF16)
        gu = (gelu_grad(st["up"]) * mm_nt(gm, wproj)).astype(BF16)
        proj_g = mm_tn(st["act"], gm).astype(BF16)
        fc_g = mm_tn(st["normed2"], gu).astype(BF16)
        fcb_g = jnp.sum(gu.astype(F32), axis=0)
        gn2 = pair_sum(mm_nt(gu, wfc))
        gh, g2_g, b2_g = norm_back(st["hidden"], g2, gn2)
        gh = gh + grad_out
        gb = gh.astype(BF16)
        go = mm_nt(gb, wout).astype(BF16)
        out_g = mm_tn(st["o"], gb).astype(BF16)
        dq, dk, dv = bwd_attention(st["q"], st["k"], st["v"], go, st["o"], st["lse"], qpos, qseg, kseg)
        dk = dk.astype(BF16)
        dv = dv.astype(BF16)
        wq, wk, wv = wqkv[:, :half], wqkv[:, half : 2 * half], wqkv[:, 2 * half :]
        from_v = mm_nt(dv, wv)
        parts = mm_nt(dk, wk)
        if l == 0:
            parts = parts + from_v + source_part
            next_source = None
        else:
            parts = parts + jnp.where(first, 0.0, from_v)
            next_source = jnp.where(first, from_v, 0.0)
        own_q = mm_nt(dq, wq)
        parts = parts.reshape(C, T, D)
        parts = lax.dynamic_update_slice(parts, (lax.dynamic_index_in_dim(parts, lo, 0) + own_q[:T][None]), (lo, 0, 0))
        parts = lax.dynamic_update_slice(parts, (lax.dynamic_index_in_dim(parts, hi, 0) + own_q[T:][None]), (hi, 0, 0))
        gn = from_group(parts.reshape(L, D))
        gr, g1_g, b1_g = norm_back(st["resid"], g1, gn)
        gr = gr + gh
        q_g = mm_tn(st["normed"], dq).astype(BF16)
        k_g = mm_tn(st["normed_all"], dk).astype(BF16)
        v_g = mm_tn(st["value_in"], dv)
        return gr, next_source, (q_g, k_g, v_g, out_g, fc_g, proj_g), (fcb_g, g1_g, b1_g, g2_g, b2_g)

    sent, st0 = forward(0, x_in.astype(F32), None)
    sent = sent.astype(BF16).astype(F32)
    y, st1 = forward(1, sent, st0["normed_all"])
    gr1, src, big1, small1 = backward(1, st1, g_out.astype(F32), None)
    gx, _, big0, small0 = backward(0, st0, gr1, src)

    dpb, cb = bits_of("dp"), bits_of("ctx")
    dp_bits = [("dp", b) for b in range(dpb)]
    ctx_bits = [("ctx", b) for b in range(cb)]
    x_first = dp_bits + ctx_bits
    z_first = ctx_bits + dp_bits
    y_first = [("dp", b) for b in reversed(range(dpb))] + ctx_bits

    def sided(grad):
        dp = lax.axis_index("dp")
        size = lax.axis_size("dp")
        top = size // 2
        route = [(c * size + d, c * size + (d ^ top)) for c in range(2) for d in range(size) if (d >= top) != (c == 1)]
        got = lax.ppermute(grad, ("section", "dp"), route)
        total = (grad.astype(F32) + got.astype(F32)).astype(BF16)
        return scatter_sum(total, y_first[1:], skip_first=True)

    shared_half = big0[2] + big1[2]
    zero = jnp.zeros_like(shared_half)
    res = []
    for l, (q_g, k_g, v_g, out_g, fc_g, proj_g) in ((1, big1), (0, big0)):
        fc_s = scatter_sum(fc_g, x_first)
        proj_s = sided(proj_g)
        out_s = sided(out_g)
        if l == 1:
            v_use = jnp.where(first, zero, v_g)
        else:
            v_use = jnp.where(first, shared_half, v_g)
        qkv_s = scatter_sum(jnp.concatenate([q_g, k_g, v_use.astype(BF16)], axis=1), z_first)
        res.append((qkv_s, out_s, fc_s, proj_s))
    res = res[::-1]

    dp_top = lax.axis_index("dp") >= lax.axis_size("dp") // 2
    holder = jnp.where(dp_top, 1, 0) == core
    mine_l = tuple(jnp.where(first, a, b) for a, b in zip(res[0], res[1]))
    other_l = tuple(jnp.where(first, b, a) for a, b in zip(res[0], res[1]))
    got_l = tuple(swap(a) for a in other_l)

    def columns(a, b):
        left = jnp.where(first, a, b).astype(F32)
        right = jnp.where(first, b, a).astype(F32)
        return left, right

    ql, qr = columns(mine_l[0], got_l[0])
    qkv_out = jnp.concatenate([ql[:, :half], qr[:, :half], ql[:, half : 2 * half], qr[:, half : 2 * half], qr[:, 2 * half :]], axis=1)
    fc_out = jnp.concatenate(columns(mine_l[2], got_l[2]), axis=1)
    out_out = jnp.where(holder, mine_l[1], got_l[1]).astype(F32)
    proj_out = jnp.where(holder, mine_l[3], got_l[3]).astype(F32)
    shared_own = mine_l[0][:, 2 * half :]
    shared_out = jnp.where(first, shared_own, swap(shared_own)).astype(F32)

    def small_vector(parts, own):
        fcb_g, g1_g, b1_g, g2_g, b2_g = parts
        spread = lax.dynamic_update_slice(jnp.zeros((F,), F32), fcb_g, (core * FH,))
        keep = jnp.where(own, 1.0, 0.0)
        J = lax.axis_size("dp") * C
        return jnp.concatenate([spread.reshape(J, F // J)] + [(keep * v).reshape(J, D // J) for v in (g1_g, b1_g, g2_g, b2_g)], axis=1)

    vec0 = small_vector(small0, core == 0)
    vec1 = small_vector(small1, core == 1)
    vec = jnp.where(first, vec0, vec1) + swap(jnp.where(first, vec1, vec0))
    J = lax.axis_size("dp") * C
    vec = scatter_sum(vec, x_first)[0]
    fj, dj = F // J, D // J
    fcb_out = vec[:fj]
    ln = [vec[fj + i * dj : fj + (i + 1) * dj] for i in range(4)]

    end = jnp.where(first, gx, y)
    stay = jnp.where(upper, end[T:], end[:T])
    go_away = jnp.where(upper, end[:T], end[T:])
    come = lax.ppermute(go_away.astype(BF16), "ctx", reverse).astype(F32)
    block = jnp.where(upper, jnp.stack([come, stay]), jnp.stack([stay, come]))
    return (block[None], qkv_out[None], out_out[None], fc_out[None], fcb_out[None], proj_out[None], shared_out,
            ln[0][None], ln[1][None], ln[2][None], ln[3][None])


def solution(mesh):
    placed = (
        P("section", "dp", "ctx", None), P("dp", "ctx"), P("section", None), P("section", None),
        P("section", None, None), P("section", None, None), P("section", None), P("section", None),
        P("section", None, None), P("section", None), P("section", None, None), P(),
    )
    both = ("dp", "ctx")
    return jax.shard_map(
        shards, mesh=mesh, in_specs=placed,
        out_specs=(P("section", "dp", "ctx", None), P("section", both, None), P("section", both, None),
                   P("section", both, None), P("section", both), P("section", both, None), P(both, None),
                   P("section", both), P("section", both), P("section", both), P("section", both)),
        check_vma=False,
    )
```

time: 2050 us -> 569 us (0.28)
  waiting for transfers between devices: 1510 us -> 193 us
  matrix products: 259 us -> 102 us
  starting transfers between devices: 19 us -> 86 us
  other arithmetic: 118 us -> 66 us
  Pallas kernels: 0 us -> 42 us
  blocking collectives: 25.3 us -> 0 us
  local copies, waits for them, and re-layouts: 94.7 us -> 69.5 us
    reduce_scatter x11 -> x0, waiting for transfers between devices: 786 us -> none  [the longest x1 178 us: shards(): lax.psum_scatter(fc_part[None], ('dp', 'ctx'), scatter_dimension=1, tiled...]
    unnamed x28 -> x0, waiting for transfers between devices: 583 us -> none
    ppermute x8 -> x69, waiting for transfers between devices: 2.19 us -> 193 us  [the longest x32 116 us: halve(): lax.ppermute(send, axis_name, xor_route(lax.axis_size(axis_name), bit))]
    dot_general x56 -> x36, matrix products: 259 us -> 102 us  [the longest x12 40.1 us: mm_nt(): lax.dot_general(left, right, (((1,), (1,)), ((), ())), preferred_element_...]
    all_gather x6 -> x0, waiting for transfers between devices: 119 us -> none  [the longest x3 69.7 us: gather_keys(): lax.all_gather(parts[1], 'ctx', axis=0, tiled=True)]
    ppermute x8 -> x69, starting transfers between devices: 17.6 us -> 86 us  [the longest x24 32.6 us: swap(): return lax.ppermute(x, 'section', [(0, 1), (1, 0)])]
    pallas_call x0 -> x4, Pallas kernels: none -> 42 us  [the longest x2 22.3 us: bwd_attention(): pl.pallas_call(functools.partial(bwd_attention_kernel, T), grid=(pairs,),...]
    all_gather x3 -> x0, blocking collectives: 25.3 us -> none  [gather_keys(): lax.all_gather(parts[2], 'ctx', axis=0, tiled=True)]
  transfers between devices with their start and end apart: 31 -> 69, of which waited for: 24 -> 30; matrix products, arithmetic and copies ran while one was open for 15% -> 35% of each run, Pallas kernels for 0% -> 6%
where the time goes in v1:
time: 569 us; the launch traced here: 561 us
  waiting for transfers between devices  193 us (34%)
  matrix products  102 us (18%)
  starting transfers between devices  86 us (15%)
  local copies, waits for them, and re-layouts  69.5 us (12%)
  other arithmetic  66 us (12%)
  Pallas kernels  42 us (7%)
    ppermute x32, waiting for transfers between devices, halve(): lax.ppermute(send, axis_name, xor_route(lax.axis_size(axis_name), bit))  116 us
    ppermute x2, waiting for transfers between devices, from_group(): come = lax.ppermute(pair, 'ctx', route).astype(F32)  49.8 us
    dot_general x12, matrix products, mm_nt(): lax.dot_general(left, right, (((1,), (1,)), ((), ())), preferred_element_...  40.1 us
    ppermute x24, starting transfers between devices, swap(): return lax.ppermute(x, 'section', [(0, 1), (1, 0)])  32.6 us
    dot_general x12, matrix products, mm(): return jnp.dot(left, right, preferred_element_type=F32)  32.5 us
    ppermute x32, starting transfers between devices, halve(): lax.ppermute(send, axis_name, xor_route(lax.axis_size(axis_name), bit))  31.8 us
    dot_general x12, matrix products, mm_tn(): lax.dot_general(left, right, (((0,), (0,)), ((), ())), preferred_element_...  29.5 us
    pallas_call x2, Pallas kernels, bwd_attention(): pl.pallas_call(functools.partial(bwd_attention_kernel, T), grid=(pairs,),...  22.3 us
  transfers between devices with their start and end apart: 69, of which 30 were waited for; matrix products, arithmetic and copies ran while one was open for 35% of the time, Pallas kernels for 6%

profile of v1, /device:TPU:1, one launch (start us, length us, event | category | flops | bytes accessed | tf_op | source)
XLA Modules:
  0.0 560.9 jit_solution(15207319747248256365)
XLA Ops:
  20.4 4.7 copy.48
  28.0 3.4 dynamic-slice_bitcast_fusion.1
  51.3 9.3 %collective-permute-done.4 = bf16[256,768]{1,0:T(8,128)(2,1)S(1)} collective-permute-done((bf16[256,768]{1,0:T(8,128)(2,1)S(1)}, bf16[256,768]{1,0:T(8,128)(2,1)S(1)}, u32[]{:S(2)}, u32[]{:S(2)}) %collective-permute-start.4) | collective-permute-done | bytes 393248 | tf_op jit(solution)/shard_map/ppermute | solution.py:272
  68.4 10.0 %attention_forward.2 = (bf16[512,384]{1,0:T(8,128)(2,1)}, f32[3,512,128]{2,1,0:T(8,128)}) custom-call(bf16[512,384]{1,0:T(8,128)(2,1)} %convolution_convert_fusion.17.q_ref, bf16[1024,384]{1,0:T(8,128)(2,1)} %convolution_convert_fusion.7.k_ref, bf16[1024,384]{1,0:T(8,128)(2,1)} %convolution_convert_fusion.6.v_ref, s32[512,1]{1,0:T(8,128)} %copy.53.qpos_ref, ...), custom_call_target="tpu_custom_call" | custom-call | tf_op jit(solution)/shard_map/attention_forward/pallas_call | solution.py:97
  78.3 3.0 fusion.159
  86.7 4.1 convolution_add_fusion.1
  90.9 5.0 fusion.160
  96.0 2.3 collective-permute-done.13
  100.6 9.5 %collective-permute-done.14 = bf16[256,768]{1,0:T(8,128)(2,1)S(1)} collective-permute-done((bf16[256,768]{1,0:T(8,128)(2,1)S(1)}, bf16[256,768]{1,0:T(8,128)(2,1)S(1)}, u32[]{:S(2)}, u32[]{:S(2)}) %collective-permute-start.14) | collective-permute-done | bytes 393248 | tf_op jit(solution)/shard_map/ppermute | solution.py:272
  118.2 9.7 %attention_forward.3 = (bf16[512,384]{1,0:T(8,128)(2,1)}, f32[3,512,128]{2,1,0:T(8,128)}) custom-call(bf16[512,384]{1,0:T(8,128)(2,1)} %convolution_convert_fusion.16.q_ref, bf16[1024,384]{1,0:T(8,128)(2,1)} %convolution_convert_fusion.5.k_ref, bf16[1024,384]{1,0:T(8,128)(2,1)} %convolution_convert_fusion.4.v_ref, s32[512,1]{1,0:T(8,128)} %copy.53.qpos_ref, ...), custom_call_target="tpu_custom_call" | custom-call | tf_op jit(solution)/shard_map/attention_forward/pallas_call | solution.py:97
  127.9 3.1 fusion.161
  131.2 2.3 collective-permute-done.16
  136.5 3.4 convolution_add_fusion
  139.9 4.5 convert_reduce_fusion
  145.0 3.2 convolution_convert_fusion.2
  148.2 3.2 fusion.162
  151.4 4.4 collective-permute-start.17
  159.4 3.7 fusion.164
  165.1 3.2 convolution_convert_fusion
  168.2 4.5 collective-permute-start.63
  178.2 11.2 %attention_backward.2 = (bf16[512,384]{1,0:T(8,128)(2,1)}, f32[1024,384]{1,0:T(8,128)}, f32[1024,384]{1,0:T(8,128)}) custom-call(bf16[512,384]{1,0:T(8,128)(2,1)} %convolution_convert_fusion.16.q_ref, bf16[1024,384]{1,0:T(8,128)(2,1)} %convolution_convert_fusion.5.k_ref, bf16[1024,384]{1,0:T(8,128)(2,1)} %convolution_convert_fusion.4.v_ref, ...), custom_call_target="tpu_custom_call" | custom-call | tf_op jit(solution)/shard_map/attention_backward/pallas_call | solution.py:159
  189.4 4.1 select_convert_fusion
  193.5 2.6 fusion.77
  199.4 2.8 convolution_convert_fusion.8
  203.6 3.9 copy.62
  208.9 3.5 select_add_fusion.1
  218.6 25.6 %collective-permute-done.19 = bf16[256,768]{1,0:T(8,128)(2,1)S(1)} collective-permute-done((bf16[256,768]{1,0:T(8,128)(2,1)S(1)}, bf16[256,768]{1,0:T(8,128)(2,1)S(1)}, u32[]{:S(2)}, u32[]{:S(2)}) %collective-permute-start.19) | collective-permute-done | bytes 393248 | tf_op jit(solution)/shard_map/ppermute | solution.py:297
  247.0 11.1 %collective-permute-done.50 = bf16[2,2,48,1536]{3,2,0,1:T(8,128)(2,1)S(1)} collective-permute-done((bf16[2,2,48,1536]{3,2,0,1:T(8,128)(2,1)S(1)}, bf16[2,2,48,1536]{3,2,0,1:T(8,128)(2,1)S(1)}, u32[]{:S(2)}, u32[]{:S(2)}) %collective-permute-start.50) | collective-permute-done | bytes 589856 | tf_op jit(solution)/shard_map/ppermute | solution.py:181
  261.5 12.0 %collective-permute-done.51 = bf16[2,48,1536]{2,1,0:T(8,128)(2,1)S(1)} collective-permute-done((bf16[2,48,1536]{2,1,0:T(8,128)(2,1)S(1)}, bf16[2,48,1536]{2,1,0:T(8,128)(2,1)S(1)}, u32[]{:S(2)}, u32[]{:S(2)}) %collective-permute-start.51) | collective-permute-done | bytes 294944 | tf_op jit(solution)/shard_map/ppermute | solution.py:181
  273.5 2.8 collective-permute-start.43
  276.3 4.1 collective-permute-done.32
  281.6 3.9 collective-permute-done.33
  286.3 3.0 add_convert_fusion
  294.1 2.8 fusion.35
  297.2 7.5 %convert_reduce_fusion.1 = (f32[1536]{0:T(1024)S(1)}, bf16[512,1536]{1,0:T(8,128)(2,1)}) fusion(bf16[1536,768]{1,0:T(8,128)(2,1)} %collective-permute-done.12, pred[]{:T(512)S(6)} %eq.16, bf16[1,3072,768]{2,1,0:T(8,128)(2,1)} %param.22, s32[]{:T(128)S(6)} %select_n.571, f32[512,768]{1,0:T(8,128)S(1)} %fusion.35, f32[512,1536]{1,0:T(8,128)S(1)} %copy-done.74), kind=kOutput, calls=%fused_computation.25 | convolution fusion | flops 1226045952 | bytes 11016197 | tf_op jit(solution)/shard_map/dot_general | solution.py:23
  305.6 3.1 convolution_convert_fusion.3
  308.8 5.3 fusion.163
  320.3 5.8 %convolution_convert_fusion.1 = bf16[1536,768]{1,0:T(8,128)(2,1)} fusion(f32[512,768]{1,0:T(8,128)} %copy-done.35, f32[512,1536]{1,0:T(8,128)} %copy-done.73), kind=kOutput, calls=%fused_computation.7 | convolution fusion | flops 1216610304 | bytes 7077888 | tf_op jit(solution)/shard_map/dot_general | solution.py:27
  333.6 11.1 %attention_backward.3 = (bf16[512,384]{1,0:T(8,128)(2,1)}, f32[1024,384]{1,0:T(8,128)}, f32[1024,384]{1,0:T(8,128)}) custom-call(bf16[512,384]{1,0:T(8,128)(2,1)} %convolution_convert_fusion.17.q_ref, bf16[1024,384]{1,0:T(8,128)(2,1)} %convolution_convert_fusion.7.k_ref, bf16[1024,384]{1,0:T(8,128)(2,1)} %convolution_convert_fusion.6.v_ref, ...), custom_call_target="tpu_custom_call" | custom-call | tf_op jit(solution)/shard_map/attention_backward/pallas_call | solution.py:159
  346.4 2.8 fusion.90
  349.2 2.6 fusion.85
  355.4 2.7 copy.61
  359.5 2.4 collective-permute-start.36
  361.9 3.5 select_add_fusion
  374.5 24.2 %collective-permute-done.23 = bf16[256,768]{1,0:T(8,128)(2,1)S(1)} collective-permute-done((bf16[256,768]{1,0:T(8,128)(2,1)S(1)}, bf16[256,768]{1,0:T(8,128)(2,1)S(1)}, u32[]{:S(2)}, u32[]{:S(2)}) %collective-permute-start.23) | collective-permute-done | bytes 393248 | tf_op jit(solution)/shard_map/ppermute | solution.py:297
  399.6 6.8 %collective-permute-done.37 = bf16[2,2,48,768]{3,2,0,1:T(8,128)(2,1)S(1)} collective-permute-done((bf16[2,2,48,768]{3,2,0,1:T(8,128)(2,1)S(1)}, bf16[2,2,48,768]{3,2,0,1:T(8,128)(2,1)S(1)}, u32[]{:S(2)}, u32[]{:S(2)}) %collective-permute-start.37) | collective-permute-done | bytes 294944 | tf_op jit(solution)/shard_map/ppermute | solution.py:181
  406.6 5.9 %collective-permute-done.65 = bf16[2,192,768]{2,1,0:T(8,128)(2,1)S(1)} collective-permute-done((bf16[2,192,768]{2,1,0:T(8,128)(2,1)S(1)}, bf16[2,192,768]{2,1,0:T(8,128)(2,1)S(1)}, u32[]{:S(2)}, u32[]{:S(2)}) %collective-permute-start.65) | collective-permute-done | bytes 589856 | tf_op jit(solution)/shard_map/ppermute | solution.py:181
  412.7 6.4 %collective-permute-done.46 = bf16[2,2,48,1536]{3,2,0,1:T(8,128)(2,1)S(1)} collective-permute-done((bf16[2,2,48,1536]{3,2,0,1:T(8,128)(2,1)S(1)}, bf16[2,2,48,1536]{3,2,0,1:T(8,128)(2,1)S(1)}, u32[]{:S(2)}, u32[]{:S(2)}) %collective-permute-start.46) | collective-permute-done | bytes 589856 | tf_op jit(solution)/shard_map/ppermute | solution.py:181
  420.4 3.1 collective-permute-done.38
  423.6 2.6 collective-permute-start.39
  429.7 6.8 %collective-permute-start.44 = (bf16[48,768]{1,0:T(8,128)(2,1)S(1)}, bf16[48,768]{1,0:T(8,128)(2,1)S(1)}, u32[]{:S(2)}, u32[]{:S(2)}) collective-permute-start(bf16[48,768]{1,0:T(8,128)(2,1)S(1)} %broadcast_select_fusion.18), channel_id=1, source_target_pairs={{0,16},{16,0},{1,17},{17,1},{2,18},{18,2},{3,19},{19,3},{4,20},{20... | collective-permute-start | bytes 221192 | tf_op jit(solution)/shard_map/ppermute | solution.py:60
  437.4 2.3 collective-permute-start.59
  441.3 2.7 collective-permute-start.28
  444.2 19.7 %collective-permute-done.28 = bf16[2,2,48,1152]{3,2,1,0:T(8,128)(2,1)S(1)} collective-permute-done((bf16[2,2,48,1152]{3,2,1,0:T(8,128)(2,1)S(1)}, bf16[2,2,48,1152]{3,2,1,0:T(8,128)(2,1)S(1)}, u32[]{:S(2)}, u32[]{:S(2)}) %collective-permute-start.28) | collective-permute-done | bytes 442400 | tf_op jit(solution)/shard_map/ppermute | solution.py:181
  464.5 8.5 %collective-permute-done.48 = bf16[48,1536]{1,0:T(8,128)(2,1)S(1)} collective-permute-done((bf16[48,1536]{1,0:T(8,128)(2,1)S(1)}, bf16[48,1536]{1,0:T(8,128)(2,1)S(1)}, u32[]{:S(2)}, u32[]{:S(2)}) %collective-permute-start.48) | collective-permute-done | bytes 147488 | tf_op jit(solution)/shard_map/ppermute | solution.py:181
  473.3 5.4 collective-permute-done.29
  484.9 2.5 fusion.45
  502.2 3.3 fusion.44
  508.8 2.4 collective-permute-start.58
  515.3 4.1 collective-permute-start.35
  521.6 4.0 collective-permute-done.60
  528.1 2.8 collective-permute-start.68
  530.9 8.4 %collective-permute-done.61 = bf16[2,192,768]{2,1,0:T(8,128)(2,1)S(1)} collective-permute-done((bf16[2,192,768]{2,1,0:T(8,128)(2,1)S(1)}, bf16[2,192,768]{2,1,0:T(8,128)(2,1)S(1)}, u32[]{:S(2)}, u32[]{:S(2)}) %collective-permute-start.61) | collective-permute-done | bytes 589856 | tf_op jit(solution)/shard_map/ppermute | solution.py:181
  542.8 11.9 %collective-permute-done.62 = bf16[192,768]{1,0:T(8,128)(2,1)S(1)} collective-permute-done((bf16[192,768]{1,0:T(8,128)(2,1)S(1)}, bf16[192,768]{1,0:T(8,128)(2,1)S(1)}, u32[]{:S(2)}, u32[]{:S(2)}) %collective-permute-start.62) | collective-permute-done | bytes 294944 | tf_op jit(solution)/shard_map/ppermute | solution.py:181
  (514 shorter events, 188.1 us)
Async XLA Ops:
  0.7 39.1 %collective-permute-start.6 = (s32[2,256]{1,0:T(2,128)}, s32[2,256]{1,0:T(2,128)}, u32[]{:S(2)}, u32[]{:S(2)}) collective-permute-start(s32[2,256]{1,0:T(2,128)} %param.13), channel_id=1, source_target_pairs={{0,1},{1,2},{2,3},{3,0},{4,5},{5,6},{6,7},{7,4},{8,9},{9,10},{10,1... | collective-permute-start | bytes 6152 | tf_op jit(solution)/shard_map/ppermute | solution.py:231
  2.8 40.9 %collective-permute-start.8 = (s32[2,256]{1,0:T(2,128)}, s32[2,256]{1,0:T(2,128)S(1)}, u32[]{:S(2)}, u32[]{:S(2)}) collective-permute-start(s32[2,256]{1,0:T(2,128)} %param.13), channel_id=1, source_target_pairs={{0,3},{1,0},{2,1},{3,2},{4,7},{5,4},{6,5},{7,6},{8,11},{9,8},{10,9... | collective-permute-start | bytes 6152 | tf_op jit(solution)/shard_map/ppermute | solution.py:231
  4.9 35.9 %collective-permute-start.7 = (s32[2,256]{1,0:T(2,128)}, s32[2,256]{1,0:T(2,128)}, u32[]{:S(2)}, u32[]{:S(2)}) collective-permute-start(s32[2,256]{1,0:T(2,128)} %param.13), channel_id=1, source_target_pairs={{0,2},{1,3},{2,0},{3,1},{4,6},{5,7},{6,4},{7,5},{8,10},{9,11},{10,... | collective-permute-start | bytes 6152 | tf_op jit(solution)/shard_map/ppermute | solution.py:231
  14.6 31.8 %collective-permute-start.2 = (f32[6144]{0:T(1024)}, f32[6144]{0:T(1024)}, u32[]{:S(2)}, u32[]{:S(2)}) collective-permute-start(f32[6144]{0:T(1024)} %constant_dynamic-update-slice_fusion), channel_id=1, source_target_pairs={{0,16},{16,0},{1,17},{17,1},{2,18},{18,2},{3,19},{19,3},{4,20},{20... | collective-permute-start | bytes 73736 | tf_op jit(solution)/shard_map/ppermute | solution.py:60
  18.2 23.6 %collective-permute-start = (bf16[256,768]{1,0:T(8,128)(2,1)}, bf16[256,768]{1,0:T(8,128)(2,1)}, u32[]{:S(2)}, u32[]{:S(2)}) collective-permute-start(bf16[256,768]{1,0:T(8,128)(2,1)} %get-tuple-element.84), channel_id=1, source_target_pairs={{0,3},{1,2},{2,1},{3,0},{4,7},{5,6},{6,5},{7,4},{8,11},{9,10},{10,... | collective-permute-start | bytes 1179656 | tf_op jit(solution)/shard_map/ppermute | solution.py:221
  39.8 38.5 %collective-permute-start.9 = (bf16[384,768]{1,0:T(8,128)(2,1)}, bf16[384,768]{1,0:T(8,128)(2,1)S(1)}, u32[]{:S(2)}, u32[]{:S(2)}) collective-permute-start(bf16[384,768]{1,0:T(8,128)(2,1)} %dynamic-slice_bitcast_fusion.11), channel_id=1, source_target_pairs={{0,16},{16,0},{1,17},{17,1},{2,18},{18,2},{3,19},{19,3},{4,20},{20... | collective-permute-start | bytes 1769480 | tf_op jit(solution)/shard_map/ppermute | solution.py:60
  40.9 50.0 %collective-permute-start.12 = (bf16[1536,768]{1,0:T(8,128)(2,1)}, bf16[1536,768]{1,0:T(8,128)(2,1)}, u32[]{:S(2)}, u32[]{:S(2)}) collective-permute-start(bf16[1536,768]{1,0:T(8,128)(2,1)} %dynamic-slice_bitcast_fusion), channel_id=1, source_target_pairs={{0,16},{16,0},{1,17},{17,1},{2,18},{18,2},{3,19},{19,3},{4,20},{20... | collective-permute-start | bytes 7077896 | tf_op jit(solution)/shard_map/ppermute | solution.py:60
  41.9 44.9 %collective-permute-start.11 = (bf16[768,1536]{1,0:T(8,128)(2,1)}, bf16[768,1536]{1,0:T(8,128)(2,1)}, u32[]{:S(2)}, u32[]{:S(2)}) collective-permute-start(bf16[768,1536]{1,0:T(8,128)(2,1)} %dynamic-slice_bitcast_fusion.1), channel_id=1, source_target_pairs={{0,16},{16,0},{1,17},{17,1},{2,18},{18,2},{3,19},{19,3},{4,20},{20... | collective-permute-start | bytes 7077896 | tf_op jit(solution)/shard_map/ppermute | solution.py:60
  43.8 4.1 collective-permute-start.1
  46.5 14.4 %collective-permute-start.3 = (bf16[768,1152]{0,1:T(8,128)(2,1)}, bf16[768,1152]{0,1:T(8,128)(2,1)S(1)}, u32[]{:S(2)}, u32[]{:S(2)}) collective-permute-start(bf16[768,1152]{0,1:T(8,128)(2,1)} %pad_maximum_fusion.1), channel_id=1, source_target_pairs={{0,16},{16,0},{1,17},{17,1},{2,18},{18,2},{3,19},{19,3},{4,20},{20... | collective-permute-start | bytes 5308424 | tf_op jit(solution)/shard_map/ppermute | solution.py:60
  50.1 10.5 %collective-permute-start.4 = (bf16[256,768]{1,0:T(8,128)(2,1)S(1)}, bf16[256,768]{1,0:T(8,128)(2,1)S(1)}, u32[]{:S(2)}, u32[]{:S(2)}) collective-permute-start(bf16[256,768]{1,0:T(8,128)(2,1)S(1)} %broadcast_select_fusion.10), channel_id=1, source_target_pairs={{0,1},{1,0},{2,3},{3,2},{4,5},{5,4},{6,7},{7,6},{8,9},{9,8},{10,11... | collective-permute-start | bytes 1179656 | tf_op jit(solution)/shard_map/ppermute | solution.py:272
  60.6 3.8 collective-permute-start.5
  99.5 10.6 %collective-permute-start.14 = (bf16[256,768]{1,0:T(8,128)(2,1)S(1)}, bf16[256,768]{1,0:T(8,128)(2,1)S(1)}, u32[]{:S(2)}, u32[]{:S(2)}) collective-permute-start(bf16[256,768]{1,0:T(8,128)(2,1)S(1)} %broadcast_select_fusion.9), channel_id=1, source_target_pairs={{0,1},{1,0},{2,3},{3,2},{4,5},{5,4},{6,7},{7,6},{8,9},{9,8},{10,11... | collective-permute-start | bytes 1179656 | tf_op jit(solution)/shard_map/ppermute | solution.py:272
  110.1 2.4 collective-permute-start.15
  131.0 2.5 collective-permute-start.16
  151.4 21.3 %collective-permute-start.17 = (bf16[512,768]{1,0:T(8,128)(2,1)S(1)}, bf16[512,768]{1,0:T(8,128)(2,1)S(1)}, u32[]{:S(2)}, u32[]{:S(2)}) collective-permute-start(bf16[512,768]{1,0:T(8,128)(2,1)S(1)} %get-tuple-element.116), channel_id=1, source_target_pairs={{0,16},{16,0},{1,17},{17,1},{2,18},{18,2},{3,19},{19,3},{4,20},{20... | collective-permute-start | bytes 2359304 | tf_op jit(solution)/shard_map/ppermute | solution.py:60
  158.2 57.7 %collective-permute-start.49 = (bf16[2,2,2,48,1536]{4,3,1,2,0:T(8,128)(2,1)}, bf16[2,2,2,48,1536]{4,3,1,2,0:T(8,128)(2,1)}, u32[]{:S(2)}, u32[]{:S(2)}) collective-permute-start(bf16[2,2,2,48,1536]{4,3,1,2,0:T(8,128)(2,1)} %bitcast.382), channel_id=1, source_target_pairs={{0,4},{4,0},{8,12},{12,8},{1,5},{5,1},{9,13},{13,9},{2,6},{6,2},{1... | collective-permute-start | bytes 3538952 | tf_op jit(solution)/shard_map/ppermute | solution.py:181
  163.1 337.3 %collective-permute-start.25 = (bf16[512,768]{1,0:T(8,128)(2,1)}, bf16[512,768]{1,0:T(8,128)(2,1)}, u32[]{:S(2)}, u32[]{:S(2)}) collective-permute-start(bf16[512,768]{1,0:T(8,128)(2,1)} %get-tuple-element.120), channel_id=1, source_target_pairs={{0,16},{16,0},{1,17},{17,1},{2,18},{18,2},{3,19},{19,3},{4,20},{20... | collective-permute-start | bytes 2359304 | tf_op jit(solution)/shard_map/ppermute | solution.py:60
  168.2 118.0 %collective-permute-start.63 = (bf16[1536,768]{1,0:T(8,128)(2,1)}, bf16[1536,768]{1,0:T(8,128)(2,1)}, u32[]{:S(2)}, u32[]{:S(2)}) collective-permute-start(bf16[1536,768]{1,0:T(8,128)(2,1)} %convolution_convert_fusion), channel_id=1, source_target_pairs={{8,0},{12,4},{16,24},{20,28},{9,1},{13,5},{17,25},{21,29},{10,2},{... | collective-permute-start | bytes 7077896 | tf_op jit(solution)/shard_map/ppermute | solution.py:380
  207.5 10.5 %collective-permute-start.40 = (bf16[384,768]{1,0:T(8,128)(2,1)}, bf16[384,768]{1,0:T(8,128)(2,1)S(1)}, u32[]{:S(2)}, u32[]{:S(2)}) collective-permute-start(bf16[384,768]{1,0:T(8,128)(2,1)} %convolution_convert_fusion.10), channel_id=1, source_target_pairs={{8,0},{12,4},{16,24},{20,28},{9,1},{13,5},{17,25},{21,29},{10,2},{... | collective-permute-start | bytes 1769480 | tf_op jit(solution)/shard_map/ppermute | solution.py:380
  214.6 30.9 %collective-permute-start.31 = (bf16[2,2,2,48,1152]{4,3,0,1,2:T(8,128)(2,1)S(1)}, bf16[2,2,2,48,1152]{4,3,0,1,2:T(8,128)(2,1)S(1)}, u32[]{:S(2)}, u32[]{:S(2)}) collective-permute-start(bf16[2,2,2,48,1152]{4,3,0,1,2:T(8,128)(2,1)S(1)} %bitcast.420), channel_id=1, source_target_pairs={{0,1},{1,0},{2,3},{3,2},{4,5},{5,4},{6,7},{7,6},{8,9},{9,8},{10,11... | collective-permute-start | bytes 2654216 | tf_op jit(solution)/shard_map/ppermute | solution.py:181
  215.9 28.3 %collective-permute-start.19 = (bf16[256,768]{1,0:T(8,128)(2,1)S(1)}, bf16[256,768]{1,0:T(8,128)(2,1)S(1)}, u32[]{:S(2)}, u32[]{:S(2)}) collective-permute-start(bf16[256,768]{1,0:T(8,128)(2,1)S(1)} %fusion.63), channel_id=1, source_target_pairs={{0,1},{1,0},{2,3},{3,2},{4,5},{5,4},{6,7},{7,6},{8,9},{9,8},{10,11... | collective-permute-start | bytes 1179656 | tf_op jit(solution)/shard_map/ppermute | solution.py:297
  218.2 26.2 %collective-permute-start.41 = (bf16[2,2,48,768]{3,2,0,1:T(8,128)(2,1)S(1)}, bf16[2,2,48,768]{3,2,0,1:T(8,128)(2,1)S(1)}, u32[]{:S(2)}, u32[]{:S(2)}) collective-permute-start(bf16[2,2,48,768]{3,2,0,1:T(8,128)(2,1)S(1)} %bitcast.422), channel_id=1, source_target_pairs={{0,4},{4,0},{8,12},{12,8},{1,5},{5,1},{9,13},{13,9},{2,6},{6,2},{1... | collective-permute-start | bytes 884744 | tf_op jit(solution)/shard_map/ppermute | solution.py:181
  244.2 13.9 %collective-permute-start.50 = (bf16[2,2,48,1536]{3,2,0,1:T(8,128)(2,1)S(1)}, bf16[2,2,48,1536]{3,2,0,1:T(8,128)(2,1)S(1)}, u32[]{:S(2)}, u32[]{:S(2)}) collective-permute-start(bf16[2,2,48,1536]{3,2,0,1:T(8,128)(2,1)S(1)} %dynamic-slice_bitcast_fusion.9), channel_id=1, source_target_pairs={{0,8},{4,12},{8,0},{12,4},{1,9},{5,13},{9,1},{13,5},{2,10},{6,14},... | collective-permute-start | bytes 1769480 | tf_op jit(solution)/shard_map/ppermute | solution.py:181
  244.4 47.4 %collective-permute-start.20 = (bf16[512,768]{1,0:T(8,128)(2,1)S(1)}, bf16[512,768]{1,0:T(8,128)(2,1)S(1)}, u32[]{:S(2)}, u32[]{:S(2)}) collective-permute-start(bf16[512,768]{1,0:T(8,128)(2,1)S(1)} %fusion.76), channel_id=1, source_target_pairs={{0,16},{16,0},{1,17},{17,1},{2,18},{18,2},{3,19},{19,3},{4,20},{20... | collective-permute-start | bytes 2359304 | tf_op jit(solution)/shard_map/ppermute | solution.py:60
  245.5 14.1 %collective-permute-start.42 = (bf16[2,48,768]{2,1,0:T(8,128)(2,1)S(1)}, bf16[2,48,768]{2,1,0:T(8,128)(2,1)S(1)}, u32[]{:S(2)}, u32[]{:S(2)}) collective-permute-start(bf16[2,48,768]{2,1,0:T(8,128)(2,1)S(1)} %dynamic-slice_bitcast_fusion.24), channel_id=1, source_target_pairs={{0,1},{1,0},{2,3},{3,2},{4,5},{5,4},{6,7},{7,6},{8,9},{9,8},{10,11... | collective-permute-start | bytes 442376 | tf_op jit(solution)/shard_map/ppermute | solution.py:181
  258.0 22.4 %collective-permute-start.32 = (bf16[2,2,48,1152]{3,2,0,1:T(8,128)(2,1)S(1)}, bf16[2,2,48,1152]{3,2,0,1:T(8,128)(2,1)S(1)}, u32[]{:S(2)}, u32[]{:S(2)}) collective-permute-start(bf16[2,2,48,1152]{3,2,0,1:T(8,128)(2,1)S(1)} %dynamic-slice_bitcast_fusion.12), channel_id=1, source_target_pairs={{0,2},{1,3},{2,0},{3,1},{4,6},{5,7},{6,4},{7,5},{8,10},{9,11},{10,... | collective-permute-start | bytes 1327112 | tf_op jit(solution)/shard_map/ppermute | solution.py:181
  259.7 13.8 %collective-permute-start.51 = (bf16[2,48,1536]{2,1,0:T(8,128)(2,1)S(1)}, bf16[2,48,1536]{2,1,0:T(8,128)(2,1)S(1)}, u32[]{:S(2)}, u32[]{:S(2)}) collective-permute-start(bf16[2,48,1536]{2,1,0:T(8,128)(2,1)S(1)} %dynamic-slice_bitcast_fusion.18), channel_id=1, source_target_pairs={{0,1},{1,0},{2,3},{3,2},{4,5},{5,4},{6,7},{7,6},{8,9},{9,8},{10,11... | collective-permute-start | bytes 884744 | tf_op jit(solution)/shard_map/ppermute | solution.py:181
  273.5 152.8 %collective-permute-start.43 = (bf16[48,768]{1,0:T(8,128)(2,1)}, bf16[48,768]{1,0:T(8,128)(2,1)}, u32[]{:S(2)}, u32[]{:S(2)}) collective-permute-start(bf16[48,768]{1,0:T(8,128)(2,1)} %dynamic-slice_bitcast_fusion.28), channel_id=1, source_target_pairs={{0,2},{1,3},{2,0},{3,1},{4,6},{5,7},{6,4},{7,5},{8,10},{9,11},{10,... | collective-permute-start | bytes 221192 | tf_op jit(solution)/shard_map/ppermute | solution.py:181
  280.6 4.8 collective-permute-start.33
  291.6 74.5 %collective-permute-start.64 = (bf16[2,2,192,768]{3,2,0,1:T(8,128)(2,1)}, bf16[2,2,192,768]{3,2,0,1:T(8,128)(2,1)}, u32[]{:S(2)}, u32[]{:S(2)}) collective-permute-start(bf16[2,2,192,768]{3,2,0,1:T(8,128)(2,1)} %bitcast.380), channel_id=1, source_target_pairs={{0,4},{4,0},{8,12},{12,8},{1,5},{5,1},{9,13},{13,9},{2,6},{6,2},{1... | collective-permute-start | bytes 3538952 | tf_op jit(solution)/shard_map/ppermute | solution.py:181
  314.0 12.0 %collective-permute-start.21 = (bf16[512,768]{1,0:T(8,128)(2,1)}, bf16[512,768]{1,0:T(8,128)(2,1)}, u32[]{:S(2)}, u32[]{:S(2)}) collective-permute-start(bf16[512,768]{1,0:T(8,128)(2,1)} %get-tuple-element.118), channel_id=1, source_target_pairs={{0,16},{16,0},{1,17},{17,1},{2,18},{18,2},{3,19},{19,3},{4,20},{20... | collective-permute-start | bytes 2359304 | tf_op jit(solution)/shard_map/ppermute | solution.py:60
  318.4 50.5 %collective-permute-start.45 = (bf16[2,2,2,48,1536]{4,3,1,2,0:T(8,128)(2,1)}, bf16[2,2,2,48,1536]{4,3,1,2,0:T(8,128)(2,1)}, u32[]{:S(2)}, u32[]{:S(2)}) collective-permute-start(bf16[2,2,2,48,1536]{4,3,1,2,0:T(8,128)(2,1)} %bitcast.383), channel_id=1, source_target_pairs={{0,4},{4,0},{8,12},{12,8},{1,5},{5,1},{9,13},{13,9},{2,6},{6,2},{1... | collective-permute-start | bytes 3538952 | tf_op jit(solution)/shard_map/ppermute | solution.py:181
  359.5 13.9 %collective-permute-start.36 = (bf16[384,768]{1,0:T(8,128)(2,1)}, bf16[384,768]{1,0:T(8,128)(2,1)S(1)}, u32[]{:S(2)}, u32[]{:S(2)}) collective-permute-start(bf16[384,768]{1,0:T(8,128)(2,1)} %convolution_convert_fusion.11), channel_id=1, source_target_pairs={{8,0},{12,4},{16,24},{20,28},{9,1},{13,5},{17,25},{21,29},{10,2},{... | collective-permute-start | bytes 1769480 | tf_op jit(solution)/shard_map/ppermute | solution.py:380
  366.1 33.0 %collective-permute-start.27 = (bf16[2,2,2,48,1152]{4,3,2,1,0:T(8,128)(2,1)S(1)}, bf16[2,2,2,48,1152]{4,3,2,1,0:T(8,128)(2,1)S(1)}, u32[]{:S(2)}, u32[]{:S(2)}) collective-permute-start(bf16[2,2,2,48,1152]{4,3,2,1,0:T(8,128)(2,1)S(1)} %dynamic-slice_bitcast_fusion.2), channel_id=1, source_target_pairs={{0,1},{1,0},{2,3},{3,2},{4,5},{5,4},{6,7},{7,6},{8,9},{9,8},{10,11... | collective-permute-start | bytes 2654216 | tf_op jit(solution)/shard_map/ppermute | solution.py:181
  371.0 93.0 %collective-permute-start.52 = (bf16[48,1536]{1,0:T(8,128)(2,1)S(1)}, bf16[48,1536]{1,0:T(8,128)(2,1)S(1)}, u32[]{:S(2)}, u32[]{:S(2)}) collective-permute-start(bf16[48,1536]{1,0:T(8,128)(2,1)S(1)} %copy-done.71), channel_id=1, source_target_pairs={{0,2},{1,3},{2,0},{3,1},{4,6},{5,7},{6,4},{7,5},{8,10},{9,11},{10,... | collective-permute-start | bytes 442376 | tf_op jit(solution)/shard_map/ppermute | solution.py:181
  373.4 25.3 %collective-permute-start.23 = (bf16[256,768]{1,0:T(8,128)(2,1)S(1)}, bf16[256,768]{1,0:T(8,128)(2,1)S(1)}, u32[]{:S(2)}, u32[]{:S(2)}) collective-permute-start(bf16[256,768]{1,0:T(8,128)(2,1)S(1)} %fusion.62), channel_id=1, source_target_pairs={{0,1},{1,0},{2,3},{3,2},{4,5},{5,4},{6,7},{7,6},{8,9},{9,8},{10,11... | collective-permute-start | bytes 1179656 | tf_op jit(solution)/shard_map/ppermute | solution.py:297
  398.7 13.8 %collective-permute-start.65 = (bf16[2,192,768]{2,1,0:T(8,128)(2,1)S(1)}, bf16[2,192,768]{2,1,0:T(8,128)(2,1)S(1)}, u32[]{:S(2)}, u32[]{:S(2)}) collective-permute-start(bf16[2,192,768]{2,1,0:T(8,128)(2,1)S(1)} %dynamic-slice_bitcast_fusion.7), channel_id=1, source_target_pairs={{0,1},{1,0},{2,3},{3,2},{4,5},{5,4},{6,7},{7,6},{8,9},{9,8},{10,11... | collective-permute-start | bytes 1769480 | tf_op jit(solution)/shard_map/ppermute | solution.py:181
  399.1 7.4 %collective-permute-start.37 = (bf16[2,2,48,768]{3,2,0,1:T(8,128)(2,1)S(1)}, bf16[2,2,48,768]{3,2,0,1:T(8,128)(2,1)S(1)}, u32[]{:S(2)}, u32[]{:S(2)}) collective-permute-start(bf16[2,2,48,768]{3,2,0,1:T(8,128)(2,1)S(1)} %bitcast.421), channel_id=1, source_target_pairs={{0,4},{4,0},{8,12},{12,8},{1,5},{5,1},{9,13},{13,9},{2,6},{6,2},{1... | collective-permute-start | bytes 884744 | tf_op jit(solution)/shard_map/ppermute | solution.py:181
  406.5 12.7 %collective-permute-start.46 = (bf16[2,2,48,1536]{3,2,0,1:T(8,128)(2,1)S(1)}, bf16[2,2,48,1536]{3,2,0,1:T(8,128)(2,1)S(1)}, u32[]{:S(2)}, u32[]{:S(2)}) collective-permute-start(bf16[2,2,48,1536]{3,2,0,1:T(8,128)(2,1)S(1)} %dynamic-slice_bitcast_fusion.10), channel_id=1, source_target_pairs={{0,8},{4,12},{8,0},{12,4},{1,9},{5,13},{9,1},{13,5},{2,10},{6,14},... | collective-permute-start | bytes 1769480 | tf_op jit(solution)/shard_map/ppermute | solution.py:181
  412.5 101.7 %collective-permute-start.34 = (bf16[48,1152]{1,0:T(8,128)(2,1)}, bf16[48,1152]{1,0:T(8,128)(2,1)}, u32[]{:S(2)}, u32[]{:S(2)}) collective-permute-start(bf16[48,1152]{1,0:T(8,128)(2,1)} %dynamic-slice_bitcast_fusion.26), channel_id=1, source_target_pairs={{0,8},{4,12},{8,0},{12,4},{1,9},{5,13},{9,1},{13,5},{2,10},{6,14},... | collective-permute-start | bytes 331784 | tf_op jit(solution)/shard_map/ppermute | solution.py:181
  419.1 4.4 collective-permute-start.38
  423.6 5.2 collective-permute-start.39
  426.3 15.0 %collective-permute-start.47 = (bf16[2,48,1536]{2,1,0:T(8,128)(2,1)S(1)}, bf16[2,48,1536]{2,1,0:T(8,128)(2,1)S(1)}, u32[]{:S(2)}, u32[]{:S(2)}) collective-permute-start(bf16[2,48,1536]{2,1,0:T(8,128)(2,1)S(1)} %dynamic-slice_bitcast_fusion.19), channel_id=1, source_target_pairs={{0,1},{1,0},{2,3},{3,2},{4,5},{5,4},{6,7},{7,6},{8,9},{9,8},{10,11... | collective-permute-start | bytes 884744 | tf_op jit(solution)/shard_map/ppermute | solution.py:181
  429.7 7.7 %collective-permute-start.44 = (bf16[48,768]{1,0:T(8,128)(2,1)S(1)}, bf16[48,768]{1,0:T(8,128)(2,1)S(1)}, u32[]{:S(2)}, u32[]{:S(2)}) collective-permute-start(bf16[48,768]{1,0:T(8,128)(2,1)S(1)} %broadcast_select_fusion.18), channel_id=1, source_target_pairs={{0,16},{16,0},{1,17},{17,1},{2,18},{18,2},{3,19},{19,3},{4,20},{20... | collective-permute-start | bytes 221192 | tf_op jit(solution)/shard_map/ppermute | solution.py:60
  437.4 45.2 %collective-permute-start.59 = (bf16[1536,768]{1,0:T(8,128)(2,1)S(1)}, bf16[1536,768]{1,0:T(8,128)(2,1)S(1)}, u32[]{:S(2)}, u32[]{:S(2)}) collective-permute-start(bf16[1536,768]{1,0:T(8,128)(2,1)S(1)} %copy-done.48), channel_id=1, source_target_pairs={{8,0},{12,4},{16,24},{20,28},{9,1},{13,5},{17,25},{21,29},{10,2},{... | collective-permute-start | bytes 7077896 | tf_op jit(solution)/shard_map/ppermute | solution.py:380
  441.3 22.5 %collective-permute-start.28 = (bf16[2,2,48,1152]{3,2,1,0:T(8,128)(2,1)S(1)}, bf16[2,2,48,1152]{3,2,1,0:T(8,128)(2,1)S(1)}, u32[]{:S(2)}, u32[]{:S(2)}) collective-permute-start(bf16[2,2,48,1152]{3,2,1,0:T(8,128)(2,1)S(1)} %dynamic-slice_bitcast_fusion.13), channel_id=1, source_target_pairs={{0,2},{1,3},{2,0},{3,1},{4,6},{5,7},{6,4},{7,5},{8,10},{9,11},{10,... | collective-permute-start | bytes 1327112 | tf_op jit(solution)/shard_map/ppermute | solution.py:181
  463.8 9.1 %collective-permute-start.48 = (bf16[48,1536]{1,0:T(8,128)(2,1)S(1)}, bf16[48,1536]{1,0:T(8,128)(2,1)S(1)}, u32[]{:S(2)}, u32[]{:S(2)}) collective-permute-start(bf16[48,1536]{1,0:T(8,128)(2,1)S(1)} %dynamic-slice_bitcast_fusion.23), channel_id=1, source_target_pairs={{0,2},{1,3},{2,0},{3,1},{4,6},{5,7},{6,4},{7,5},{8,10},{9,11},{10,... | collective-permute-start | bytes 442376 | tf_op jit(solution)/shard_map/ppermute | solution.py:181
  464.0 20.5 %collective-permute-start.24 = (bf16[512,768]{1,0:T(8,128)(2,1)S(1)}, bf16[512,768]{1,0:T(8,128)(2,1)S(1)}, u32[]{:S(2)}, u32[]{:S(2)}) collective-permute-start(bf16[512,768]{1,0:T(8,128)(2,1)S(1)} %fusion.75), channel_id=1, source_target_pairs={{0,16},{16,0},{1,17},{17,1},{2,18},{18,2},{3,19},{19,3},{4,20},{20... | collective-permute-start | bytes 2359304 | tf_op jit(solution)/shard_map/ppermute | solution.py:60
  472.9 5.7 %collective-permute-start.29 = (bf16[2,48,1152]{2,1,0:T(8,128)(2,1)S(1)}, bf16[2,48,1152]{2,1,0:T(8,128)(2,1)S(1)}, u32[]{:S(2)}, u32[]{:S(2)}) collective-permute-start(bf16[2,48,1152]{2,1,0:T(8,128)(2,1)S(1)} %dynamic-slice_bitcast_fusion.21), channel_id=1, source_target_pairs={{0,4},{4,0},{8,12},{12,8},{1,5},{5,1},{9,13},{13,9},{2,6},{6,2},{1... | collective-permute-start | bytes 663560 | tf_op jit(solution)/shard_map/ppermute | solution.py:181
  478.6 3.2 collective-permute-start.53
  481.8 61.0 %collective-permute-start.66 = (bf16[192,768]{1,0:T(8,128)(2,1)}, bf16[192,768]{1,0:T(8,128)(2,1)}, u32[]{:S(2)}, u32[]{:S(2)}) collective-permute-start(bf16[192,768]{1,0:T(8,128)(2,1)} %dynamic-slice_bitcast_fusion.16), channel_id=1, source_target_pairs={{0,2},{1,3},{2,0},{3,1},{4,6},{5,7},{6,4},{7,5},{8,10},{9,11},{10,... | collective-permute-start | bytes 884744 | tf_op jit(solution)/shard_map/ppermute | solution.py:181
  482.7 31.6 %collective-permute-start.30 = (bf16[48,1152]{1,0:T(8,128)(2,1)}, bf16[48,1152]{1,0:T(8,128)(2,1)}, u32[]{:S(2)}, u32[]{:S(2)}) collective-permute-start(bf16[48,1152]{1,0:T(8,128)(2,1)} %dynamic-slice_bitcast_fusion.27), channel_id=1, source_target_pairs={{0,8},{4,12},{8,0},{12,4},{1,9},{5,13},{9,1},{13,5},{2,10},{6,14},... | collective-permute-start | bytes 331784 | tf_op jit(solution)/shard_map/ppermute | solution.py:181
  496.9 2.5 collective-permute-start.55
  499.5 26.2 %collective-permute-start.60 = (bf16[2,2,192,768]{3,2,0,1:T(8,128)(2,1)}, bf16[2,2,192,768]{3,2,0,1:T(8,128)(2,1)S(1)}, u32[]{:S(2)}, u32[]{:S(2)}) collective-permute-start(bf16[2,2,192,768]{3,2,0,1:T(8,128)(2,1)} %bitcast.419), channel_id=1, source_target_pairs={{0,4},{4,0},{8,12},{12,8},{1,5},{5,1},{9,13},{13,9},{2,6},{6,2},{1... | collective-permute-start | bytes 3538952 | tf_op jit(solution)/shard_map/ppermute | solution.py:181
  500.4 5.2 collective-permute-start.56
  505.7 3.2 collective-permute-start.57
  508.8 3.4 collective-permute-start.58
  512.2 45.1 %collective-permute-start.26 = (bf16[256,768]{1,0:T(8,128)(2,1)S(1)}, bf16[256,768]{1,0:T(8,128)(2,1)S(1)}, u32[]{:S(2)}, u32[]{:S(2)}) collective-permute-start(bf16[256,768]{1,0:T(8,128)(2,1)S(1)} %select_convert_fusion.1), channel_id=1, source_target_pairs={{0,3},{1,2},{2,1},{3,0},{4,7},{5,6},{6,5},{7,4},{8,11},{9,10},{10,... | collective-permute-start | bytes 1179656 | tf_op jit(solution)/shard_map/ppermute | solution.py:437
  515.3 5.3 collective-permute-start.35
  526.0 13.3 %collective-permute-start.61 = (bf16[2,192,768]{2,1,0:T(8,128)(2,1)S(1)}, bf16[2,192,768]{2,1,0:T(8,128)(2,1)S(1)}, u32[]{:S(2)}, u32[]{:S(2)}) collective-permute-start(bf16[2,192,768]{2,1,0:T(8,128)(2,1)S(1)} %dynamic-slice_bitcast_fusion.8), channel_id=1, source_target_pairs={{0,1},{1,0},{2,3},{3,2},{4,5},{5,4},{6,7},{7,6},{8,9},{9,8},{10,11... | collective-permute-start | bytes 1769480 | tf_op jit(solution)/shard_map/ppermute | solution.py:181
  528.1 14.0 %collective-permute-start.68 = (bf16[48,384]{1,0:T(8,128)(2,1)S(1)}, bf16[48,384]{1,0:T(8,128)(2,1)S(1)}, u32[]{:S(2)}, u32[]{:S(2)}) collective-permute-start(bf16[48,384]{1,0:T(8,128)(2,1)S(1)} %slice.190), channel_id=1, source_target_pairs={{0,16},{16,0},{1,17},{17,1},{2,18},{18,2},{3,19},{19,3},{4,20},{20... | collective-permute-start | bytes 110600 | tf_op jit(solution)/shard_map/ppermute | solution.py:60
  539.5 15.2 %collective-permute-start.62 = (bf16[192,768]{1,0:T(8,128)(2,1)S(1)}, bf16[192,768]{1,0:T(8,128)(2,1)S(1)}, u32[]{:S(2)}, u32[]{:S(2)}) collective-permute-start(bf16[192,768]{1,0:T(8,128)(2,1)S(1)} %dynamic-slice_bitcast_fusion.17), channel_id=1, source_target_pairs={{0,2},{1,3},{2,0},{3,1},{4,6},{5,7},{6,4},{7,5},{8,10},{9,11},{10,... | collective-permute-start | bytes 884744 | tf_op jit(solution)/shard_map/ppermute | solution.py:181
  555.8 2.8 collective-permute-start.67
  (90 other events, 576.8 us)

commit v2 on v1

--- a/solution.py
+++ b/solution.py
@@ -60,50 +60,447 @@
     return lax.ppermute(x, "section", [(0, 1), (1, 0)])
 
 
-def fwd_attention_kernel(T, q_ref, k_ref, v_ref, qpos_ref, qseg_ref, kseg_ref, o_ref, lse_ref, bias):
-    L = k_ref.shape[0]
-
-    @pl.when(pl.program_id(0) == 0)
-    def _():
-        kpos = lax.broadcasted_iota(jnp.int32, (2 * T, L), 1)
-        allowed = (kpos <= qpos_ref[...]) & (kseg_ref[...] == qseg_ref[...])
-        bias[...] = jnp.where(allowed, 0.0, MASKED)
-
+MESH = pl.DeviceIdType.MESH
+HBM = pl.BlockSpec(memory_space=pl.ANY)
+VM = pl.BlockSpec(memory_space=pltpu.VMEM)
+
+
+class Sems:
+    def __init__(self, ref):
+        self.ref, self.used = ref, 0
+
+    def one(self):
+        self.used += 1
+        return self.ref.at[self.used - 1]
+
+
+def push(src, dst, send, recv, to):
+    return pltpu.make_async_remote_copy(src_ref=src, dst_ref=dst, send_sem=send, recv_sem=recv, device_id=to,
+                                        device_id_type=MESH)
+
+
+def greet(peers):
+    barrier = pltpu.get_barrier_semaphore()
+    for peer in peers:
+        pl.semaphore_signal(barrier, inc=1, device_id=peer, device_id_type=MESH)
+    pl.semaphore_wait(barrier, len(peers))
+
+
+def attention_block(l, blk, T, keys, pairs, q, k, v, o, lse, bias):
+    rows = slice(blk * T, (blk + 1) * T)
     lane = lax.broadcasted_iota(jnp.int32, (T, 128), 1)
-    for part in range(2):
-        rows = slice(part * T, (part + 1) * T)
-        keys = L // 2 if part == 0 else L
-        q2 = q_ref[rows, :]
+
+    def body(i, carry):
+        cols = pl.ds(pl.multiple_of(i * 128, 128), 128)
+        q2 = q[l, rows, cols] * jnp.asarray(HEAD**-0.5, BF16)
+        k2 = k[l, :keys, cols]
+        v2 = jnp.concatenate([v[l, :keys, cols], jnp.ones((keys, 128), BF16)], axis=1)
         outs, lses = [], []
         for h in range(2):
-            qh = jnp.where((lane >= 64) == (h == 1), q2, jnp.zeros_like(q2)) * jnp.asarray(HEAD**-0.5, BF16)
-            s = mm_nt(qh, k_ref[:keys, :]) + bias[rows, :keys]
+            qh = jnp.where((lane >= 64) == (h == 1), q2, jnp.zeros_like(q2))
+            s = mm_nt(qh, k2) + bias[rows, :keys]
             top = jnp.max(s, axis=-1, keepdims=True)
-            e = jnp.exp(s - top)
-            total = jnp.sum(e, axis=-1, keepdims=True)
-            prob = (e * (1.0 / total)).astype(BF16)
-            outs.append(mm(prob, v_ref[:keys, :]))
+            e = jnp.exp(s - top).astype(BF16)
+            both = mm(e, v2)
+            total = both[:, 128:]
+            outs.append(both[:, :128] / total)
             lses.append(top + jnp.log(total))
-        o_ref[rows, :] = jnp.where(lane < 64, outs[0], outs[1]).astype(BF16)
-        lse_ref[0, rows, :] = jnp.where(lane < 64, lses[0], lses[1])
-
-
-def fwd_attention(q, k, v, qpos, qseg, kseg):
-    rows, width = q.shape
-    T, L = rows // 2, k.shape[0]
-    pairs = width // 128
-    col = lambda n: pl.BlockSpec((n, 128), lambda i: (0, i))
-    full = lambda a: pl.BlockSpec(a.shape, lambda i: (0, 0))
+        o[l, rows, cols] = jnp.where(lane < 64, outs[0], outs[1]).astype(BF16)
+        lse[l, i, rows, :] = jnp.where(lane < 64, lses[0], lses[1])
+        return carry
+
+    lax.fori_loop(0, pairs, body, 0)
+
+
+def column(row_values):
+    T = row_values.shape[1]
+    at = lax.broadcasted_iota(jnp.int32, (T, T), 0) == lax.broadcasted_iota(jnp.int32, (T, T), 1)
+    spread = jnp.where(at, jnp.broadcast_to(row_values, (T, T)), 0).astype(F32)
+    return jnp.sum(spread, axis=1, keepdims=True).astype(jnp.int32)
+
+
+def forward_kernel(C, T, D, F, ends, segs, g1, b1, g2, b2, qkv, wo, fc, fcb, proj, shared,
+                   xall_o, q_o, k_o, v_o, o_o, lse_o, r_o, hr_o, hh_o, up_o, act_o, y_o, gy_o, sm_o, wqk_o, wv_o, wout_o,
+                   wfc_o, wproj_o, kseg_o,
+                   e, seg, sm, wqk, wv, wout, wfc, wproj, xall, q, k, v, o, lse, r, hr, hh, up, act, y, bias,
+                   br_s, br_r, ml_s, ml_r, dma):
+    core, dp, z = lax.axis_index("section"), lax.axis_index("dp"), lax.axis_index("ctx")
+    N, L, H, FH = C // 2, C * T, D // 2, F // 2
+    T2 = T // 2
+    row = z // N
+    lo = z + row * (C - 1 - 2 * z)
+    hi = C - 1 - lo
+    base = row * N
+    pairs = H // 128
+    sems = Sems(dma)
+    sib = (1 - core, dp, z)
+    mirror = (core, dp, C - 1 - z)
+    ahead = [(core, dp, base + lax.rem(z - base + n, N)) for n in range(1, N)]
+    behind = [base + lax.rem(z - base + N - n, N) for n in range(1, N)]
+    line = [(core, dp, lax.rem(z + n, C)) for n in range(1, C)]
+    pos = lambda blk: lo + blk * (hi - lo)
+    rows_at = lambda p: pl.ds(pl.multiple_of(p * T, T), T)
+    saves = []
+
+    def save(src, dst):
+        cp = pltpu.make_async_copy(src, dst, sems.one())
+        cp.start()
+        saves.append(cp)
+
+    e_load = pltpu.make_async_copy(ends.at[0, row], e.at[core, row], sems.one())
+    e_load.start()
+    qc = pl.ds(pl.multiple_of(core * H, 128), H)
+    kc = pl.ds(pl.multiple_of(D + core * H, 128), H)
+    qo = pl.ds(pl.multiple_of((1 - core) * H, 128), H)
+    ko = pl.ds(pl.multiple_of(D + (1 - core) * H, 128), H)
+    loads = [
+        pltpu.make_async_copy(qkv.at[0, :, qc], wqk.at[core, :, pl.ds(0, H)], sems.one()),
+        pltpu.make_async_copy(qkv.at[0, :, kc], wqk.at[core, :, pl.ds(H, H)], sems.one()),
+        pltpu.make_async_copy(wo.at[0, pl.ds(pl.multiple_of(core * H, H), H), :], wout.at[core], sems.one()),
+        pltpu.make_async_copy(fc.at[0, :, pl.ds(pl.multiple_of(core * FH, 128), FH)], wfc.at[core], sems.one()),
+        pltpu.make_async_copy(proj.at[0, pl.ds(pl.multiple_of(core * FH, FH), FH), :], wproj.at[core], sems.one()),
+    ]
+    for cp in loads:
+        cp.start()
+    v_sem = sems.one()
+    v_shared = pltpu.make_async_copy(shared, wv.at[0], v_sem)
+    v_fresh = pltpu.make_async_copy(qkv.at[0, :, pl.ds(2 * D, H)], wv.at[1], v_sem)
+
+    @pl.when(core == 0)
+    def _():
+        v_shared.start()
+
+    @pl.when(core == 1)
+    def _():
+        v_fresh.start()
+
+    seg_load = pltpu.make_async_copy(segs.at[row], seg.at[z], sems.one())
+    seg_load.start()
+    sm[core] = jnp.zeros_like(sm[core])
+    sm[core, 0:1, :D] = g1[...]
+    sm[core, 1:2, :D] = b1[...]
+    sm[core, 2:3, :D] = g2[...]
+    sm[core, 3:4, :D] = b2[...]
+    sm[core, 4:5, :] = fcb[...]
+
+    greet([sib] + line)
+
+    own_s, own_r = sems.one(), sems.one()
+    own_push = push(ends.at[0, row], e.at[core, row], own_s, own_r, sib)
+    own_come = push(ends.at[0, row], e.at[1 - core, row], own_s, own_r, sib)
+    far_s, far_r = sems.one(), sems.one()
+    far_push = push(ends.at[0, 1 - row], e.at[core, row], far_s, far_r, mirror)
+    far_come = push(ends.at[0, 1 - row], e.at[core, 1 - row], far_s, far_r, mirror)
+    fwd_s, fwd_r = sems.one(), sems.one()
+    fwd_push = push(e.at[core, 1 - row], e.at[core, 1 - row], fwd_s, fwd_r, sib)
+    fwd_come = push(e.at[1 - core, 1 - row], e.at[1 - core, 1 - row], fwd_s, fwd_r, sib)
+
+    @pl.when(core == 0)
+    def _():
+        far_push.start()
+
+    own_push.start()
+    sm_push = push(sm.at[core], sm.at[core], sems.one(), sems.one(), sib)
+    sm_push.start()
+    seg_push = []
+    for n in range(1, C):
+        to = lax.rem(z + n, C)
+        cp = push(segs.at[to // N], seg.at[z], sems.one(), sems.one(), line[n - 1])
+        cp.start()
+        seg_push.append(cp)
+    qk_push = [
+        push(qkv.at[0, :, qo], wqk.at[core, :, pl.ds(0, H)], sems.one(), sems.one(), sib),
+        push(qkv.at[0, :, ko], wqk.at[core, :, pl.ds(H, H)], sems.one(), sems.one(), sib),
+    ]
+    for cp in qk_push:
+        cp.start()
+    v_push = push(qkv.at[0, :, pl.ds(2 * D, H)], wv.at[0], sems.one(), sems.one(), sib)
+
+    @pl.when(core == 0)
+    def _():
+        v_push.start()
+
+    rest_push = [
+        push(wo.at[0, pl.ds(pl.multiple_of((1 - core) * H, H), H), :], wout.at[core], sems.one(), sems.one(), sib),
+        push(fc.at[0, :, pl.ds(pl.multiple_of((1 - core) * FH, 128), FH)], wfc.at[core], sems.one(), sems.one(), sib),
+        push(proj.at[0, pl.ds(pl.multiple_of((1 - core) * FH, FH), FH), :], wproj.at[core], sems.one(), sems.one(), sib),
+    ]
+
+    seg_load.wait()
+    for n, cp in enumerate(seg_push):
+        cp.wait()
+    kseg = jnp.concatenate([seg[n] for n in range(C)], axis=1)
+    kseg_o[...] = kseg
+    for blk in range(2):
+        rows = slice(blk * T, (blk + 1) * T)
+        qpos = pos(blk) * T + lax.broadcasted_iota(jnp.int32, (T, L), 0)
+        kpos = lax.broadcasted_iota(jnp.int32, (T, L), 1)
+        allowed = (kpos <= qpos) & (kseg == column(seg[pos(blk)]))
+        bias[rows, :] = jnp.where(allowed, 0.0, MASKED)
+
+    xh_sends = {}
+
+    def normed_block(l, turn, blk, values):
+        p = pos(blk)
+        xall[l, rows_at(p), :] = layer_norm(values, sm[l, 0:1, :D], sm[l, 1:2, :D]).astype(BF16)
+        for n in range(N - 1):
+            part = xall.at[l, pl.ds(pl.multiple_of(p * T + core * T2, T2), T2), :]
+            s, rsem = sems.one(), sems.one()
+            cp = push(part, part, s, rsem, ahead[n])
+            cp.start()
+            src = behind[n]
+            slo = src + row * (C - 1 - 2 * src)
+            sp = slo + blk * (C - 1 - 2 * slo)
+            got = xall.at[l, pl.ds(pl.multiple_of(sp * T + core * T2, T2), T2), :]
+            other = xall.at[l, pl.ds(pl.multiple_of(sp * T + (1 - core) * T2, T2), T2), :]
+            come = push(got, got, s, rsem, ahead[n])
+            fs, fr = sems.one(), sems.one()
+            onward = push(got, got, fs, fr, sib)
+            arrive = push(other, other, fs, fr, sib)
+            xh_sends[(l, turn, n)] = (cp, come, onward, arrive, sp)
+
+    def own_products(l, blk):
+        p = pos(blk)
+        xh = xall[l, rows_at(p), :]
+        both = mm(xh, wqk[l])
+        q[l, blk * T : (blk + 1) * T, :] = both[:, :H].astype(BF16)
+        k[l, rows_at(p), :] = both[:, H:].astype(BF16)
+
+    def value_products(l, p):
+        src = l * core
+        v[l, rows_at(p), :] = mm(xall[src, rows_at(p), :], wv[src]).astype(BF16)
+
+    def key_products(l, p):
+        k[l, rows_at(p), :] = mm(xall[l, rows_at(p), :], wqk[l, :, H:]).astype(BF16)
+
+    @pl.when(core == 0)
+    def _():
+        e_load.wait()
+
+    @pl.when(core == 1)
+    def _():
+        own_come.wait_recv()
+
+    sm_push.wait()
+    blk = row
+    r[0, pl.ds(pl.multiple_of(blk * T, T), T), :] = e[0, blk]
+    normed_block(0, 0, blk, e[0, blk].astype(F32))
+
+    @pl.when(core == 0)
+    def _():
+        loads[0].wait()
+        loads[1].wait()
+        v_shared.wait()
+
+    @pl.when(core == 1)
+    def _():
+        for cp in qk_push:
+            cp.wait_recv()
+        v_push.wait_recv()
+
+    def own_products_dynamic(l, blk):
+        p = pos(blk)
+        both = mm(xall[l, rows_at(p), :], wqk[l])
+        q[l, pl.ds(pl.multiple_of(blk * T, T), T), :] = both[:, :H].astype(BF16)
+        k[l, rows_at(p), :] = both[:, H:].astype(BF16)
+        value_products(l, p)
+
+    own_products_dynamic(0, blk)
+    blk = 1 - row
+
+    @pl.when(core == 0)
+    def _():
+        far_come.wait_recv()
+        fwd_push.start()
+
+    @pl.when(core == 1)
+    def _():
+        fwd_come.wait_recv()
+
+    r[0, pl.ds(pl.multiple_of(blk * T, T), T), :] = e[0, blk]
+    normed_block(0, 1, blk, e[0, blk].astype(F32))
+    own_products_dynamic(0, blk)
+
+    def finish_layer_inputs(l):
+        for turn in range(2):
+            for n in range(N - 1):
+                cp, come, onward, arrive, sp = xh_sends[(l, turn, n)]
+                come.wait_recv()
+                onward.start()
+        for turn in range(2):
+            for n in range(N - 1):
+                cp, come, onward, arrive, sp = xh_sends[(l, turn, n)]
+                arrive.wait_recv()
+                key_products(l, sp)
+                value_products(l, sp)
+
+    def middle(l):
+        sends = []
+        for blk in range(2):
+            rows = slice(blk * T, (blk + 1) * T)
+            attention_block(l, blk, T, L // 2 if blk == 0 else L, pairs, q, k, v, o, lse, bias)
+            if l == 0 and blk == 0:
+                @pl.when(core == 0)
+                def _():
+                    loads[2].wait()
+
+                @pl.when(core == 1)
+                def _():
+                    rest_push[0].wait_recv()
+            if l == 1 and blk == 0:
+                @pl.when(core == 1)
+                def _():
+                    loads[2].wait()
+
+                @pl.when(core == 0)
+                def _():
+                    rest_push[0].wait_recv()
+            part = mm(o[l, rows, :], wout[l])
+            hr[l, rows, :] = part
+            br_s[l, rows, :] = part.astype(BF16)
+            cp = push(br_s.at[l, rows, :], br_r.at[l, rows, :], sems.one(), sems.one(), sib)
+            cp.start()
+            sends.append(cp)
+        save(q.at[l], q_o.at[l])
+        save(k.at[l], k_o.at[l])
+        save(v.at[l], v_o.at[l])
+        save(o.at[l], o_o.at[l])
+        save(lse.at[l], lse_o.at[l])
+        save(xall.at[l], xall_o.at[l])
+        mlps = []
+        for blk in range(2):
+            rows = slice(blk * T, (blk + 1) * T)
+            sends[blk].wait_recv()
+            hidden = r[l, rows, :].astype(F32) + hr[l, rows, :] + br_r[l, rows, :].astype(F32)
+            hr[l, rows, :] = hidden
+            normed2 = layer_norm(hidden, sm[l, 2:3, :D], sm[l, 3:4, :D]).astype(BF16)
+            hh[l, rows, :] = normed2
+            if blk == 0:
+                local = core == l
+
+                @pl.when(local)
+                def _():
+                    loads[3].wait()
+                    loads[4].wait()
+
+                @pl.when(jnp.logical_not(local))
+                def _():
+                    rest_push[1].wait_recv()
+                    rest_push[2].wait_recv()
+            mine = pl.ds(pl.multiple_of(core * FH, 128), FH)
+            u = mm(normed2, wfc[l]) + sm[l, 4:5, mine]
+            up[l, rows, :] = u
+            a = gelu(u).astype(BF16)
+            act[l, rows, :] = a
+            part = mm(a, wproj[l])
+            y[rows, :] = part
+            ml_s[l, rows, :] = part.astype(BF16)
+            cp = push(ml_s.at[l, rows, :], ml_r.at[l, rows, :], sems.one(), sems.one(), sib)
+            cp.start()
+            mlps.append(cp)
+        save(hr.at[l], hr_o.at[l])
+        save(hh.at[l], hh_o.at[l])
+        save(up.at[l], up_o.at[l])
+        save(act.at[l], act_o.at[l])
+        for blk in range(2):
+            rows = slice(blk * T, (blk + 1) * T)
+            mlps[blk].wait_recv()
+            out = hr[l, rows, :] + y[rows, :] + ml_r[l, rows, :].astype(F32)
+            if l == 0:
+                sent = out.astype(BF16)
+                r[1, rows, :] = sent
+                normed_block(1, blk, blk, sent.astype(F32))
+                if blk == 0:
+                    @pl.when(core == 1)
+                    def _():
+                        loads[0].wait()
+                        loads[1].wait()
+                        v_fresh.wait()
+
+                    @pl.when(core == 0)
+                    def _():
+                        for cp in qk_push:
+                            cp.wait_recv()
+                own_products(1, blk)
+                value_products(1, pos(blk))
+            else:
+                y[rows, :] = out
+        return sends + mlps
+
+    finish_layer_inputs(0)
+    for cp in rest_push:
+        cp.start()
+    pair_sends = middle(0)
+
+    @pl.when(core == 1)
+    def _():
+        far_push.start()
+
+    finish_layer_inputs(1)
+    save(r, r_o)
+    pair_sends += middle(1)
+    save(y, y_o)
+
+    @pl.when(core == 1)
+    def _():
+        far_come.wait_recv()
+        fwd_push.start()
+        e_load.wait()
+
+    @pl.when(core == 0)
+    def _():
+        fwd_come.wait_recv()
+        own_come.wait_recv()
+
+    save(e.at[1], gy_o)
+    save(sm, sm_o)
+    save(wqk, wqk_o)
+    save(wv, wv_o)
+    save(wout, wout_o)
+    save(wfc, wfc_o)
+    save(wproj, wproj_o)
+    far_push.wait_send()
+    fwd_push.wait_send()
+    own_push.wait_send()
+    for cp in qk_push + rest_push + pair_sends:
+        cp.wait_send()
+
+    @pl.when(core == 0)
+    def _():
+        v_push.wait_send()
+
+    for cp, come, onward, arrive, sp in xh_sends.values():
+        cp.wait_send()
+        onward.wait_send()
+    for cp in saves:
+        cp.wait()
+
+
+def forward_pass(C, ends, segs, g1, b1, g2, b2, qkv, wo, fc, fcb, proj, shared):
+    T, D, F = ends.shape[2], ends.shape[3], fc.shape[2]
+    N, L, H, FH = C // 2, C * T, D // 2, F // 2
+    R, pairs = 2 * T, D // 256
+    S = jax.ShapeDtypeStruct
+    outs = [S((2, L, D), BF16), S((2, R, H), BF16), S((2, L, H), BF16), S((2, L, H), BF16), S((2, R, H), BF16),
+            S((2, pairs, R, 128), F32), S((2, R, D), BF16), S((2, R, D), F32), S((2, R, D), BF16), S((2, R, FH), F32),
+            S((2, R, FH), BF16), S((R, D), F32), S((2, T, D), BF16), S((2, 8, F), F32), S((2, D, D), BF16),
+            S((2, D, H), BF16), S((2, H, D), BF16), S((2, D, FH), BF16), S((2, FH, D), BF16), S((1, L), jnp.int32)]
+    V = pltpu.VMEM
+    scratch = [V((2, 2, T, D), BF16), V((C, 1, T), jnp.int32), V((2, 8, F), F32), V((2, D, D), BF16), V((2, D, H), BF16),
+               V((2, H, D), BF16), V((2, D, FH), BF16), V((2, FH, D), BF16), V((2, L, D), BF16), V((2, R, H), BF16),
+               V((2, L, H), BF16), V((2, L, H), BF16), V((2, R, H), BF16), V((2, pairs, R, 128), F32), V((2, R, D), BF16),
+               V((2, R, D), F32), V((2, R, D), BF16), V((2, R, FH), F32), V((2, R, FH), BF16), V((R, D), F32),
+               V((R, L), F32), V((2, R, D), BF16), V((2, R, D), BF16), V((2, R, D), BF16), V((2, R, D), BF16),
+               pltpu.SemaphoreType.DMA((80 + 20 * N + 2 * C,))]
     return pl.pallas_call(
-        functools.partial(fwd_attention_kernel, T),
-        grid=(pairs,),
-        in_specs=[col(rows), col(L), col(L), full(qpos), full(qseg), full(kseg)],
-        out_specs=[col(rows), pl.BlockSpec((1, rows, 128), lambda i: (i, 0, 0))],
-        out_shape=[jax.ShapeDtypeStruct((rows, width), BF16), jax.ShapeDtypeStruct((pairs, rows, 128), F32)],
-        scratch_shapes=[pltpu.VMEM((rows, L), F32)],
-        compiler_params=pltpu.CompilerParams(vmem_limit_bytes=VMEM_LIMIT),
-        name="attention_forward",
-    )(q, k, v, qpos, qseg, kseg)
+        functools.partial(forward_kernel, C, T, D, F),
+        in_specs=[HBM, HBM, VM, VM, VM, VM, HBM, HBM, HBM, VM, HBM, HBM],
+        out_specs=[HBM] * 19 + [VM],
+        out_shape=outs,
+        scratch_shapes=scratch,
+        compiler_params=pltpu.CompilerParams(collective_id=0, has_side_effects=True, vmem_limit_bytes=VMEM_LIMIT),
+        name="forward_pass",
+    )(ends, segs, g1, b1, g2, b2, qkv, wo, fc, fcb, proj, shared)
 
 
 def bwd_attention_kernel(T, q_ref, k_ref, v_ref, go_ref, o_ref, lse_ref, qpos_ref, qseg_ref, kseg_ref,
@@ -216,68 +613,31 @@
     reverse = [(i, C - 1 - i) for i in range(C)]
     first = core == 0
 
-    mine = lax.dynamic_index_in_dim(ends[0], row, 0, keepdims=False)
-    other = lax.dynamic_index_in_dim(ends[0], 1 - row, 0, keepdims=False)
-    got = lax.ppermute(other, "ctx", reverse)
-    both = jnp.where(upper, jnp.concatenate([got, mine], 0), jnp.concatenate([mine, got], 0))
-    both_other = swap(both)
-    x_in = jnp.where(first, both, both_other)
-    g_out = jnp.where(first, both_other, both)
-
     lo = jnp.minimum(place, C - 1 - place)
     hi = C - 1 - lo
-    seg_pieces = [(place, segment_ids)]
-    for k in range(1, C):
-        seg_pieces.append((lax.rem(place + C - k, C), lax.ppermute(segment_ids, "ctx", [(i, (i + k) % C) for i in range(C)])))
-    seg_row = jnp.zeros((C, T), jnp.int32)
-    for at, piece in seg_pieces:
-        seg_row = lax.dynamic_update_slice(seg_row, lax.dynamic_index_in_dim(piece, row, 0, keepdims=True), (at, 0))
-    kseg = seg_row.reshape(1, L)
+    (xall, q, k, v, o, lse, r, hr, hh, up, act, y, gy, sm, wqk, wv, wout, wfc, wproj, kseg) = forward_pass(
+        C, ends, segment_ids.reshape(micros, 1, T), ln1_gain, ln1_bias, ln2_gain, ln2_bias, qkv_weight, out_weight,
+        fc_weight, fc_bias, proj_weight, shared_weight)
+    seg_row = kseg.reshape(C, T)
     qseg = jnp.concatenate([lax.dynamic_index_in_dim(seg_row, lo, 0, keepdims=False),
                             lax.dynamic_index_in_dim(seg_row, hi, 0, keepdims=False)]).reshape(2 * T, 1)
     qpos = jnp.concatenate([lo * T + jnp.arange(T), hi * T + jnp.arange(T)]).astype(jnp.int32).reshape(2 * T, 1)
-
-    def qkv_half(c):
-        wq = lax.dynamic_slice_in_dim(qkv_weight[0], c * half, half, 1)
-        wk = lax.dynamic_slice_in_dim(qkv_weight[0], D + c * half, half, 1)
-        wv = jnp.where(c == 0, shared_weight, qkv_weight[0][:, 2 * D :])
-        return jnp.concatenate([wq, wk, wv], axis=1)
-
-    def halves(c):
-        return (qkv_half(c), lax.dynamic_slice_in_dim(out_weight[0], c * half, half, 0),
-                lax.dynamic_slice_in_dim(fc_weight[0], c * FH, FH, 1), lax.dynamic_slice_in_dim(proj_weight[0], c * FH, FH, 0))
-
-    own_half = halves(core)
-    got_half = tuple(swap(w) for w in halves(1 - core))
-    small = jnp.concatenate([ln1_gain[0], ln1_bias[0], ln2_gain[0], ln2_bias[0], fc_bias[0]])
-    small_other = swap(small)
+    g_out = gy.reshape(2 * T, D)
+    reverse = [(i, C - 1 - i) for i in range(C)]
 
     def layer_weights(l):
-        is_own = core == l
-        ws = tuple(jnp.where(is_own, a, b) for a, b in zip(own_half, got_half))
-        sm = jnp.where(is_own, small, small_other)
-        norms = tuple(sm[i * D : (i + 1) * D] for i in range(4))
-        return ws + (norms, lax.dynamic_slice_in_dim(sm, 4 * D + core * FH, FH, 0))
+        wv_l = wv[0] if l == 0 else jnp.where(first, wv[0], wv[1])
+        norms = tuple(sm[l, i, :D] for i in range(4))
+        return (jnp.concatenate([wqk[l], wv_l], axis=1), wout[l], wfc[l], wproj[l], norms,
+                lax.dynamic_slice_in_dim(sm[l, 4], core * FH, FH, 0))
+
+    def saved(l):
+        own = jnp.concatenate([lax.dynamic_slice_in_dim(xall[l], lo * T, T, 0), lax.dynamic_slice_in_dim(xall[l], hi * T, T, 0)], 0)
+        return dict(resid=r[l].astype(F32), normed=own, normed_all=xall[l], value_in=xall[0] if l == 0 else jnp.where(first, xall[0], xall[1]),
+                    q=q[l], k=k[l], v=v[l], o=o[l], lse=lse[l], hidden=hr[l], normed2=hh[l], up=up[l], act=act[l])
 
     weights = [layer_weights(0), layer_weights(1)]
-
-    def to_group(blocks):
-        send = jnp.where(first, blocks[:T], blocks[T:])
-        out = jnp.zeros((C, T, D), blocks.dtype)
-        out = lax.dynamic_update_slice(out, blocks[:T][None], (lo, 0, 0))
-        out = lax.dynamic_update_slice(out, blocks[T:][None], (hi, 0, 0))
-        base = jnp.where(upper, N, 0)
-        for k in range(1, N):
-            route = [(g * N + i, g * N + (i + k) % N) for g in range(2) for i in range(N)]
-            piece = lax.ppermute(send, "ctx", route)
-            other_piece = swap(piece)
-            src = base + lax.rem(place - base + N - k, N)
-            slo = jnp.minimum(src, C - 1 - src)
-            a = jnp.where(first, piece, other_piece)
-            b = jnp.where(first, other_piece, piece)
-            out = lax.dynamic_update_slice(out, a[None], (slo, 0, 0))
-            out = lax.dynamic_update_slice(out, b[None], (C - 1 - slo, 0, 0))
-        return out.reshape(L, D)
+    st0, st1 = saved(0), saved(1)
 
     def from_group(parts):
         parts = parts.reshape(C, T, D)
@@ -303,24 +663,6 @@
 
     def pair_sum(x):
         return x + swap(x.astype(BF16)).astype(F32)
-
-    def forward(l, resid, first_all):
-        wqkv, wout, wfc, wproj, (g1, b1, g2, b2), fcb = weights[l]
-        normed = layer_norm(resid, g1, b1).astype(BF16)
-        normed_all = to_group(normed)
-        source_all = normed_all if l == 0 else first_all
-        value_in = jnp.where(first, source_all, normed_all)
-        q = mm(normed, wqkv[:, :half]).astype(BF16)
-        k = mm(normed_all, wqkv[:, half : 2 * half]).astype(BF16)
-        v = mm(value_in, wqkv[:, 2 * half :]).astype(BF16)
-        o, lse = fwd_attention(q, k, v, qpos, qseg, kseg)
-        hidden = resid + pair_sum(mm(o, wout))
-        normed2 = layer_norm(hidden, g2, b2).astype(BF16)
-        up = mm(normed2, wfc) + fcb
-        act = gelu(up).astype(BF16)
-        out = hidden + pair_sum(mm(act, wproj))
-        return out, dict(resid=resid, normed=normed, normed_all=normed_all, value_in=value_in, q=q, k=k, v=v, o=o,
-                         lse=lse, hidden=hidden, normed2=normed2, up=up, act=act)
 
     def backward(l, st, grad_out, source_part):
         wqkv, wout, wfc, wproj, (g1, b1, g2, b2), fcb = weights[l]
@@ -359,9 +701,6 @@
         v_g = mm_tn(st["value_in"], dv)
         return gr, next_source, (q_g, k_g, v_g, out_g, fc_g, proj_g), (fcb_g, g1_g, b1_g, g2_g, b2_g)
 
-    sent, st0 = forward(0, x_in.astype(F32), None)
-    sent = sent.astype(BF16).astype(F32)
-    y, st1 = forward(1, sent, st0["normed_all"])
     gr1, src, big1, small1 = backward(1, st1, g_out.astype(F32), None)
     gx, _, big0, small0 = backward(0, st0, gr1, src)
 

time: 569 us -> 518 us (0.910)
  matrix products: 102 us -> 48.2 us
  Pallas kernels: 42 us -> 95.3 us
  starting transfers between devices: 86 us -> 57 us
  local copies, waits for them, and re-layouts: 69.5 us -> 58.5 us
  waiting for transfers between devices: 193 us -> 183 us
    pallas_call x2 -> x1, Pallas kernels: 19.7 us -> 73 us  [forward_pass(): pl.pallas_call(functools.partial(forward_kernel, C, T, D, F), in_specs=[H...]
    dot_general x12 -> x0, matrix products: 32.5 us -> none  [mm(): return jnp.dot(left, right, preferred_element_type=F32)]
    ppermute x32, waiting for transfers between devices: 116 us -> 139 us  [halve(): lax.ppermute(send, axis_name, xor_route(lax.axis_size(axis_name), bit))]
    ppermute x6 -> x0, waiting for transfers between devices: 18.8 us -> none  [the longest x2 18.8 us: to_group(): piece = lax.ppermute(send, 'ctx', route)]
    dot_general x12, matrix products: 40.1 us -> 23 us  [mm_nt(): lax.dot_general(left, right, (((1,), (1,)), ((), ())), preferred_element_...]
    ppermute x24 -> x12, starting transfers between devices: 32.6 us -> 17.7 us  [swap(): return lax.ppermute(x, 'section', [(0, 1), (1, 0)])]
    dynamic_slice x14 -> x1, local copies, waits for them, and re-layouts: 12.4 us -> 1.06 us  [saved(): lax.dynamic_slice_in_dim(xall[l], lo * T, T, 0)]
    unnamed x177 -> x166, local copies, waits for them, and re-layouts: 21.5 us -> 10.8 us
  transfers between devices with their start and end apart: 69 -> 51, of which waited for: 30 -> 22; matrix products, arithmetic and copies ran while one was open for 35% -> 29% of each run, Pallas kernels for 6% -> 4%
where the time goes in v2:
time: 518 us; the launch traced here: 508 us
  waiting for transfers between devices  183 us (35%)
  Pallas kernels  95.3 us (18%)
  other arithmetic  63.6 us (12%)
  local copies, waits for them, and re-layouts  58.5 us (11%)
  starting transfers between devices  57 us (11%)
  matrix products  48.2 us (9%)
    ppermute x32, waiting for transfers between devices, halve(): lax.ppermute(send, axis_name, xor_route(lax.axis_size(axis_name), bit))  139 us
    pallas_call x1, Pallas kernels, forward_pass(): pl.pallas_call(functools.partial(forward_kernel, C, T, D, F), in_specs=[H...  73 us
    ppermute x2, waiting for transfers between devices, from_group(): come = lax.ppermute(pair, 'ctx', route).astype(F32)  43.9 us
    dot_general x12, matrix products, mm_tn(): lax.dot_general(left, right, (((0,), (0,)), ((), ())), preferred_element_...  25.2 us
    ppermute x32, starting transfers between devices, halve(): lax.ppermute(send, axis_name, xor_route(lax.axis_size(axis_name), bit))  23.4 us
    dot_general x12, matrix products, mm_nt(): lax.dot_general(left, right, (((1,), (1,)), ((), ())), preferred_element_...  23 us
    pallas_call x2, Pallas kernels, bwd_attention(): pl.pallas_call(functools.partial(bwd_attention_kernel, T), grid=(pairs,),...  22.3 us
    ppermute x12, starting transfers between devices, swap(): return lax.ppermute(x, 'section', [(0, 1), (1, 0)])  17.7 us
  transfers between devices with their start and end apart: 51, of which 22 were waited for; matrix products, arithmetic and copies ran while one was open for 29% of the time, Pallas kernels for 4%

profile of v2, /device:TPU:1, one launch (start us, length us, event | category | flops | bytes accessed | tf_op | source)
XLA Modules:
  0.0 507.9 jit_solution(14804825532806285960)
XLA Ops:
  1.9 73.0 %forward_pass.1 = (bf16[2,1024,768]{2,1,0:T(8,128)(2,1)}, bf16[2,512,384]{2,1,0:T(8,128)(2,1)}, bf16[2,1024,384]{2,1,0:T(8,128)(2,1)}, bf16[2,1024,384]{2,1,0:T(...) custom-call(bf16[1,2,256,768]{3,2,1,0:T(8,128)(2,1)} %ends.1, ...), custom_call_target="tpu_custom_call" | custom-call | tf_op jit(solution)/shard_map/forward_pass/pallas_call | solution.py:495
  74.9 6.4 %convert_reduce_fusion = (f32[1536]{0:T(1024)}, bf16[512,1536]{1,0:T(8,128)(2,1)S(1)}) fusion(bf16[512,768]{1,0:T(8,128)(2,1)} %bitcast.539, bf16[2,1536,768]{2,1,0:T(8,128)(2,1)} %get-tuple-element.44, f32[2,512,1536]{2,1,0:T(8,128)} %get-tuple-element.42), kind=kOutput, calls=%fused_computation.28 | convolution fusion | flops 1224473088 | bytes 7870464 | tf_op jit(solution)/shard_map/dot_general | solution.py:23
  81.3 2.8 fusion.188
  84.7 2.8 convolution_convert_fusion.2
  87.5 3.0 constant_dynamic-slice_fusion.13
  92.8 2.8 convolution_convert_fusion
  95.6 4.5 collective-permute-start.45
  102.4 1.8 convert_reduce_fusion.3
  109.9 1.8 fusion.185
  111.7 2.7 slice_bitcast_fusion.12
  120.3 3.4 slice_bitcast_fusion
  123.8 1.7 slice_bitcast_fusion.10
  126.0 2.7 multiply_reduce_fusion
  134.4 2.6 convert_add_fusion.9
  139.7 2.3 collective-permute-start.22
  142.0 10.9 %attention_backward.2 = (bf16[512,384]{1,0:T(8,128)(2,1)}, f32[1024,384]{1,0:T(8,128)}, f32[1024,384]{1,0:T(8,128)}) custom-call(bf16[512,384]{1,0:T(8,128)(2,1)} %get-tuple-element.156.q_ref, bf16[1024,384]{1,0:T(8,128)(2,1)} %get-tuple-element.154.k_ref, bf16[1024,384]{1,0:T(8,128)(2,1)} %get-tuple-element.123.v_ref, ...), custom_call_target="tpu_custom_call" | custom-call | tf_op jit(solution)/shard_map/attention_backward/pallas_call | solution.py:556
  152.9 2.5 fusion.77
  155.4 2.0 select_convert_fusion
  159.4 1.7 copy-done.32
  170.5 23.8 %collective-permute-done.2 = bf16[256,768]{1,0:T(8,128)(2,1)S(1)} collective-permute-done((bf16[256,768]{1,0:T(8,128)(2,1)S(1)}, bf16[256,768]{1,0:T(8,128)(2,1)S(1)}, u32[]{:S(2)}, u32[]{:S(2)}) %collective-permute-start.2) | collective-permute-done | bytes 393248 | tf_op jit(solution)/shard_map/ppermute | solution.py:657
  196.0 2.3 collective-permute-start.14
  198.8 4.7 collective-permute-done.24
  204.3 10.6 %collective-permute-done.33 = bf16[2,48,1536]{2,1,0:T(8,128)(2,1)S(1)} collective-permute-done((bf16[2,48,1536]{2,1,0:T(8,128)(2,1)S(1)}, bf16[2,48,1536]{2,1,0:T(8,128)(2,1)S(1)}, u32[]{:S(2)}, u32[]{:S(2)}) %collective-permute-start.33) | collective-permute-done | bytes 294944 | tf_op jit(solution)/shard_map/ppermute | solution.py:578
  214.9 3.2 collective-permute-done.14
  219.4 3.7 collective-permute-done.15
  223.9 2.4 fusion.55
  227.0 3.0 convert_reduce_fusion.1
  230.0 2.8 convolution_convert_fusion.3
  232.8 2.8 fusion.189
  235.6 3.0 add_convert_fusion
  242.9 4.7 collective-permute-start.4
  247.6 2.9 constant_dynamic-slice_fusion.15
  254.9 4.8 convolution_convert_fusion.1
  259.7 2.1 multiply_reduce_fusion.1
  261.9 1.8 multiply_add_fusion.2
  266.8 11.4 %attention_backward.3 = (bf16[512,384]{1,0:T(8,128)(2,1)}, f32[1024,384]{1,0:T(8,128)}, f32[1024,384]{1,0:T(8,128)}) custom-call(bf16[512,384]{1,0:T(8,128)(2,1)} %get-tuple-element.157.q_ref, bf16[1024,384]{1,0:T(8,128)(2,1)} %get-tuple-element.155.k_ref, bf16[1024,384]{1,0:T(8,128)(2,1)} %get-tuple-element.122.v_ref, ...), custom_call_target="tpu_custom_call" | custom-call | tf_op jit(solution)/shard_map/attention_backward/pallas_call | solution.py:556
  278.2 2.6 fusion.74
  280.7 2.9 collective-permute-start.18
  303.9 1.9 collective-permute-start.16
  308.1 20.2 %collective-permute-done.6 = bf16[256,768]{1,0:T(8,128)(2,1)S(1)} collective-permute-done((bf16[256,768]{1,0:T(8,128)(2,1)S(1)}, bf16[256,768]{1,0:T(8,128)(2,1)S(1)}, u32[]{:S(2)}, u32[]{:S(2)}) %collective-permute-start.6) | collective-permute-done | bytes 393248 | tf_op jit(solution)/shard_map/ppermute | solution.py:657
  329.8 7.0 %collective-permute-done.19 = bf16[2,2,48,768]{3,2,0,1:T(8,128)(2,1)S(1)} collective-permute-done((bf16[2,2,48,768]{3,2,0,1:T(8,128)(2,1)S(1)}, bf16[2,2,48,768]{3,2,0,1:T(8,128)(2,1)S(1)}, u32[]{:S(2)}, u32[]{:S(2)}) %collective-permute-start.19) | collective-permute-done | bytes 294944 | tf_op jit(solution)/shard_map/ppermute | solution.py:578
  336.9 6.5 %collective-permute-done.28 = bf16[2,2,48,1536]{3,2,0,1:T(8,128)(2,1)S(1)} collective-permute-done((bf16[2,2,48,1536]{3,2,0,1:T(8,128)(2,1)S(1)}, bf16[2,2,48,1536]{3,2,0,1:T(8,128)(2,1)S(1)}, u32[]{:S(2)}, u32[]{:S(2)}) %collective-permute-start.28) | collective-permute-done | bytes 589856 | tf_op jit(solution)/shard_map/ppermute | solution.py:578
  343.3 3.3 collective-permute-start.41
  346.7 3.7 collective-permute-done.47
  350.9 3.9 collective-permute-done.20
  357.5 2.4 collective-permute-done.21
  360.9 4.0 collective-permute-start.26
  368.9 21.1 %collective-permute-done.10 = bf16[2,2,48,1152]{3,2,0,1:T(8,128)(2,1)S(1)} collective-permute-done((bf16[2,2,48,1152]{3,2,0,1:T(8,128)(2,1)S(1)}, bf16[2,2,48,1152]{3,2,0,1:T(8,128)(2,1)S(1)}, u32[]{:S(2)}, u32[]{:S(2)}) %collective-permute-start.10) | collective-permute-done | bytes 442400 | tf_op jit(solution)/shard_map/ppermute | solution.py:578
  390.3 2.4 collective-permute-start.48
  392.7 13.3 %collective-permute-done.30 = bf16[48,1536]{1,0:T(8,128)(2,1)S(1)} collective-permute-done((bf16[48,1536]{1,0:T(8,128)(2,1)S(1)}, bf16[48,1536]{1,0:T(8,128)(2,1)S(1)}, u32[]{:S(2)}, u32[]{:S(2)}) %collective-permute-start.30) | collective-permute-done | bytes 147488 | tf_op jit(solution)/shard_map/ppermute | solution.py:578
  407.4 5.1 collective-permute-done.11
  414.8 1.9 collective-permute-start.12
  417.7 2.5 fusion.43
  424.4 3.6 fusion.42
  432.4 3.1 add_convert_fusion.1
  435.7 4.8 collective-permute-done.39
  440.5 3.2 collective-permute-start.40
  444.0 3.7 collective-permute-done.40
  448.9 1.9 collective-permute-start.17
  452.9 20.7 %collective-permute-done.42 = bf16[2,2,192,768]{3,2,0,1:T(8,128)(2,1)S(1)} collective-permute-done((bf16[2,2,192,768]{3,2,0,1:T(8,128)(2,1)S(1)}, bf16[2,2,192,768]{3,2,0,1:T(8,128)(2,1)S(1)}, u32[]{:S(2)}, u32[]{:S(2)}) %collective-permute-start.42) | collective-permute-done | bytes 1179680 | tf_op jit(solution)/shard_map/ppermute | solution.py:578
  474.1 2.5 collective-permute-start.50
  476.6 9.7 %collective-permute-done.43 = bf16[2,192,768]{2,1,0:T(8,128)(2,1)S(1)} collective-permute-done((bf16[2,192,768]{2,1,0:T(8,128)(2,1)S(1)}, bf16[2,192,768]{2,1,0:T(8,128)(2,1)S(1)}, u32[]{:S(2)}, u32[]{:S(2)}) %collective-permute-start.43) | collective-permute-done | bytes 589856 | tf_op jit(solution)/shard_map/ppermute | solution.py:578
  489.3 13.1 %collective-permute-done.44 = bf16[192,768]{1,0:T(8,128)(2,1)S(1)} collective-permute-done((bf16[192,768]{1,0:T(8,128)(2,1)S(1)}, bf16[192,768]{1,0:T(8,128)(2,1)S(1)}, u32[]{:S(2)}, u32[]{:S(2)}) %collective-permute-start.44) | collective-permute-done | bytes 294944 | tf_op jit(solution)/shard_map/ppermute | solution.py:578
  505.8 2.0 bitcast_convert_fusion.1
  (411 shorter events, 111.1 us)
Async XLA Ops:
  84.2 41.3 %collective-permute-start = (bf16[512,768]{1,0:T(8,128)(2,1)}, bf16[512,768]{1,0:T(8,128)(2,1)}, u32[]{:S(2)}, u32[]{:S(2)}) collective-permute-start(bf16[512,768]{1,0:T(8,128)(2,1)} %get-tuple-element.144), channel_id=1, source_target_pairs={{0,16},{16,0},{1,17},{17,1},{2,18},{18,2},{3,19},{19,3},{4,20},{20... | collective-permute-start | bytes 2359304 | tf_op jit(solution)/shard_map/ppermute | solution.py:60
  91.6 75.3 %collective-permute-start.31 = (bf16[2,2,2,48,1536]{4,3,1,2,0:T(8,128)(2,1)}, bf16[2,2,2,48,1536]{4,3,1,2,0:T(8,128)(2,1)}, u32[]{:S(2)}, u32[]{:S(2)}) collective-permute-start(bf16[2,2,2,48,1536]{4,3,1,2,0:T(8,128)(2,1)} %bitcast.520), channel_id=1, source_target_pairs={{0,4},{4,0},{8,12},{12,8},{1,5},{5,1},{9,13},{13,9},{2,6},{6,2},{1... | collective-permute-start | bytes 3538952 | tf_op jit(solution)/shard_map/ppermute | solution.py:578
  92.8 13.0 %copy-start = (f32[2,512,768]{2,1,0:T(8,128)S(1)}, f32[2,512,768]{2,1,0:T(8,128)}, u32[]{:S(2)}) copy-start(f32[2,512,768]{2,1,0:T(8,128)} %get-tuple-element.41) | copy-start | bytes 9437188
  95.6 140.0 %collective-permute-start.45 = (bf16[1536,768]{1,0:T(8,128)(2,1)}, bf16[1536,768]{1,0:T(8,128)(2,1)}, u32[]{:S(2)}, u32[]{:S(2)}) collective-permute-start(bf16[1536,768]{1,0:T(8,128)(2,1)} %convolution_convert_fusion), channel_id=1, source_target_pairs={{8,0},{12,4},{16,24},{20,28},{9,1},{13,5},{17,25},{21,29},{10,2},{... | collective-permute-start | bytes 7077896 | tf_op jit(solution)/shard_map/ppermute | solution.py:719
  139.7 28.8 %collective-permute-start.22 = (bf16[384,768]{1,0:T(8,128)(2,1)}, bf16[384,768]{1,0:T(8,128)(2,1)}, u32[]{:S(2)}, u32[]{:S(2)}) collective-permute-start(bf16[384,768]{1,0:T(8,128)(2,1)} %convolution_convert_fusion.4), channel_id=1, source_target_pairs={{8,0},{12,4},{16,24},{20,28},{9,1},{13,5},{17,25},{21,29},{10,2},{... | collective-permute-start | bytes 1769480 | tf_op jit(solution)/shard_map/ppermute | solution.py:719
  142.0 10.9 %copy-start.28 = (bf16[2,1024,768]{2,1,0:T(8,128)(2,1)S(1)}, bf16[2,1024,768]{2,1,0:T(8,128)(2,1)}, u32[]{:S(2)}) copy-start(bf16[2,1024,768]{2,1,0:T(8,128)(2,1)} %get-tuple-element.60) | copy-start | bytes 9437188
  162.6 3.1 collective-permute-start.1
  164.1 62.8 %slice-start.4 = ((s8[4718592]{0:T(1024)(128)(4,1)}), s8[4194304]{0:T(1024)(128)(4,1)S(1)}, s32[]{:S(2)}) async-start(s8[4718592]{0:T(1024)(128)(4,1)} %bitcast.551), calls=%async_computation.4 | async-start | bytes 8388608
  164.4 31.4 %collective-permute-start.13 = (bf16[2,2,2,48,1152]{4,3,0,1,2:T(8,128)(2,1)S(1)}, bf16[2,2,2,48,1152]{4,3,0,1,2:T(8,128)(2,1)S(1)}, u32[]{:S(2)}, u32[]{:S(2)}) collective-permute-start(bf16[2,2,2,48,1152]{4,3,0,1,2:T(8,128)(2,1)S(1)} %bitcast.538), channel_id=1, source_target_pairs={{0,1},{1,0},{2,3},{3,2},{4,5},{5,4},{6,7},{7,6},{8,9},{9,8},{10,11... | collective-permute-start | bytes 2654216 | tf_op jit(solution)/shard_map/ppermute | solution.py:578
  165.9 28.4 %collective-permute-start.2 = (bf16[256,768]{1,0:T(8,128)(2,1)S(1)}, bf16[256,768]{1,0:T(8,128)(2,1)S(1)}, u32[]{:S(2)}, u32[]{:S(2)}) collective-permute-start(bf16[256,768]{1,0:T(8,128)(2,1)S(1)} %fusion.106), channel_id=1, source_target_pairs={{0,1},{1,0},{2,3},{3,2},{4,5},{5,4},{6,7},{7,6},{8,9},{9,8},{10,11... | collective-permute-start | bytes 1179656 | tf_op jit(solution)/shard_map/ppermute | solution.py:657
  169.9 25.3 %collective-permute-start.23 = (bf16[2,2,48,768]{3,2,0,1:T(8,128)(2,1)S(1)}, bf16[2,2,48,768]{3,2,0,1:T(8,128)(2,1)S(1)}, u32[]{:S(2)}, u32[]{:S(2)}) collective-permute-start(bf16[2,2,48,768]{3,2,0,1:T(8,128)(2,1)S(1)} %bitcast.542), channel_id=1, source_target_pairs={{0,4},{4,0},{8,12},{12,8},{1,5},{5,1},{9,13},{13,9},{2,6},{6,2},{1... | collective-permute-start | bytes 884744 | tf_op jit(solution)/shard_map/ppermute | solution.py:578
  170.4 27.9 %collective-permute-start.32 = (bf16[2,2,48,1536]{3,2,0,1:T(8,128)(2,1)S(1)}, bf16[2,2,48,1536]{3,2,0,1:T(8,128)(2,1)S(1)}, u32[]{:S(2)}, u32[]{:S(2)}) collective-permute-start(bf16[2,2,48,1536]{3,2,0,1:T(8,128)(2,1)S(1)} %dynamic-slice_bitcast_fusion.6), channel_id=1, source_target_pairs={{0,8},{4,12},{8,0},{12,4},{1,9},{5,13},{9,1},{13,5},{2,10},{6,14},... | collective-permute-start | bytes 1769480 | tf_op jit(solution)/shard_map/ppermute | solution.py:578
  194.3 32.6 %slice-start.5 = ((s8[4718592]{0:T(1024)(128)(4,1)}), s8[524288]{0:T(1024)(128)(4,1)S(1)}, s32[]{:S(2)}) async-start(s8[4718592]{0:T(1024)(128)(4,1)} %bitcast.551), calls=%async_computation.5 | async-start | bytes 1048576
  194.5 29.4 %collective-permute-start.3 = (bf16[512,768]{1,0:T(8,128)(2,1)S(1)}, bf16[512,768]{1,0:T(8,128)(2,1)S(1)}, u32[]{:S(2)}, u32[]{:S(2)}) collective-permute-start(bf16[512,768]{1,0:T(8,128)(2,1)S(1)} %fusion.132), channel_id=1, source_target_pairs={{0,16},{16,0},{1,17},{17,1},{2,18},{18,2},{3,19},{19,3},{4,20},{20... | collective-permute-start | bytes 2359304 | tf_op jit(solution)/shard_map/ppermute | solution.py:60
  195.3 8.2 %collective-permute-start.24 = (bf16[2,48,768]{2,1,0:T(8,128)(2,1)S(1)}, bf16[2,48,768]{2,1,0:T(8,128)(2,1)S(1)}, u32[]{:S(2)}, u32[]{:S(2)}) collective-permute-start(bf16[2,48,768]{2,1,0:T(8,128)(2,1)S(1)} %dynamic-slice_bitcast_fusion.22), channel_id=1, source_target_pairs={{0,1},{1,0},{2,3},{3,2},{4,5},{5,4},{6,7},{7,6},{8,9},{9,8},{10,11... | collective-permute-start | bytes 442376 | tf_op jit(solution)/shard_map/ppermute | solution.py:578
  196.0 22.1 %collective-permute-start.14 = (bf16[2,2,48,1152]{3,2,0,1:T(8,128)(2,1)S(1)}, bf16[2,2,48,1152]{3,2,0,1:T(8,128)(2,1)S(1)}, u32[]{:S(2)}, u32[]{:S(2)}) collective-permute-start(bf16[2,2,48,1152]{3,2,0,1:T(8,128)(2,1)S(1)} %dynamic-slice_bitcast_fusion.8), channel_id=1, source_target_pairs={{0,2},{1,3},{2,0},{3,1},{4,6},{5,7},{6,4},{7,5},{8,10},{9,11},{10,... | collective-permute-start | bytes 1327112 | tf_op jit(solution)/shard_map/ppermute | solution.py:578
  198.5 16.3 %collective-permute-start.33 = (bf16[2,48,1536]{2,1,0:T(8,128)(2,1)S(1)}, bf16[2,48,1536]{2,1,0:T(8,128)(2,1)S(1)}, u32[]{:S(2)}, u32[]{:S(2)}) collective-permute-start(bf16[2,48,1536]{2,1,0:T(8,128)(2,1)S(1)} %dynamic-slice_bitcast_fusion.16), channel_id=1, source_target_pairs={{0,1},{1,0},{2,3},{3,2},{4,5},{5,4},{6,7},{7,6},{8,9},{9,8},{10,11... | collective-permute-start | bytes 884744 | tf_op jit(solution)/shard_map/ppermute | solution.py:578
  204.3 152.0 %collective-permute-start.25 = (bf16[48,768]{1,0:T(8,128)(2,1)}, bf16[48,768]{1,0:T(8,128)(2,1)}, u32[]{:S(2)}, u32[]{:S(2)}) collective-permute-start(bf16[48,768]{1,0:T(8,128)(2,1)} %dynamic-slice_bitcast_fusion.26), channel_id=1, source_target_pairs={{0,2},{1,3},{2,0},{3,1},{4,6},{5,7},{6,4},{7,5},{8,10},{9,11},{10,... | collective-permute-start | bytes 221192 | tf_op jit(solution)/shard_map/ppermute | solution.py:578
  214.9 9.0 %copy-start.41 = (bf16[2,48,1536]{2,1,0:T(8,128)(2,1)}, bf16[2,48,1536]{2,1,0:T(8,128)(2,1)S(1)}, u32[]{:S(2)}) copy-start(bf16[2,48,1536]{2,1,0:T(8,128)(2,1)S(1)} %fusion.118) | copy-start | bytes 884740
  218.3 4.8 collective-permute-start.15
  219.4 170.9 %collective-permute-start.34 = (bf16[48,1536]{1,0:T(8,128)(2,1)}, bf16[48,1536]{1,0:T(8,128)(2,1)}, u32[]{:S(2)}, u32[]{:S(2)}) collective-permute-start(bf16[48,1536]{1,0:T(8,128)(2,1)} %dynamic-slice_bitcast_fusion.20), channel_id=1, source_target_pairs={{0,2},{1,3},{2,0},{3,1},{4,6},{5,7},{6,4},{7,5},{8,10},{9,11},{10,... | collective-permute-start | bytes 442376 | tf_op jit(solution)/shard_map/ppermute | solution.py:578
  240.8 61.3 %collective-permute-start.46 = (bf16[2,2,192,768]{3,2,0,1:T(8,128)(2,1)}, bf16[2,2,192,768]{3,2,0,1:T(8,128)(2,1)}, u32[]{:S(2)}, u32[]{:S(2)}) collective-permute-start(bf16[2,2,192,768]{3,2,0,1:T(8,128)(2,1)} %bitcast.518), channel_id=1, source_target_pairs={{0,4},{4,0},{8,12},{12,8},{1,5},{5,1},{9,13},{13,9},{2,6},{6,2},{1... | collective-permute-start | bytes 3538952 | tf_op jit(solution)/shard_map/ppermute | solution.py:578
  242.9 16.8 %collective-permute-start.4 = (bf16[512,768]{1,0:T(8,128)(2,1)}, bf16[512,768]{1,0:T(8,128)(2,1)}, u32[]{:S(2)}, u32[]{:S(2)}) collective-permute-start(bf16[512,768]{1,0:T(8,128)(2,1)} %get-tuple-element.146), channel_id=1, source_target_pairs={{0,16},{16,0},{1,17},{17,1},{2,18},{18,2},{3,19},{19,3},{4,20},{20... | collective-permute-start | bytes 2359304 | tf_op jit(solution)/shard_map/ppermute | solution.py:60
  251.6 47.7 %collective-permute-start.27 = (bf16[2,2,2,48,1536]{4,3,1,2,0:T(8,128)(2,1)}, bf16[2,2,2,48,1536]{4,3,1,2,0:T(8,128)(2,1)}, u32[]{:S(2)}, u32[]{:S(2)}) collective-permute-start(bf16[2,2,2,48,1536]{4,3,1,2,0:T(8,128)(2,1)} %bitcast.521), channel_id=1, source_target_pairs={{0,4},{4,0},{8,12},{12,8},{1,5},{5,1},{9,13},{13,9},{2,6},{6,2},{1... | collective-permute-start | bytes 3538952 | tf_op jit(solution)/shard_map/ppermute | solution.py:578
  266.8 11.4 %copy-start.29 = (bf16[2,1024,768]{2,1,0:T(8,128)(2,1)S(1)}, bf16[2,1024,768]{2,1,0:T(8,128)(2,1)}, u32[]{:S(2)}) copy-start(bf16[2,1024,768]{2,1,0:T(8,128)(2,1)} %get-tuple-element.60) | copy-start | bytes 9437188
  280.7 25.2 %collective-permute-start.18 = (bf16[384,768]{1,0:T(8,128)(2,1)}, bf16[384,768]{1,0:T(8,128)(2,1)}, u32[]{:S(2)}, u32[]{:S(2)}) collective-permute-start(bf16[384,768]{1,0:T(8,128)(2,1)} %convolution_convert_fusion.5), channel_id=1, source_target_pairs={{8,0},{12,4},{16,24},{20,28},{9,1},{13,5},{17,25},{21,29},{10,2},{... | collective-permute-start | bytes 1769480 | tf_op jit(solution)/shard_map/ppermute | solution.py:719
  299.3 29.2 %collective-permute-start.9 = (bf16[2,2,2,48,1152]{4,3,0,1,2:T(8,128)(2,1)S(1)}, bf16[2,2,2,48,1152]{4,3,0,1,2:T(8,128)(2,1)S(1)}, u32[]{:S(2)}, u32[]{:S(2)}) collective-permute-start(bf16[2,2,2,48,1152]{4,3,0,1,2:T(8,128)(2,1)S(1)} %bitcast.537), channel_id=1, source_target_pairs={{0,1},{1,0},{2,3},{3,2},{4,5},{5,4},{6,7},{7,6},{8,9},{9,8},{10,11... | collective-permute-start | bytes 2654216 | tf_op jit(solution)/shard_map/ppermute | solution.py:578
  302.1 1.8 collective-permute-start.5
  303.9 144.0 %collective-permute-start.16 = (bf16[48,1152]{1,0:T(8,128)(2,1)}, bf16[48,1152]{1,0:T(8,128)(2,1)}, u32[]{:S(2)}, u32[]{:S(2)}) collective-permute-start(bf16[48,1152]{1,0:T(8,128)(2,1)} %dynamic-slice_bitcast_fusion.24), channel_id=1, source_target_pairs={{0,8},{4,12},{8,0},{12,4},{1,9},{5,13},{9,1},{13,5},{2,10},{6,14},... | collective-permute-start | bytes 331784 | tf_op jit(solution)/shard_map/ppermute | solution.py:578
  305.9 22.4 %collective-permute-start.6 = (bf16[256,768]{1,0:T(8,128)(2,1)S(1)}, bf16[256,768]{1,0:T(8,128)(2,1)S(1)}, u32[]{:S(2)}, u32[]{:S(2)}) collective-permute-start(bf16[256,768]{1,0:T(8,128)(2,1)S(1)} %fusion.105), channel_id=1, source_target_pairs={{0,1},{1,0},{2,3},{3,2},{4,5},{5,4},{6,7},{7,6},{8,9},{9,8},{10,11... | collective-permute-start | bytes 1179656 | tf_op jit(solution)/shard_map/ppermute | solution.py:657
  328.3 15.0 %collective-permute-start.28 = (bf16[2,2,48,1536]{3,2,0,1:T(8,128)(2,1)S(1)}, bf16[2,2,48,1536]{3,2,0,1:T(8,128)(2,1)S(1)}, u32[]{:S(2)}, u32[]{:S(2)}) collective-permute-start(bf16[2,2,48,1536]{3,2,0,1:T(8,128)(2,1)S(1)} %dynamic-slice_bitcast_fusion.7), channel_id=1, source_target_pairs={{0,8},{4,12},{8,0},{12,4},{1,9},{5,13},{9,1},{13,5},{2,10},{6,14},... | collective-permute-start | bytes 1769480 | tf_op jit(solution)/shard_map/ppermute | solution.py:578
  328.5 8.2 %collective-permute-start.19 = (bf16[2,2,48,768]{3,2,0,1:T(8,128)(2,1)S(1)}, bf16[2,2,48,768]{3,2,0,1:T(8,128)(2,1)S(1)}, u32[]{:S(2)}, u32[]{:S(2)}) collective-permute-start(bf16[2,2,48,768]{3,2,0,1:T(8,128)(2,1)S(1)} %bitcast.541), channel_id=1, source_target_pairs={{0,4},{4,0},{8,12},{12,8},{1,5},{5,1},{9,13},{13,9},{2,6},{6,2},{1... | collective-permute-start | bytes 884744 | tf_op jit(solution)/shard_map/ppermute | solution.py:578
  336.8 13.6 %collective-permute-start.47 = (bf16[2,192,768]{2,1,0:T(8,128)(2,1)S(1)}, bf16[2,192,768]{2,1,0:T(8,128)(2,1)S(1)}, u32[]{:S(2)}, u32[]{:S(2)}) collective-permute-start(bf16[2,192,768]{2,1,0:T(8,128)(2,1)S(1)} %dynamic-slice_bitcast_fusion.4), channel_id=1, source_target_pairs={{0,1},{1,0},{2,3},{3,2},{4,5},{5,4},{6,7},{7,6},{8,9},{9,8},{10,11... | collective-permute-start | bytes 1769480 | tf_op jit(solution)/shard_map/ppermute | solution.py:578
  343.3 89.0 %collective-permute-start.41 = (bf16[1536,768]{1,0:T(8,128)(2,1)}, bf16[1536,768]{1,0:T(8,128)(2,1)}, u32[]{:S(2)}, u32[]{:S(2)}) collective-permute-start(bf16[1536,768]{1,0:T(8,128)(2,1)} %convolution_convert_fusion.1), channel_id=1, source_target_pairs={{8,0},{12,4},{16,24},{20,28},{9,1},{13,5},{17,25},{21,29},{10,2},{... | collective-permute-start | bytes 7077896 | tf_op jit(solution)/shard_map/ppermute | solution.py:719
  350.4 4.4 collective-permute-start.20
  350.9 18.0 %copy-start.22 = (bf16[2,192,768]{2,1,0:T(8,128)(2,1)}, bf16[2,192,768]{2,1,0:T(8,128)(2,1)S(1)}, u32[]{:S(2)}) copy-start(bf16[2,192,768]{2,1,0:T(8,128)(2,1)S(1)} %fusion.83) | copy-start | bytes 1769476
  354.9 5.1 collective-permute-start.21
  356.3 11.4 %collective-permute-start.29 = (bf16[2,48,1536]{2,1,0:T(8,128)(2,1)S(1)}, bf16[2,48,1536]{2,1,0:T(8,128)(2,1)S(1)}, u32[]{:S(2)}, u32[]{:S(2)}) collective-permute-start(bf16[2,48,1536]{2,1,0:T(8,128)(2,1)S(1)} %dynamic-slice_bitcast_fusion.17), channel_id=1, source_target_pairs={{0,1},{1,0},{2,3},{3,2},{4,5},{5,4},{6,7},{7,6},{8,9},{9,8},{10,11... | collective-permute-start | bytes 884744 | tf_op jit(solution)/shard_map/ppermute | solution.py:578
  360.9 4.9 collective-permute-start.26
  365.7 51.9 %collective-permute-start.7 = (bf16[512,768]{1,0:T(8,128)(2,1)S(1)}, bf16[512,768]{1,0:T(8,128)(2,1)S(1)}, u32[]{:S(2)}, u32[]{:S(2)}) collective-permute-start(bf16[512,768]{1,0:T(8,128)(2,1)S(1)} %fusion.131), channel_id=1, source_target_pairs={{0,16},{16,0},{1,17},{17,1},{2,18},{18,2},{3,19},{19,3},{4,20},{20... | collective-permute-start | bytes 2359304 | tf_op jit(solution)/shard_map/ppermute | solution.py:60
  367.7 38.7 %copy-start.42 = (bf16[2,48,1536]{2,1,0:T(8,128)(2,1)S(1)}, bf16[2,48,1536]{2,1,0:T(8,128)(2,1)}, u32[]{:S(2)}) copy-start(bf16[2,48,1536]{2,1,0:T(8,128)(2,1)} %copy-done.41) | copy-start | bytes 884740
  367.7 22.4 %collective-permute-start.10 = (bf16[2,2,48,1152]{3,2,0,1:T(8,128)(2,1)S(1)}, bf16[2,2,48,1152]{3,2,0,1:T(8,128)(2,1)S(1)}, u32[]{:S(2)}, u32[]{:S(2)}) collective-permute-start(bf16[2,2,48,1152]{3,2,0,1:T(8,128)(2,1)S(1)} %dynamic-slice_bitcast_fusion.9), channel_id=1, source_target_pairs={{0,2},{1,3},{2,0},{3,1},{4,6},{5,7},{6,4},{7,5},{8,10},{9,11},{10,... | collective-permute-start | bytes 1327112 | tf_op jit(solution)/shard_map/ppermute | solution.py:578
  390.0 15.9 %collective-permute-start.30 = (bf16[48,1536]{1,0:T(8,128)(2,1)S(1)}, bf16[48,1536]{1,0:T(8,128)(2,1)S(1)}, u32[]{:S(2)}, u32[]{:S(2)}) collective-permute-start(bf16[48,1536]{1,0:T(8,128)(2,1)S(1)} %dynamic-slice_bitcast_fusion.21), channel_id=1, source_target_pairs={{0,2},{1,3},{2,0},{3,1},{4,6},{5,7},{6,4},{7,5},{8,10},{9,11},{10,... | collective-permute-start | bytes 442376 | tf_op jit(solution)/shard_map/ppermute | solution.py:578
  390.2 27.4 %copy-start.5 = (bf16[2,512,768]{2,1,0:T(8,128)(2,1)S(1)}, bf16[2,512,768]{2,1,0:T(8,128)(2,1)}, u32[]{:S(2)}) copy-start(bf16[2,512,768]{2,1,0:T(8,128)(2,1)} %get-tuple-element.37) | copy-start | bytes 4718596
  390.2 27.4 %copy-start.53 = (f32[768]{0:T(1024)S(1)}, f32[768]{0:T(1024)}, u32[]{:S(2)}) copy-start(f32[768]{0:T(1024)} %get-tuple-element.85) | copy-start | bytes 9220
  390.2 27.4 %copy-start.58 = (f32[512]{0:T(512)S(1)}, f32[512]{0:T(512)}, u32[]{:S(2)}) copy-start(f32[512]{0:T(512)} %broadcast_multiply_fusion.19) | copy-start | bytes 6148
  390.2 27.4 %copy-start.66 = (f32[512]{0:T(512)S(1)}, f32[512]{0:T(512)}, u32[]{:S(2)}) copy-start(f32[512]{0:T(512)} %add_rsqrt_fusion.3) | copy-start | bytes 6148
  390.3 99.0 %collective-permute-start.48 = (bf16[192,768]{1,0:T(8,128)(2,1)}, bf16[192,768]{1,0:T(8,128)(2,1)}, u32[]{:S(2)}, u32[]{:S(2)}) collective-permute-start(bf16[192,768]{1,0:T(8,128)(2,1)} %dynamic-slice_bitcast_fusion.14), channel_id=1, source_target_pairs={{0,2},{1,3},{2,0},{3,1},{4,6},{5,7},{6,4},{7,5},{8,10},{9,11},{10,... | collective-permute-start | bytes 884744 | tf_op jit(solution)/shard_map/ppermute | solution.py:578
  406.0 6.5 %collective-permute-start.11 = (bf16[2,48,1152]{2,1,0:T(8,128)(2,1)S(1)}, bf16[2,48,1152]{2,1,0:T(8,128)(2,1)S(1)}, u32[]{:S(2)}, u32[]{:S(2)}) collective-permute-start(bf16[2,48,1152]{2,1,0:T(8,128)(2,1)S(1)} %dynamic-slice_bitcast_fusion.19), channel_id=1, source_target_pairs={{0,4},{4,0},{8,12},{12,8},{1,5},{5,1},{9,13},{13,9},{2,6},{6,2},{1... | collective-permute-start | bytes 663560 | tf_op jit(solution)/shard_map/ppermute | solution.py:578
  412.5 2.3 collective-permute-start.35
  414.8 33.0 %collective-permute-start.12 = (bf16[48,1152]{1,0:T(8,128)(2,1)}, bf16[48,1152]{1,0:T(8,128)(2,1)S(1)}, u32[]{:S(2)}, u32[]{:S(2)}) collective-permute-start(bf16[48,1152]{1,0:T(8,128)(2,1)} %dynamic-slice_bitcast_fusion.25), channel_id=1, source_target_pairs={{0,8},{4,12},{8,0},{12,4},{1,9},{5,13},{9,1},{13,5},{2,10},{6,14},... | collective-permute-start | bytes 331784 | tf_op jit(solution)/shard_map/ppermute | solution.py:578
  422.4 5.6 %collective-permute-start.36 = (f32[16,384]{1,0:T(8,128)S(1)}, f32[16,384]{1,0:T(8,128)S(1)}, u32[]{:S(2)}, u32[]{:S(2)}) collective-permute-start(f32[16,384]{1,0:T(8,128)S(1)} %broadcast_select_fusion.8), channel_id=1, source_target_pairs={{0,16},{16,0},{1,17},{17,1},{2,18},{18,2},{3,19},{19,3},{4,20},{20... | collective-permute-start | bytes 73736 | tf_op jit(solution)/shard_map/ppermute | solution.py:60
  428.1 3.0 collective-permute-start.37
  431.1 73.3 %collective-permute-start.8 = (bf16[256,768]{1,0:T(8,128)(2,1)S(1)}, bf16[256,768]{1,0:T(8,128)(2,1)S(1)}, u32[]{:S(2)}, u32[]{:S(2)}) collective-permute-start(bf16[256,768]{1,0:T(8,128)(2,1)S(1)} %select_convert_fusion.1), channel_id=1, source_target_pairs={{0,3},{1,2},{2,1},{3,0},{4,7},{5,6},{6,5},{7,4},{8,11},{9,10},{10,... | collective-permute-start | bytes 1179656 | tf_op jit(solution)/shard_map/ppermute | solution.py:776
  432.3 3.1 collective-permute-start.38
  435.5 5.0 collective-permute-start.39
  440.5 7.1 %collective-permute-start.40 = (f32[1,384]{1,0:T(1,128)S(1)}, f32[1,384]{1,0:T(1,128)S(1)}, u32[]{:S(2)}, u32[]{:S(2)}) collective-permute-start(f32[1,384]{1,0:T(1,128)S(1)} %fusion.173), channel_id=1, source_target_pairs={{0,2},{1,3},{2,0},{3,1},{4,6},{5,7},{6,4},{7,5},{8,10},{9,11},{10,... | collective-permute-start | bytes 4616 | tf_op jit(solution)/shard_map/ppermute | solution.py:578
  447.7 25.9 %collective-permute-start.42 = (bf16[2,2,192,768]{3,2,0,1:T(8,128)(2,1)S(1)}, bf16[2,2,192,768]{3,2,0,1:T(8,128)(2,1)S(1)}, u32[]{:S(2)}, u32[]{:S(2)}) collective-permute-start(bf16[2,2,192,768]{3,2,0,1:T(8,128)(2,1)S(1)} %bitcast.536), channel_id=1, source_target_pairs={{0,4},{4,0},{8,12},{12,8},{1,5},{5,1},{9,13},{13,9},{2,6},{6,2},{1... | collective-permute-start | bytes 3538952 | tf_op jit(solution)/shard_map/ppermute | solution.py:578
  448.9 3.0 collective-permute-start.17
  473.9 12.4 %collective-permute-start.43 = (bf16[2,192,768]{2,1,0:T(8,128)(2,1)S(1)}, bf16[2,192,768]{2,1,0:T(8,128)(2,1)S(1)}, u32[]{:S(2)}, u32[]{:S(2)}) collective-permute-start(bf16[2,192,768]{2,1,0:T(8,128)(2,1)S(1)} %dynamic-slice_bitcast_fusion.5), channel_id=1, source_target_pairs={{0,1},{1,0},{2,3},{3,2},{4,5},{5,4},{6,7},{7,6},{8,9},{9,8},{10,11... | collective-permute-start | bytes 1769480 | tf_op jit(solution)/shard_map/ppermute | solution.py:578
  474.1 14.6 %collective-permute-start.50 = (bf16[48,384]{1,0:T(8,128)(2,1)S(1)}, bf16[48,384]{1,0:T(8,128)(2,1)S(1)}, u32[]{:S(2)}, u32[]{:S(2)}) collective-permute-start(bf16[48,384]{1,0:T(8,128)(2,1)S(1)} %slice.256), channel_id=1, source_target_pairs={{0,16},{16,0},{1,17},{17,1},{2,18},{18,2},{3,19},{19,3},{4,20},{20... | collective-permute-start | bytes 110600 | tf_op jit(solution)/shard_map/ppermute | solution.py:60
  476.6 25.8 %copy-start.23 = (bf16[2,192,768]{2,1,0:T(8,128)(2,1)S(1)}, bf16[2,192,768]{2,1,0:T(8,128)(2,1)}, u32[]{:S(2)}) copy-start(bf16[2,192,768]{2,1,0:T(8,128)(2,1)} %copy-done.22) | copy-start | bytes 1769476
  486.6 15.8 %collective-permute-start.44 = (bf16[192,768]{1,0:T(8,128)(2,1)S(1)}, bf16[192,768]{1,0:T(8,128)(2,1)S(1)}, u32[]{:S(2)}, u32[]{:S(2)}) collective-permute-start(bf16[192,768]{1,0:T(8,128)(2,1)S(1)} %dynamic-slice_bitcast_fusion.15), channel_id=1, source_target_pairs={{0,2},{1,3},{2,0},{3,1},{4,6},{5,7},{6,4},{7,5},{8,10},{9,11},{10,... | collective-permute-start | bytes 884744 | tf_op jit(solution)/shard_map/ppermute | solution.py:578
  503.5 2.2 collective-permute-start.49
  (70 other events, 242.2 us)

commit v3 on v2

v3 whole, which is shorter than its diff:
```python
import functools

import jax
import jax.numpy as jnp
from jax import lax
from jax.experimental import pallas as pl
from jax.experimental.pallas import tpu as pltpu
from jax.sharding import PartitionSpec as P

HEAD = 64
SECTION, DP, CTX = "section", "dp", "ctx"
EPSILON = 1e-05
MASKED = -1000000000.0
F32 = jnp.float32
BF16 = jnp.bfloat16
VMEM_LIMIT = 63 * 2**20


def mm(left, right):
    return jnp.dot(left, right, preferred_element_type=F32)


def mm_nt(left, right):
    return lax.dot_general(left, right, (((1,), (1,)), ((), ())), preferred_element_type=F32)


def mm_tn(left, right):
    return lax.dot_general(left, right, (((0,), (0,)), ((), ())), preferred_element_type=F32)


def unit_norm(values):
    mean = jnp.mean(values, axis=-1, keepdims=True)
    centred = values - mean
    rstd = lax.rsqrt(jnp.mean(centred * centred, axis=-1, keepdims=True) + EPSILON)
    return centred * rstd, rstd


def layer_norm(values, gain, bias):
    return unit_norm(values)[0] * gain + bias


def gelu_both(u):
    t = jnp.tanh(0.7978845608028654 * (u + 0.044715 * u * u * u))
    half = 0.5 * (1.0 + t)
    return u * half, half + 0.5 * u * (1.0 - t * t) * (0.7978845608028654 + 3 * 0.044715 * 0.7978845608028654 * u * u)


def swap(x):
    return lax.ppermute(x, SECTION, [(0, 1), (1, 0)])


MESH = pl.DeviceIdType.MESH
HBM = pl.BlockSpec(memory_space=pl.ANY)
VM = pl.BlockSpec(memory_space=pltpu.VMEM)


class Sems:
    def __init__(self, ref):
        self.ref, self.used = ref, 0

    def one(self):
        self.used += 1
        return self.ref.at[self.used - 1]


def push(src, dst, send, recv, to):
    return pltpu.make_async_remote_copy(src_ref=src, dst_ref=dst, send_sem=send, recv_sem=recv, device_id=to,
                                        device_id_type=MESH)


def greet(peers):
    barrier = pltpu.get_barrier_semaphore()
    for peer in peers:
        pl.semaphore_signal(barrier, inc=1, device_id=peer, device_id_type=MESH)
    pl.semaphore_wait(barrier, len(peers))


def attention_block(l, blk, T, keys, pairs, q, k, v, o, lse, bias):
    rows = slice(blk * T, (blk + 1) * T)
    lane = lax.broadcasted_iota(jnp.int32, (T, 128), 1)

    def body(i, carry):
        cols = pl.ds(pl.multiple_of(i * 128, 128), 128)
        q2 = q[l, rows, cols] * jnp.asarray(HEAD**-0.5, BF16)
        k2 = k[l, :keys, cols]
        v2 = jnp.concatenate([v[l, :keys, cols], jnp.ones((keys, 128), BF16)], axis=1)
        outs, lses = [], []
        for h in range(2):
            qh = jnp.where((lane >= 64) == (h == 1), q2, jnp.zeros_like(q2))
            s = mm_nt(qh, k2) + bias[rows, :keys]
            top = jnp.max(s, axis=-1, keepdims=True)
            e = jnp.exp(s - top).astype(BF16)
            both = mm(e, v2)
            total = both[:, 128:]
            outs.append(both[:, :128] / total)
            lses.append(top + jnp.log(total))
        o[l, rows, cols] = jnp.where(lane < 64, outs[0], outs[1]).astype(BF16)
        lse[l, i, rows, :] = jnp.where(lane < 64, lses[0], lses[1])
        return carry

    lax.fori_loop(0, pairs, body, 0)


def column(row_values):
    T = row_values.shape[1]
    at = lax.broadcasted_iota(jnp.int32, (T, T), 0) == lax.broadcasted_iota(jnp.int32, (T, T), 1)
    spread = jnp.where(at, jnp.broadcast_to(row_values, (T, T)), 0).astype(F32)
    return jnp.sum(spread, axis=1, keepdims=True).astype(jnp.int32)


def forward_kernel(C, T, D, F, ends, segs, g1, b1, g2, b2, qkv, wo, fc, fcb, proj, shared,
                   xall_o, q_o, k_o, v_o, o_o, lse_o, r_o, hr_o, hh_o, gp_o, act_o, y_o, yb_o, gy_o, sm_o, watt_o, wfc_o, wproj_o,
                   kseg_o,
                   e, seg, sm, wqk, wv, wout, wfc, wproj, xall, q, k, v, o, lse, r, hr, hh, gp, act, y, yb, wvt, bias,
                   br_s, br_r, ml_s, ml_r, dma):
    core, dp, z = lax.axis_index(SECTION), lax.axis_index(DP), lax.axis_index(CTX)
    N, L, H, FH = C // 2, C * T, D // 2, F // 2
    T2 = T // 2
    row = z // N
    lo = z + row * (C - 1 - 2 * z)
    hi = C - 1 - lo
    base = row * N
    pairs = H // 128
    sems = Sems(dma)
    sib = (1 - core, dp, z)
    mirror = (core, dp, C - 1 - z)
    ahead = [(core, dp, base + lax.rem(z - base + n, N)) for n in range(1, N)]
    behind = [base + lax.rem(z - base + N - n, N) for n in range(1, N)]
    line = [(core, dp, lax.rem(z + n, C)) for n in range(1, C)]
    pos = lambda blk: lo + blk * (hi - lo)
    rows_at = lambda p: pl.ds(pl.multiple_of(p * T, T), T)
    saves = []

    def save(src, dst):
        cp = pltpu.make_async_copy(src, dst, sems.one())
        cp.start()
        saves.append(cp)

    e_load = pltpu.make_async_copy(ends.at[0, row], e.at[core, row], sems.one())
    e_load.start()
    qc = pl.ds(pl.multiple_of(core * H, 128), H)
    kc = pl.ds(pl.multiple_of(D + core * H, 128), H)
    qo = pl.ds(pl.multiple_of((1 - core) * H, 128), H)
    ko = pl.ds(pl.multiple_of(D + (1 - core) * H, 128), H)
    loads = [
        pltpu.make_async_copy(qkv.at[0, :, qc], wqk.at[core, :, pl.ds(0, H)], sems.one()),
        pltpu.make_async_copy(qkv.at[0, :, kc], wqk.at[core, :, pl.ds(H, H)], sems.one()),
        pltpu.make_async_copy(wo.at[0, pl.ds(pl.multiple_of(core * H, H), H), :], wout.at[core], sems.one()),
        pltpu.make_async_copy(fc.at[0, :, pl.ds(pl.multiple_of(core * FH, 128), FH)], wfc.at[core], sems.one()),
        pltpu.make_async_copy(proj.at[0, pl.ds(pl.multiple_of(core * FH, FH), FH), :], wproj.at[core], sems.one()),
    ]
    for cp in loads:
        cp.start()
    v_sem = sems.one()
    v_shared = pltpu.make_async_copy(shared, wv.at[0], v_sem)
    v_fresh = pltpu.make_async_copy(qkv.at[0, :, pl.ds(2 * D, H)], wv.at[1], v_sem)

    @pl.when(core == 0)
    def _():
        v_shared.start()

    @pl.when(core == 1)
    def _():
        v_fresh.start()

    seg_load = pltpu.make_async_copy(segs.at[row], seg.at[z], sems.one())
    seg_load.start()
    sm[core] = jnp.zeros_like(sm[core])
    sm[core, 0:1, :D] = g1[...]
    sm[core, 1:2, :D] = b1[...]
    sm[core, 2:3, :D] = g2[...]
    sm[core, 3:4, :D] = b2[...]
    sm[core, 4:5, :] = fcb[...]

    greet([sib] + line)

    own_s, own_r = sems.one(), sems.one()
    own_push = push(ends.at[0, row], e.at[core, row], own_s, own_r, sib)
    own_come = push(ends.at[0, row], e.at[1 - core, row], own_s, own_r, sib)
    far_s, far_r = sems.one(), sems.one()
    far_push = push(ends.at[0, 1 - row], e.at[core, row], far_s, far_r, mirror)
    far_come = push(ends.at[0, 1 - row], e.at[core, 1 - row], far_s, far_r, mirror)
    fwd_s, fwd_r = sems.one(), sems.one()
    fwd_push = push(e.at[core, 1 - row], e.at[core, 1 - row], fwd_s, fwd_r, sib)
    fwd_come = push(e.at[1 - core, 1 - row], e.at[1 - core, 1 - row], fwd_s, fwd_r, sib)

    @pl.when(core == 0)
    def _():
        far_push.start()

    own_push.start()
    sm_push = push(sm.at[core], sm.at[core], sems.one(), sems.one(), sib)
    sm_push.start()
    seg_push = []
    for n in range(1, C):
        to = lax.rem(z + n, C)
        cp = push(segs.at[to // N], seg.at[z], sems.one(), sems.one(), line[n - 1])
        cp.start()
        seg_push.append(cp)
    qk_push = [
        push(qkv.at[0, :, qo], wqk.at[core, :, pl.ds(0, H)], sems.one(), sems.one(), sib),
        push(qkv.at[0, :, ko], wqk.at[core, :, pl.ds(H, H)], sems.one(), sems.one(), sib),
    ]
    for cp in qk_push:
        cp.start()
    v_push = push(qkv.at[0, :, pl.ds(2 * D, H)], wv.at[0], sems.one(), sems.one(), sib)

    @pl.when(core == 0)
    def _():
        v_push.start()

    rest_push = [
        push(wo.at[0, pl.ds(pl.multiple_of((1 - core) * H, H), H), :], wout.at[core], sems.one(), sems.one(), sib),
        push(fc.at[0, :, pl.ds(pl.multiple_of((1 - core) * FH, 128), FH)], wfc.at[core], sems.one(), sems.one(), sib),
        push(proj.at[0, pl.ds(pl.multiple_of((1 - core) * FH, FH), FH), :], wproj.at[core], sems.one(), sems.one(), sib),
    ]

    seg_load.wait()
    for n, cp in enumerate(seg_push):
        cp.wait()
    kseg = jnp.concatenate([seg[n] for n in range(C)], axis=1)
    kseg_o[...] = kseg
    for blk in range(2):
        rows = slice(blk * T, (blk + 1) * T)
        qpos = pos(blk) * T + lax.broadcasted_iota(jnp.int32, (T, L), 0)
        kpos = lax.broadcasted_iota(jnp.int32, (T, L), 1)
        allowed = (kpos <= qpos) & (kseg == column(seg[pos(blk)]))
        bias[rows, :] = jnp.where(allowed, 0.0, MASKED)

    xh_sends = {}

    def normed_block(l, turn, blk, values):
        p = pos(blk)
        xall[l, rows_at(p), :] = layer_norm(values, sm[l, 0:1, :D], sm[l, 1:2, :D]).astype(BF16)
        for n in range(N - 1):
            part = xall.at[l, pl.ds(pl.multiple_of(p * T + core * T2, T2), T2), :]
            s, rsem = sems.one(), sems.one()
            cp = push(part, part, s, rsem, ahead[n])
            cp.start()
            src = behind[n]
            slo = src + row * (C - 1 - 2 * src)
            sp = slo + blk * (C - 1 - 2 * slo)
            got = xall.at[l, pl.ds(pl.multiple_of(sp * T + core * T2, T2), T2), :]
            other = xall.at[l, pl.ds(pl.multiple_of(sp * T + (1 - core) * T2, T2), T2), :]
            come = push(got, got, s, rsem, ahead[n])
            fs, fr = sems.one(), sems.one()
            onward = push(got, got, fs, fr, sib)
            arrive = push(other, other, fs, fr, sib)
            xh_sends[(l, turn, n)] = (cp, come, onward, arrive, sp)

    def own_products(l, blk):
        p = pos(blk)
        xh = xall[l, rows_at(p), :]
        both = mm(xh, wqk[l])
        q[l, blk * T : (blk + 1) * T, :] = both[:, :H].astype(BF16)
        k[l, rows_at(p), :] = both[:, H:].astype(BF16)

    def value_products(l, p):
        src = l * core
        v[l, rows_at(p), :] = mm(xall[src, rows_at(p), :], wv[src]).astype(BF16)

    def key_products(l, p):
        k[l, rows_at(p), :] = mm(xall[l, rows_at(p), :], wqk[l, :, H:]).astype(BF16)

    @pl.when(core == 0)
    def _():
        e_load.wait()

    @pl.when(core == 1)
    def _():
        own_come.wait_recv()

    sm_push.wait()
    blk = row
    r[0, pl.ds(pl.multiple_of(blk * T, T), T), :] = e[0, blk]
    normed_block(0, 0, blk, e[0, blk].astype(F32))

    @pl.when(core == 0)
    def _():
        loads[0].wait()
        loads[1].wait()
        v_shared.wait()

    @pl.when(core == 1)
    def _():
        for cp in qk_push:
            cp.wait_recv()
        v_push.wait_recv()

    def own_products_dynamic(l, blk):
        p = pos(blk)
        both = mm(xall[l, rows_at(p), :], wqk[l])
        q[l, pl.ds(pl.multiple_of(blk * T, T), T), :] = both[:, :H].astype(BF16)
        k[l, rows_at(p), :] = both[:, H:].astype(BF16)
        value_products(l, p)

    own_products_dynamic(0, blk)
    blk = 1 - row

    @pl.when(core == 0)
    def _():
        far_come.wait_recv()
        fwd_push.start()

    @pl.when(core == 1)
    def _():
        fwd_come.wait_recv()

    r[0, pl.ds(pl.multiple_of(blk * T, T), T), :] = e[0, blk]
    normed_block(0, 1, blk, e[0, blk].astype(F32))
    own_products_dynamic(0, blk)

    def finish_layer_inputs(l):
        for turn in range(2):
            for n in range(N - 1):
                cp, come, onward, arrive, sp = xh_sends[(l, turn, n)]
                come.wait_recv()
                onward.start()
        for turn in range(2):
            for n in range(N - 1):
                cp, come, onward, arrive, sp = xh_sends[(l, turn, n)]
                arrive.wait_recv()
                key_products(l, sp)
                value_products(l, sp)

    def middle(l):
        sends = []
        for blk in range(2):
            rows = slice(blk * T, (blk + 1) * T)
            attention_block(l, blk, T, L // 2 if blk == 0 else L, pairs, q, k, v, o, lse, bias)
            if l == 0 and blk == 0:
                @pl.when(core == 0)
                def _():
                    loads[2].wait()

                @pl.when(core == 1)
                def _():
                    rest_push[0].wait_recv()
            if l == 1 and blk == 0:
                @pl.when(core == 1)
                def _():
                    loads[2].wait()

                @pl.when(core == 0)
                def _():
                    rest_push[0].wait_recv()
            part = mm(o[l, rows, :], wout[l])
            hr[l, rows, :] = part
            br_s[l, rows, :] = part.astype(BF16)
            cp = push(br_s.at[l, rows, :], br_r.at[l, rows, :], sems.one(), sems.one(), sib)
            cp.start()
            sends.append(cp)
        save(q.at[l], q_o.at[l])
        save(k.at[l], k_o.at[l])
        save(v.at[l], v_o.at[l])
        save(o.at[l], o_o.at[l])
        save(lse.at[l], lse_o.at[l])
        save(xall.at[l], xall_o.at[l])
        mlps = []
        for blk in range(2):
            rows = slice(blk * T, (blk + 1) * T)
            sends[blk].wait_recv()
            hidden = r[l, rows, :].astype(F32) + hr[l, rows, :] + br_r[l, rows, :].astype(F32)
            hr[l, rows, :] = hidden
            normed2 = layer_norm(hidden, sm[l, 2:3, :D], sm[l, 3:4, :D]).astype(BF16)
            hh[l, rows, :] = normed2
            if blk == 0:
                local = core == l

                @pl.when(local)
                def _():
                    loads[3].wait()
                    loads[4].wait()

                @pl.when(jnp.logical_not(local))
                def _():
                    rest_push[1].wait_recv()
                    rest_push[2].wait_recv()
            mine = pl.ds(pl.multiple_of(core * FH, 128), FH)
            u = mm(normed2, wfc[l]) + sm[l, 4:5, mine]
            a, slope = gelu_both(u)
            a = a.astype(BF16)
            gp[l, rows, :] = slope.astype(BF16)
            act[l, rows, :] = a
            part = mm(a, wproj[l])
            y[rows, :] = part
            ml_s[l, rows, :] = part.astype(BF16)
            cp = push(ml_s.at[l, rows, :], ml_r.at[l, rows, :], sems.one(), sems.one(), sib)
            cp.start()
            mlps.append(cp)
        save(hr.at[l], hr_o.at[l])
        save(hh.at[l], hh_o.at[l])
        save(gp.at[l], gp_o.at[l])
        save(act.at[l], act_o.at[l])
        for blk in range(2):
            rows = slice(blk * T, (blk + 1) * T)
            mlps[blk].wait_recv()
            out = hr[l, rows, :] + y[rows, :] + ml_r[l, rows, :].astype(F32)
            if l == 0:
                sent = out.astype(BF16)
                r[1, rows, :] = sent
                normed_block(1, blk, blk, sent.astype(F32))
                if blk == 0:
                    @pl.when(core == 1)
                    def _():
                        loads[0].wait()
                        loads[1].wait()
                        v_fresh.wait()

                    @pl.when(core == 0)
                    def _():
                        for cp in qk_push:
                            cp.wait_recv()
                own_products(1, blk)
                value_products(1, pos(blk))
            else:
                y[rows, :] = out
                yb[rows, :] = out.astype(BF16)
        return sends + mlps

    finish_layer_inputs(0)
    for cp in rest_push:
        cp.start()
    pair_sends = middle(0)

    @pl.when(core == 1)
    def _():
        far_push.start()

    finish_layer_inputs(1)
    save(r, r_o)
    pair_sends += middle(1)
    save(y, y_o)
    save(yb, yb_o)

    @pl.when(core == 1)
    def _():
        far_come.wait_recv()
        fwd_push.start()
        e_load.wait()

    @pl.when(core == 0)
    def _():
        fwd_come.wait_recv()
        own_come.wait_recv()

    save(e.at[1], gy_o)
    save(sm, sm_o)
    for l in range(2):
        wvt[l] = jnp.transpose(wv[l * core])
        save(wqk.at[l], watt_o.at[l, pl.ds(0, D)])
        save(wout.at[l], watt_o.at[l, pl.ds(D, H)])
        save(wvt.at[l], watt_o.at[l, pl.ds(D + H, H)])
    save(wfc, wfc_o)
    save(wproj, wproj_o)
    far_push.wait_send()
    fwd_push.wait_send()
    own_push.wait_send()
    for cp in qk_push + rest_push + pair_sends:
        cp.wait_send()

    @pl.when(core == 0)
    def _():
        v_push.wait_send()

    for cp, come, onward, arrive, sp in xh_sends.values():
        cp.wait_send()
        onward.wait_send()
    for cp in saves:
        cp.wait()


def forward_pass(C, ends, segs, g1, b1, g2, b2, qkv, wo, fc, fcb, proj, shared):
    T, D, F = ends.shape[2], ends.shape[3], fc.shape[2]
    N, L, H, FH = C // 2, C * T, D // 2, F // 2
    R, pairs = 2 * T, D // 256
    S = jax.ShapeDtypeStruct
    outs = [S((2, L, D), BF16), S((2, R, H), BF16), S((2, L, H), BF16), S((2, L, H), BF16), S((2, R, H), BF16),
            S((2, pairs, R, 128), F32), S((2, R, D), BF16), S((2, R, D), F32), S((2, R, D), BF16), S((2, R, FH), BF16),
            S((2, R, FH), BF16), S((R, D), F32), S((R, D), BF16), S((2, T, D), BF16), S((2, 8, F), F32), S((2, 2 * D, D), BF16),
            S((2, D, FH), BF16), S((2, FH, D), BF16), S((1, L), jnp.int32)]
    V = pltpu.VMEM
    scratch = [V((2, 2, T, D), BF16), V((C, 1, T), jnp.int32), V((2, 8, F), F32), V((2, D, D), BF16), V((2, D, H), BF16),
               V((2, H, D), BF16), V((2, D, FH), BF16), V((2, FH, D), BF16), V((2, L, D), BF16), V((2, R, H), BF16),
               V((2, L, H), BF16), V((2, L, H), BF16), V((2, R, H), BF16), V((2, pairs, R, 128), F32), V((2, R, D), BF16),
               V((2, R, D), F32), V((2, R, D), BF16), V((2, R, FH), BF16), V((2, R, FH), BF16), V((R, D), F32),
               V((R, D), BF16), V((2, H, D), BF16), V((R, L), F32), V((2, R, D), BF16), V((2, R, D), BF16), V((2, R, D), BF16), V((2, R, D), BF16),
               pltpu.SemaphoreType.DMA((80 + 20 * N + 2 * C,))]
    return pl.pallas_call(
        functools.partial(forward_kernel, C, T, D, F),
        in_specs=[HBM, HBM, VM, VM, VM, VM, HBM, HBM, HBM, VM, HBM, HBM],
        out_specs=[HBM] * 18 + [VM],
        out_shape=outs,
        scratch_shapes=scratch,
        compiler_params=pltpu.CompilerParams(collective_id=0, has_side_effects=True, vmem_limit_bytes=VMEM_LIMIT),
        name="forward_pass",
    )(ends, segs, g1, b1, g2, b2, qkv, wo, fc, fcb, proj, shared)


class Job:
    def __init__(self, env, buf, lead, cols, order, sided, land, credits, first_layer, active, earlier):
        self.env, self.buf, self.lead, self.cols = env, buf, lead, cols
        self.sided, self.land, self.credits, self.first_layer, self.active = sided, land, credits, first_layer, active
        self.earlier = earlier
        self.bits = list(range(env.m - 2 if sided else env.m - 1, -1, -1))
        self.fixed, self.z_done, self.steps, self.at = {}, False, [], 0
        self.used = 0
        if sided:
            self.steps.append(("side", None, None))
        for item in order:
            if item == "z":
                for s in range(1, env.C):
                    self.steps.append(("z", s, dict(self.fixed)))
                self.z_done = True
            else:
                self.steps.append(("bit", item, (dict(self.fixed), self.z_done)))
                self.fixed[item] = env.bit(item)
        self.plans = [self.plan(i) for i in range(len(self.steps))]

    def view(self, fixed, zat):
        at = tuple(self.lead) + tuple(fixed.get(b, slice(None)) for b in self.bits)
        return at + (slice(None) if zat is None else zat, slice(None), self.cols)

    def plan(self, i):
        env = self.env
        kind, what, state = self.steps[i]
        moves = []
        if kind == "side":
            other = env.dp_xor(env.m - 1)
            moves.append((env.bit(env.m - 1) != env.core, self.view({}, None), other, env.bit(env.m - 1) == env.core,
                          self.view({}, None), other))
            return [self.bind(move, self.land[i]) for move in moves]
        active = self.active if not self.sided else (env.bit(env.m - 1) == env.core)
        if kind == "bit":
            fixed, z_done = state
            zat = env.z if z_done else None
            other = env.dp_xor(what)
            mine = env.bit(what)
            moves.append((active, self.view({**fixed, what: 1 - mine}, zat), other, active,
                          self.view({**fixed, what: mine}, zat), other))
            return [self.bind(move, self.land[i]) for move in moves]
        s, C, z = what, env.C, env.z
        zm = C - 1 - z
        for side, (p, sign) in enumerate(((z, 1), (zm, -1))):
            out_at = z + sign * (C - s)
            in_at = z + sign * (C - s - 1)
            moves.append((both(active, p < s), self.view(state, out_at), env.line(z + sign),
                          both(active, both(p >= 1, p <= s)), self.view(state, in_at), env.line(z - sign)))
        return [self.bind(move, self.land[i].at[side]) for side, move in enumerate(moves)]

    def bind(self, move, slot):
        send_if, src, to, recv_if, dst, source = move
        env = self.env
        sem_s, sem_r = env.sems.one(), env.sems.one()
        credit = self.credits.at[self.used]
        self.used += 1
        return send_if, src, to, recv_if, dst, source, slot, sem_s, sem_r, credit

    def send(self, i):
        for send_if, src, to, recv_if, dst, source, slot, sem_s, sem_r, credit in self.plans[i]:
            cp = push(self.buf.at[src], slot, sem_s, sem_r, to)

            def go(cp=cp, credit=credit):
                if not self.first_layer:
                    when(self.earlier, lambda: pl.semaphore_wait(credit, 1))
                cp.start()

            when(send_if, go)
            self.env.sent.append((send_if, cp))

    def take(self, i):
        for send_if, src, to, recv_if, dst, source, slot, sem_s, sem_r, credit in self.plans[i]:
            cp = push(slot, slot, sem_s, sem_r, to)

            def got(cp=cp, dst=dst, slot=slot, credit=credit, source=source):
                cp.wait_recv()
                self.buf[dst] = self.buf[dst] + slot[...]
                if self.first_layer:
                    pl.semaphore_signal(credit, inc=1, device_id=source, device_id_type=MESH)

            when(recv_if, got)

    def start(self):
        self.send(0)

    def advance(self):
        if self.at >= len(self.steps):
            return
        self.take(self.at)
        self.at += 1
        if self.at < len(self.steps):
            self.send(self.at)

    def own(self):
        return self.view(self.fixed, self.env.z)


def both(a, b):
    if a is True:
        return b
    if b is True:
        return a
    return jnp.logical_and(a, b)


def when(condition, fn):
    if condition is True:
        fn()
    else:
        pl.when(condition)(fn)


class Env:
    def __init__(self, C, m, core, dp, z, sems):
        self.C, self.m, self.core, self.dp, self.z, self.sems, self.sent = C, m, core, dp, z, sems, []

    def bit(self, b):
        return lax.rem(lax.div(self.dp, 1 << b), 2)

    def dp_xor(self, b):
        return (self.core, self.dp + (1 << b) * (1 - 2 * self.bit(b)), self.z)

    def line(self, z):
        return (self.core, self.dp, z)


def job_table(m):
    xs, ys = list(range(m)), list(range(m - 1, -1, -1))
    rest = list(range(m - 1))
    return {
        "P0": ("gproj", (0, 3), rest + ["z"], True), "P1": ("gproj", (1, 3), rest + ["z"], True),
        "P2": ("gproj", (2, 3), rest + ["z"], True),
        "F0": ("gfc", (0, 3), xs + ["z"], False), "F1": ("gfc", (1, 3), xs + ["z"], False),
        "F2": ("gfc", (2, 3), ["z"] + xs, False),
        "O": ("gout", (0, 1), rest + ["z"], True),
        "Q": ("gq", (0, 1), xs + ["z"], False), "K": ("gk", (0, 1), ["z"] + xs, False),
        "V": ("gv", (0, 1), ys + ["z"], False),
    }


def grad_shapes(C, m, D, F):
    H, FH, J = D // 2, F // 2, C << m
    full, side = (2,) * m + (C,), (2,) * (m - 1) + (C,)
    return {"gproj": side + (F // J, D), "gfc": full + (D // J, FH), "gout": side + (D // J, D),
            "gq": full + (D // J, H), "gk": full + (D // J, H), "gv": full + (D // J, H)}


def landing_shapes(C, m, D, F):
    shapes = grad_shapes(C, m, D, F)
    result = {}
    for name, (buf, (at, parts), order, sided) in job_table(m).items():
        shape = list(shapes[buf])
        shape[-1] //= parts
        n = m - 1 if sided else m
        lead = {b: 2 for b in range(n)}
        tail = [shape[-2], shape[-1]]
        zdim = [C]
        steps = []
        if sided:
            steps.append(tuple([2] * n + zdim + tail))
        for item in order:
            if item == "z":
                zdim = []
                for s in range(1, C):
                    steps.append(tuple([2] + [2] * len(lead) + tail))
            else:
                lead.pop(item)
                steps.append(tuple([2] * len(lead) + zdim + tail))
        result[name] = steps
    return result


def norm_grad(values, gain, grad):
    unit, rstd = unit_norm(values)
    scaled = grad * gain
    m1 = jnp.mean(scaled, axis=-1, keepdims=True)
    m2 = jnp.mean(scaled * unit, axis=-1, keepdims=True)
    back = rstd * (scaled - m1 - unit * m2)
    return back, jnp.sum(grad * unit, axis=0, keepdims=True), jnp.sum(grad, axis=0, keepdims=True)


def attention_back_pair(i, T, L, q, k, v, o, lse, goa, bias, dq, dk, dv, dv_at):
    cols = slice(i * 128, (i + 1) * 128)
    lane = lax.broadcasted_iota(jnp.int32, (T, 128), 1)
    scale = jnp.asarray(HEAD**-0.5, BF16)
    totals = None
    for blk in (1, 0):
        rows = slice(blk * T, (blk + 1) * T)
        keys = L if blk else L // 2
        q2, go2 = q[rows, cols] * scale, goa[rows, cols]
        prod = go2.astype(F32) * o[rows, cols].astype(F32)
        k2, v2 = k[:keys, cols], v[:keys, cols]
        dqs, dks, dvs = [], None, None
        for h in range(2):
            sel = (lane >= 64) == (h == 1)
            qh = jnp.where(sel, q2, jnp.zeros_like(q2))
            goh = jnp.where(sel, go2, jnp.zeros_like(go2))
            delta = jnp.sum(jnp.where(sel, prod, 0.0), axis=-1, keepdims=True)
            s = mm_nt(qh, k2) + bias[rows, :keys]
            prob = jnp.exp(s - lse[i, rows, 64 * h : 64 * h + 1])
            gp = mm_nt(goh, v2)
            gs = (prob * (gp - delta)).astype(BF16)
            dqs.append(mm(gs, k2))
            one_k = mm_tn(gs, qh)
            one_v = mm_tn(prob.astype(BF16), goh)
            dks = one_k if dks is None else dks + one_k
            dvs = one_v if dvs is None else dvs + one_v
        dq[rows, cols] = (jnp.where(lane < 64, dqs[0], dqs[1]) * HEAD**-0.5).astype(BF16)
        if blk:
            totals = (dks, dvs)
        else:
            dk[:keys, cols] = (totals[0][:keys] + dks).astype(BF16)
            dk[keys:, cols] = totals[0][keys:].astype(BF16)
            dv[dv_at, :keys, cols] = (totals[1][:keys] + dvs).astype(BF16)
            dv[dv_at, keys:, cols] = totals[1][keys:].astype(BF16)


LOADED = ("gp", "act", "hh", "hr", "o", "q", "k", "v", "lse", "xall", "r")


def backward_kernel(C, m, T, D, F, fused, names_in, *refs):
    n_in = len(names_in)
    hbm = dict(zip(names_in, refs[:n_in]))
    outs, (vm, dma, credits) = refs[n_in:-3], refs[-3:]
    ends_o, small_o = outs[:2]
    core, dp, z = lax.axis_index(SECTION), lax.axis_index(DP), lax.axis_index(CTX)
    N, L, H, FH = C // 2, C * T, D // 2, F // 2
    row = lax.div(z, N)
    lo = z + row * (C - 1 - 2 * z)
    hi = C - 1 - lo
    base = row * N
    pairs = H // 128
    sems = Sems(dma)
    env = Env(C, m, core, dp, z, sems)
    sib = (1 - core, dp, z)
    mirror = (core, dp, C - 1 - z)
    pos = lambda blk: lo + blk * (hi - lo)
    block = lambda at: pl.ds(pl.multiple_of(at * T, T), T)
    other_nodes = [base + lax.rem(z - base + n, N) for n in range(1, N)]
    sent = env.sent
    loads = {}

    def load(name, l, src=None, dst=None):
        cp = pltpu.make_async_copy(hbm[name].at[l] if src is None else src, vm[name] if dst is None else dst, sems.one())
        cp.start()
        loads[(name, l)] = cp

    def need(*names):
        for name in names:
            loads[name].wait()

    def pushed(src, dst, to, condition=True, until=sent):
        cp = push(src, dst, sems.one(), sems.one(), to)
        when(condition, cp.start)
        until.append((condition, cp))
        return cp

    load("gy", 1, hbm["gy"].at[0], vm["gm"].at[slice(0, T)])
    load("gy", 0, hbm["gy"].at[1], vm["gm"].at[slice(T, 2 * T)])
    load("wproj", 1, dst=vm["wa"])
    load("gp", 1)
    load("wfc", 1)
    load("act", 1)
    load("hh", 1)
    load("hr", 1)
    load("sm", 0, hbm["sm"], vm["sm"])
    for name in ("o", "q", "k", "v", "lse", "xall", "r"):
        load(name, 1)
    y_keep = pltpu.make_async_copy(hbm["y"].at[block(row)], ends_o.at[0, row], sems.one())
    when(core == 1, y_keep.start)

    kseg = hbm["kseg"]
    for blk in range(2):
        rows = slice(blk * T, (blk + 1) * T)
        qpos = pos(blk) * T + lax.broadcasted_iota(jnp.int32, (T, L), 0)
        kpos = lax.broadcasted_iota(jnp.int32, (T, L), 1)
        mine = kseg[0:1, 0:T]
        for n in range(1, C):
            mine = jnp.where(pos(blk) == n, kseg[0:1, n * T : (n + 1) * T], mine)
        allowed = (kpos <= qpos) & (kseg[...] == column(mine))
        vm["bias"][rows, :] = jnp.where(allowed, 0.0, MASKED)

    greet([sib] + [env.line(lax.rem(z + n, C)) for n in range(1, C)] + [env.dp_xor(b) for b in range(m)])

    y_push = pushed(hbm["yb"].at[block(1 - row)], vm["far"], mirror, core == 1)

    table = job_table(m)
    jobs = {}

    def start(name, l):
        if not fused:
            return
        buf, (at, parts), order, sided = table[name]
        width = vm[buf].shape[-1] // parts
        earlier = True if name != "V" else core == 1
        active = True if l == 0 else earlier
        jobs[(name, l)] = Job(env, vm[buf], (l,), slice(at * width, (at + 1) * width), order, sided, vm["land"][name],
                              credits[name], l == 1, active, earlier)
        jobs[(name, l)].start()

    def adv(l, *names):
        if not fused:
            return
        for name in names:
            jobs[(name, l)].advance()

    gm, gp, go, ghh, wa, wfc = vm["gm"], vm["gp"], vm["go"], vm["ghh"], vm["wa"], vm["wfc"]
    sm, sg = vm["sm"], vm["sg"]

    def put(buf, l, cols, value):
        shape = vm[buf].shape[1:-1] + (value.shape[-1],)
        vm[buf][(l,) + (slice(None),) * (len(shape) - 1) + (cols,)] = value.astype(BF16).reshape(shape)

    def layer_back(l, poll):
        again = []
        need(("wproj", l), ("gp", l))
        bias_sum = None
        for blk in range(2):
            rows = slice(blk * T, (blk + 1) * T)
            if l == 1:
                need(("gy", 1 - blk))
                go[rows, :] = gm[rows, :].astype(F32)
            gu = (gp[rows, :].astype(F32) * mm_nt(gm[rows, :], wa[...])).astype(BF16)
            gp[rows, :] = gu
            part = jnp.sum(gu.astype(F32), axis=0, keepdims=True)
            bias_sum = part if bias_sum is None else bias_sum + part
        sg[l, 4:5, :] = bias_sum
        load("watt", l, dst=wa)
        need(("wfc", l))
        shares = []
        for blk in range(2):
            rows = slice(blk * T, (blk + 1) * T)
            part = mm_nt(gp[rows, :], wfc[...])
            ghh[rows, :] = part
            vm["a_s"][rows, :] = part.astype(BF16)
            shares.append(pushed(vm["a_s"].at[rows, :], vm["a_r"].at[rows, :], sib, until=again))
        if l == 1:
            load("wfc", 0)
        poll("up")
        need(("act", l))
        third = D // 3
        for i in range(3):
            cols = slice(i * third, (i + 1) * third)
            put("gproj", l, cols, mm_tn(vm["act"][...], gm[:, cols]))
            start("P%d" % i, l)
        poll("proj")
        if l == 1:
            load("act", 0)
        need(("hh", l))
        third = FH // 3
        for i in (2, 0, 1):
            cols = slice(i * third, (i + 1) * third)
            put("gfc", l, cols, mm_tn(vm["hh"][...], gp[:, cols]))
            start("F%d" % i, l)
        poll("fc")
        if l == 1:
            load("hh", 0)
            load("gp", 0)
        need(("hr", l), ("watt", l))
        if l == 1:
            need(("sm", 0))
        sums = None
        for blk in range(2):
            rows = slice(blk * T, (blk + 1) * T)
            shares[blk].wait_recv()
            grad = ghh[rows, :] + vm["a_r"][rows, :].astype(F32)
            back, gain_sum, bias_sum = norm_grad(vm["hr"][rows, :], sm[l, 2:3, :D], grad)
            total = go[rows, :] + back
            go[rows, :] = total
            low = total.astype(BF16)
            gm[rows, :] = low
            vm["goa"][rows, :] = mm_nt(low, wa[D : D + H, :]).astype(BF16)
            sums = (gain_sum, bias_sum) if sums is None else (sums[0] + gain_sum, sums[1] + bias_sum)
        sg[l, 2:3, :D] = sums[0]
        sg[l, 3:4, :D] = sums[1]
        if l == 1:
            load("hr", 0)
        need(("o", l))
        put("gout", l, slice(0, D), mm_tn(vm["o"][...], gm[...]))
        start("O", l)
        poll("norm")
        need(("q", l), ("k", l), ("v", l), ("lse", l))
        for i in range(pairs):
            attention_back_pair(i, T, L, vm["q"], vm["k"], vm["v"], vm["o"], vm["lse"], vm["goa"], vm["bias"], vm["dq"],
                                vm["dk"], vm["dv"], l)
            poll("pair%d" % i)
        if l == 1:
            for name in ("o", "q", "k", "v", "lse"):
                load(name, 0)
        else:
            def merge():
                vm["dv"][0] = (vm["dv"][0].astype(F32) + vm["dv"][1].astype(F32)).astype(BF16)

            when(core == 0, merge)
        dk, dv, dq = vm["dk"], vm["dv"], vm["dq"]

        def key_part(at):
            part_v = dv[l, block(at), :]
            if l == 1:
                part_v = jnp.where(core == 1, part_v, jnp.zeros_like(part_v))
            return mm_nt(dk[block(at), :], wa[:D, H:]) + mm(part_v, wa[D + H :, :])

        crossing, gives = [], []
        for n, node in enumerate(other_nodes):
            dlo = node + row * (C - 1 - 2 * node)
            dhi = C - 1 - dlo
            vm["fs_s"][n] = key_part(dlo + (1 - core) * (dhi - dlo)).astype(BF16)
            gives.append(pushed(vm["fs_s"].at[n], vm["fs_r"].at[n], sib, until=again))
        for n, node in enumerate(other_nodes):
            dlo = node + row * (C - 1 - 2 * node)
            keep = key_part(dlo + core * (C - 1 - 2 * dlo))
            gives[n].wait_recv()
            vm["fx_s"][l, n] = (keep + vm["fs_r"][n].astype(F32)).astype(BF16)
            crossing.append(pushed(vm["fx_s"].at[l, n], vm["fx_r"].at[l, n], (core, dp, node)))
        poll("cross")
        for blk in range(2):
            rows = slice(blk * T, (blk + 1) * T)
            ghh[rows, :] = key_part(pos(blk)) + mm_nt(dq[rows, :], wa[:D, :H])
        early = pl.ds(pl.multiple_of((1 - core) * T, T), T)
        late = pl.ds(pl.multiple_of(core * T, T), T)
        vm["b_s"][early, :] = ghh[early, :].astype(BF16)
        shares = [pushed(vm["b_s"].at[early, :], vm["b_r"].at[early, :], sib, until=again)]
        if l == 1:
            load("wproj", 0, dst=wa)
        need(("xall", l))
        xall = vm["xall"]
        put("gk", l, slice(0, H), mm_tn(xall[...], dk[...]))
        start("K", l)
        put("gq", l, slice(0, H), mm_tn(xall[block(lo), :], dq[:T, :]) + mm_tn(xall[block(hi), :], dq[T:, :]))
        start("Q", l)
        put("gv", l, slice(0, H), mm_tn(xall[...], dv[l]))
        start("V", l)
        poll("qkv")
        if l == 1:
            load("xall", 0)
        need(("r", l))
        for n in range(N - 1):
            crossing[n].wait_recv()
            ghh[late, :] += vm["fx_r"][l, n].astype(F32)
        vm["b_s"][late, :] = ghh[late, :].astype(BF16)
        shares.append(pushed(vm["b_s"].at[late, :], vm["b_r"].at[late, :], sib, until=again))
        for cp in shares:
            cp.wait_recv()
        sums = None
        for blk in range(2):
            rows = slice(blk * T, (blk + 1) * T)
            grad = ghh[rows, :] + vm["b_r"][rows, :].astype(F32)
            back, gain_sum, bias_sum = norm_grad(vm["r"][rows, :].astype(F32), sm[l, 0:1, :D], grad)
            total = go[rows, :] + back
            go[rows, :] = total
            if l == 1:
                gm[rows, :] = total.astype(BF16)
            sums = (gain_sum, bias_sum) if sums is None else (sums[0] + gain_sum, sums[1] + bias_sum)
        sg[l, 0:1, :D] = sums[0]
        sg[l, 1:2, :D] = sums[1]
        if l == 1:
            load("r", 0)
        for condition, cp in again:
            when(condition, cp.wait_send)

    def poll_first(where):
        plan = {
            "norm": ["F2"], "pair0": ["F2"], "pair2": ["F2"], "cross": ["F0", "F1", "F2"], "qkv": ["F2"],
        }
        adv(1, *plan.get(where, []))

    def poll_second(where):
        plan = {
            "up": ["P0", "P1", "P2", "K", "F0", "F1"],
            "proj": ["F0", "F1", "K", "O"],
            "fc": ["F0", "F1", "K", "Q", "V", "P0", "P1", "P2"],
            "norm": ["F0", "F1", "K", "Q", "V", "O"],
            "pair0": ["P0", "P1", "P2", "K", "Q", "V", "O"],
            "pair1": ["P0", "P1", "P2", "Q", "V", "O"],
            "pair2": ["P0", "P1", "P2", "Q", "V", "O"],
        }
        adv(1, *plan.get(where, []))
        if where in ("pair0", "pair1", "pair2"):
            adv(0, "F2")
        if where == "cross":
            adv(0, "F0", "F1", "F2")
        if where == "qkv":
            adv(0, "F2", "F0", "F1")

    layer_back(1, poll_first)
    layer_back(0, poll_second)

    keep = pl.ds(pl.multiple_of(row * T, T), T)
    away = pl.ds(pl.multiple_of((1 - row) * T, T), T)
    vm["far_s"][...] = go[away, :].astype(BF16)
    x_push = pushed(vm["far_s"], vm["far"], mirror, core == 0)
    x_keep = pltpu.make_async_copy(go.at[keep, :], ends_o.at[0, row], sems.one())
    when(core == 0, x_keep.start)

    sv, sv_r = vm["sv"], vm["sv_r"]
    sv[0] = jnp.zeros_like(sv[0])
    sv[0, 0:4, :] = sg[core, 0:4, :]
    sv[0, 4:5, :] = sg[0, 4:5, :]
    sv[0, 5:6, :] = sg[1, 4:5, :]
    around = [env.dp_xor(b) for b in range(m)]
    b = 1
    while b < C:
        around.append(env.line(z + b * (1 - 2 * lax.rem(lax.div(z, b), 2))))
        b *= 2
    small_at = [0]
    small_cp = [pushed(sv.at[0], sv_r.at[0], around[0])]

    def small_step():
        i = small_at[0]
        small_cp[0].wait_recv()
        sv[i + 1] = sv[i] + sv_r[i]
        small_at[0] += 1
        if i + 1 < len(around):
            small_cp[0] = pushed(sv.at[i + 1], sv_r.at[i + 1], around[i + 1])

    def finish_ends():
        when(core == 0, x_push.wait_recv)
        when(core == 1, y_push.wait_recv)
        vm["far_f"][...] = vm["far"][...].astype(F32)
        far_keep = pltpu.make_async_copy(vm["far_f"], ends_o.at[0, 1 - row], sems.one())
        far_keep.start()
        far_keep.wait()
        when(core == 0, x_keep.wait)
        when(core == 1, y_keep.wait)

    if fused:
        for name in ("P0", "F0", "P1", "F1", "P2", "F2", "K", "O", "Q", "V"):
            for _ in range(len(jobs[(name, 1)].steps)):
                adv(1, name)
        order = ["F0", "F1", "F2", "K", "P0", "P1", "P2", "Q", "O", "V"]
        while any(jobs[(name, 0)].at < len(jobs[(name, 0)].steps) for name in order):
            adv(0, *order)
            if small_at[0] < len(around):
                small_step()
    while small_at[0] < len(around):
        small_step()
    last = len(around)
    small_o[...] = sv[last]

    if fused:
        hand_over(core, sib, env, vm, jobs, m, D, H, FH, pushed, sv, last, outs)
    else:
        leave = []
        for name, out in zip(("gproj", "gfc", "gout", "gq", "gk", "gv"), outs[2:]):
            leave.append(pltpu.make_async_copy(vm[name], out, sems.one()))
            leave[-1].start()
        for cp in leave:
            cp.wait()
    finish_ends()
    for condition, cp in sent:
        when(condition, cp.wait_send)


def hand_over(core, sib, env, vm, jobs, m, D, H, FH, pushed, sv, last, outs):
    small_o, qkv_o, out_o, fc_o, proj_o, shared_o = outs[1:]
    vm["fb_s"][...] = jnp.where(core == 0, sv[last, 5:6, :], sv[last, 4:5, :])
    fin = vm["fin"]
    top = env.bit(m - 1) == core
    own = lambda name, l: (l,) + jobs[(name, 0)].own()[1:]
    arrive = [
        pushed(vm["gfc"].at[own("F0", 1 - core)[:-1]], fin["fc"], sib),
        pushed(vm["gq"].at[own("Q", 1 - core)], fin["q"], sib),
        pushed(vm["gk"].at[own("K", 1 - core)], fin["k"], sib),
        pushed(vm["gv"].at[own("V", 0)], fin["v"], sib),
        pushed(vm["fb_s"], fin["fb"], sib),
    ]
    out_push = pushed(vm["gout"].at[own("O", 1 - core)], fin["out"], sib, top)
    proj_push = pushed(vm["gproj"].at[own("P0", 1 - core)[:-1]], fin["proj"], sib, top)

    here = pl.ds(pl.multiple_of(core * H, 128), H)
    there = pl.ds(pl.multiple_of((1 - core) * H, 128), H)
    here_k = pl.ds(pl.multiple_of(D + core * H, 128), H)
    there_k = pl.ds(pl.multiple_of(D + (1 - core) * H, 128), H)
    qkv_o[0, :, here] = vm["gq"][own("Q", core)].astype(F32)
    qkv_o[0, :, here_k] = vm["gk"][own("K", core)].astype(F32)
    fc_o[0, :, pl.ds(pl.multiple_of(core * FH, 128), FH)] = vm["gfc"][own("F0", core)[:-1]].astype(F32)

    def top_out():
        out_o[0] = vm["gout"][own("O", core)].astype(F32)
        proj_o[0] = vm["gproj"][own("P0", core)[:-1]].astype(F32)

    when(top, top_out)
    for cp in arrive:
        cp.wait_recv()

    def other_out():
        out_push.wait_recv()
        proj_push.wait_recv()
        out_o[0] = fin["out"][...].astype(F32)
        proj_o[0] = fin["proj"][...].astype(F32)

    when(jnp.logical_not(top), other_out)
    qkv_o[0, :, there] = fin["q"][...].astype(F32)
    qkv_o[0, :, there_k] = fin["k"][...].astype(F32)
    fc_o[0, :, pl.ds(pl.multiple_of((1 - core) * FH, 128), FH)] = fin["fc"][...].astype(F32)
    fresh = pl.ds(2 * D, H)

    def fresh_first():
        qkv_o[0, :, fresh] = fin["v"][...].astype(F32)
        shared_o[...] = vm["gv"][own("V", 0)].astype(F32)

    def fresh_second():
        qkv_o[0, :, fresh] = vm["gv"][own("V", 1)].astype(F32)
        shared_o[...] = fin["v"][...].astype(F32)

    when(core == 0, fresh_first)
    when(core == 1, fresh_second)
    small_o[6:7, :] = fin["fb"][...]


def backward_pass(C, m, T, D, F, inputs):
    N, L, H, FH, R, J = C // 2, C * T, D // 2, F // 2, 2 * T, C << m
    fused = (D // J) % 16 == 0 and (F // J) % 16 == 0 and m > 0
    pairs = H // 128
    S, V = jax.ShapeDtypeStruct, pltpu.VMEM
    names = tuple(inputs)
    outs = [S((1, 2, T, D), F32), S((8, FH), F32)]
    flat = {"gproj": (FH, D), "gfc": (D, FH), "gout": (H, D), "gq": (D, H), "gk": (D, H), "gv": (D, H)}
    if fused:
        outs += [S((1, D // J, 5 * H), F32), S((1, D // J, D), F32), S((1, D // J, F), F32), S((1, F // J, D), F32),
                 S((D // J, H), F32)]
        grads = grad_shapes(C, m, D, F)
        land = {name: [V(shape, BF16) for shape in steps] for name, steps in landing_shapes(C, m, D, F).items()}
    else:
        outs += [S((2,) + shape, BF16) for shape in flat.values()]
        grads, land = flat, {}
    stages = m + C.bit_length() - 1
    vm = dict(
        gm=V((R, D), BF16), gp=V((R, FH), BF16), act=V((R, FH), BF16), hh=V((R, D), BF16), hr=V((R, D), F32),
        o=V((R, H), BF16), q=V((R, H), BF16), k=V((L, H), BF16), v=V((L, H), BF16), lse=V((pairs, R, 128), F32),
        xall=V((L, D), BF16), r=V((R, D), BF16), sm=V((2, 8, F), F32), sg=V((2, 8, FH), F32), bias=V((R, L), F32),
        wa=V((2 * D, D), BF16), wfc=V((D, FH), BF16), go=V((R, D), F32), ghh=V((R, D), F32), a_s=V((R, D), BF16),
        a_r=V((R, D), BF16), b_s=V((R, D), BF16), b_r=V((R, D), BF16), goa=V((R, H), BF16), dq=V((R, H), BF16),
        dk=V((L, H), BF16), dv=V((2, L, H), BF16), fs_s=V((N - 1, T, D), BF16), fs_r=V((N - 1, T, D), BF16),
        fx_s=V((2, N - 1, T, D), BF16), fx_r=V((2, N - 1, T, D), BF16), far=V((T, D), BF16), far_s=V((T, D), BF16),
        far_f=V((T, D), F32), sv=V((stages + 1, 8, FH), F32), sv_r=V((stages, 8, FH), F32), fb_s=V((1, FH), F32),
        fin=dict(fc=V((D // J, FH), BF16), q=V((D // J, H), BF16), k=V((D // J, H), BF16), v=V((D // J, H), BF16),
                 out=V((D // J, D), BF16), proj=V((F // J, D), BF16), fb=V((1, FH), F32)),
        land=land, **{name: V((2,) + shape, BF16) for name, shape in grads.items()})
    moves = 1 + m + 2 * (C - 1)
    credits = {name: pltpu.SemaphoreType.REGULAR((moves,)) for name in job_table(m)} if fused else {}
    in_specs = [VM if name == "kseg" else HBM for name in names]
    return pl.pallas_call(
        functools.partial(backward_kernel, C, m, T, D, F, fused, names),
        in_specs=in_specs,
        out_specs=[HBM, VM] + [VM if fused else HBM] * (len(outs) - 2),
        out_shape=outs,
        scratch_shapes=[vm, pltpu.SemaphoreType.DMA((120 + 40 * moves,)), credits],
        compiler_params=pltpu.CompilerParams(collective_id=1, has_side_effects=True, vmem_limit_bytes=VMEM_LIMIT),
        name="backward_pass",
    )(*inputs.values())


def xor_route(size, bit):
    return [(i, i ^ (1 << bit)) for i in range(size)]


def halve(grad, axis_name, bit, at):
    mine = (lax.axis_index(axis_name) >> bit) & 1
    keep = lax.dynamic_index_in_dim(grad, mine, at, keepdims=False)
    send = lax.dynamic_index_in_dim(grad, 1 - mine, at, keepdims=False)
    got = lax.ppermute(send, axis_name, xor_route(lax.axis_size(axis_name), bit))
    return (keep.astype(F32) + got.astype(F32)).astype(grad.dtype)


def bits_of(axis_name):
    return lax.axis_size(axis_name).bit_length() - 1


def scatter_sum(grad, order, skip_first=False):
    dims = [(DP, b) for b in reversed(range(bits_of(DP)))] + [(CTX, b) for b in reversed(range(bits_of(CTX)))]
    if skip_first:
        dims = dims[1:]
    parts = len(dims)
    rows, cols = grad.shape
    grad = grad.reshape((2,) * parts + (rows >> parts, cols))
    for item in order:
        at = dims.index(item)
        grad = halve(grad, item[0], item[1], at)
        dims.pop(at)
    return grad


def shards(ends, segment_ids, ln1_gain, ln1_bias, qkv_weight, out_weight, ln2_gain, ln2_bias, fc_weight, fc_bias,
           proj_weight, shared_weight):
    core = lax.axis_index(SECTION)
    first = core == 0
    C, m = lax.axis_size(CTX), bits_of(DP)
    J = C << m
    micros, T, D = ends.shape[1:]
    F = fc_weight.shape[2]
    half, FH = D // 2, F // 2
    names = ("xall", "q", "k", "v", "o", "lse", "r", "hr", "hh", "gp", "act", "y", "yb", "gy", "sm", "watt", "wfc", "wproj", "kseg")
    kept = dict(zip(names, forward_pass(
        C, ends, segment_ids.reshape(micros, 1, T), ln1_gain, ln1_bias, ln2_gain, ln2_bias, qkv_weight, out_weight,
        fc_weight, fc_bias, proj_weight, shared_weight)))
    block, small, *grads = backward_pass(C, m, T, D, F, kept)
    if len(grads) == 5:
        qkv_out, out_out, fc_out, proj_out, shared_out = grads
        other_bias = small[6]
    else:
        qkv_out, out_out, fc_out, proj_out, shared_out = scattered(grads, core, m, half)
        other_bias = swap(jnp.where(first, small[5], small[4]))
    own_bias = jnp.where(first, small[4], small[5])
    bias_grad = jnp.concatenate([jnp.where(first, own_bias, other_bias), jnp.where(first, other_bias, own_bias)])
    j = lax.axis_index(DP) * C + lax.axis_index(CTX)
    fcb_out = lax.dynamic_slice_in_dim(bias_grad, j * (F // J), F // J, 0)
    ln = lax.dynamic_slice_in_dim(small[:4], j * (D // J), D // J, 1)
    return (block, qkv_out, out_out, fc_out, fcb_out[None], proj_out, shared_out, ln[0:1], ln[1:2], ln[2:3], ln[3:4])


def scattered(grads, core, m, half):
    gproj, gfc, gout, gq, gk, gv = grads
    first = core == 0
    x_first = [(DP, b) for b in range(m)] + [(CTX, b) for b in range(bits_of(CTX))]
    y_first = [(DP, b) for b in reversed(range(m))] + x_first[m:]

    def sided(grad):
        dp, size = lax.axis_index(DP), lax.axis_size(DP)
        top = size // 2
        route = [(c * size + d, c * size + (d ^ top)) for c in range(2) for d in range(size) if (d >= top) != (c == 1)]
        got = lax.ppermute(grad, (SECTION, DP), route)
        return scatter_sum((grad.astype(F32) + got.astype(F32)).astype(BF16), y_first[1:], skip_first=True)

    res = []
    for l in range(2):
        qkv = jnp.concatenate([gq[l], gk[l], gv[l]], axis=1)
        res.append((scatter_sum(qkv, x_first), sided(gout[l]), scatter_sum(gfc[l], x_first), sided(gproj[l])))
    holder = jnp.where(lax.axis_index(DP) >= lax.axis_size(DP) // 2, 1, 0) == core
    mine = tuple(jnp.where(first, a, b) for a, b in zip(res[0], res[1]))
    got = tuple(swap(jnp.where(first, b, a)) for a, b in zip(res[0], res[1]))
    left, right = [jnp.where(first, a, b).astype(F32) for a, b in zip(mine, got)], [jnp.where(first, b, a).astype(F32) for a, b in zip(mine, got)]
    fresh0 = res[0][0][:, 2 * half :]
    fresh0_other = swap(fresh0)
    fresh = jnp.where(first, fresh0_other, res[1][0][:, 2 * half :]).astype(F32)
    qkv_out = jnp.concatenate([left[0][:, :half], right[0][:, :half], left[0][:, half : 2 * half], right[0][:, half : 2 * half], fresh], axis=1)
    fc_out = jnp.concatenate([left[2], right[2]], axis=1)
    out_out = jnp.where(holder, mine[1], got[1]).astype(F32)
    proj_out = jnp.where(holder, mine[3], got[3]).astype(F32)
    shared_out = jnp.where(first, fresh0, fresh0_other).astype(F32)
    return qkv_out[None], out_out[None], fc_out[None], proj_out[None], shared_out


def solution(mesh):
    placed = (
        P(SECTION, DP, CTX, None), P(DP, CTX), P(SECTION, None), P(SECTION, None),
        P(SECTION, None, None), P(SECTION, None, None), P(SECTION, None), P(SECTION, None),
        P(SECTION, None, None), P(SECTION, None), P(SECTION, None, None), P(),
    )
    both = (DP, CTX)
    return jax.shard_map(
        shards, mesh=mesh, in_specs=placed,
        out_specs=(P(SECTION, DP, CTX, None), P(SECTION, both, None), P(SECTION, both, None),
                   P(SECTION, both, None), P(SECTION, both), P(SECTION, both, None), P(both, None),
                   P(SECTION, both), P(SECTION, both), P(SECTION, both), P(SECTION, both)),
        check_vma=False,
    )
```

time: 518 us -> 269 us (0.52); the launches traced: 508 us -> 265 us
  waiting for transfers between devices: 183 us -> 0 us
  Pallas kernels: 95.3 us -> 253 us
  other arithmetic: 63.6 us -> 1.66 us
  starting transfers between devices: 57 us -> 0 us
  local copies, waits for them, and re-layouts: 58.5 us -> 9.03 us
  matrix products: 48.2 us -> 0 us
    ppermute x51 -> x0, waiting for transfers between devices: 183 us -> none  [the longest x32 139 us: halve(): lax.ppermute(send, axis_name, xor_route(lax.axis_size(axis_name), bit))]
    pallas_call x2 -> x1, Pallas kernels: 22.3 us -> 180 us  [backward_pass(): pl.pallas_call(functools.partial(backward_kernel, C, m, T, D, F, fused, n...]
    ppermute x51 -> x0, starting transfers between devices: 57 us -> none  [the longest x32 23.4 us: halve(): lax.ppermute(send, axis_name, xor_route(lax.axis_size(axis_name), bit))]
    dot_general x24 -> x0, matrix products: 48.2 us -> none  [the longest x12 25.2 us: mm_tn(): lax.dot_general(left, right, (((0,), (0,)), ((), ())), preferred_element_...]
    convert_element_type x36 -> x0, other arithmetic: 19.7 us -> none  [the longest x4 8.78 us: sided(): total = (grad.astype(F32) + got.astype(F32)).astype(BF16)]
    dynamic_slice x18 -> x1, local copies, waits for them, and re-layouts: 14.7 us -> 0.07 us  [shards(): ln = lax.dynamic_slice_in_dim(small[:4], j * (D // J), D // J, 1)]
    squeeze x30 -> x0, local copies, waits for them, and re-layouts: 13.3 us -> none  [the longest x24 3.96 us: halve(): send = lax.dynamic_index_in_dim(grad, 1 - mine, at, keepdims=False)]
    reduce_sum x8 -> x0, other arithmetic: 12.4 us -> none  [the longest x4 9.77 us: norm_back(): jnp.sum(grad * unit, axis=0)]
  transfers between devices with their start and end apart: 51 -> 0, of which waited for: 22 -> 0; matrix products, arithmetic and copies ran while one was open for 29% -> 0% of each run, Pallas kernels for 4% -> 0%
where the time goes in v3:
time: 269 us; the launch traced here: 265 us
  Pallas kernels  253 us (94%)
  local copies, waits for them, and re-layouts  9.03 us (3%)
    pallas_call x1, Pallas kernels, backward_pass(): pl.pallas_call(functools.partial(backward_kernel, C, m, T, D, F, fused, n...  180 us
    pallas_call x1, Pallas kernels, forward_pass(): pl.pallas_call(functools.partial(forward_kernel, C, T, D, F), in_specs=[H...  73.6 us
    unnamed x16, local copies, waits for them, and re-layouts  6.37 us

profile of v3, /device:TPU:1, one launch (start us, length us, event | category | flops | bytes accessed | tf_op | source)
XLA Modules:
  0.0 265.1 jit_solution(6404890739491157047)
XLA Ops:
  0.6 1.3 reshape.31.segs
  1.9 73.6 %forward_pass.1 = (bf16[2,1024,768]{2,1,0:T(8,128)(2,1)}, bf16[2,512,384]{2,1,0:T(8,128)(2,1)}, bf16[2,1024,384]{2,1,0:T(8,128)(2,1)}, bf16[2,1024,384]{2,1,0:T(...) custom-call(bf16[1,2,256,768]{3,2,1,0:T(8,128)(2,1)} %ends.1, ...), custom_call_target="tpu_custom_call" | custom-call | tf_op jit(solution)/shard_map/forward_pass/pallas_call | solution.py:489
  75.5 179.7 %backward_pass.1 = (f32[1,2,256,768]{3,2,1,0:T(8,128)}, f32[8,1536]{1,0:T(8,128)}, f32[1,48,1920]{2,1,0:T(8,128)}, f32[1,48,768]{2,1,0:T(8,128)}, f32[1,48,3072]...) custom-call(bf16[2,1024,768]{2,1,0:T(8,128)(2,1)} %get-tuple-element.37.refs_0_, ...), custom_call_target="tpu_custom_call" | custom-call | tf_op jit(solution)/shard_map/backward_pass/pallas_call | solution.py:1143
  255.2 0.0 copy-start.2
  255.2 0.0 copy-start.3
  255.2 0.0 copy-start.1
  255.2 0.0 copy-start
  255.2 1.0 fusion.1
  256.2 0.7 fusion.2
  256.9 0.8 slice.27
  257.7 0.1 constant_dynamic-slice_fusion
  257.8 0.5 fusion.3
  258.3 0.0 copy-start.4
  258.3 2.7 %copy.29 = f32[1,2,256,768]{3,2,1,0:T(8,128)} copy(f32[1,2,256,768]{3,2,1,0:T(8,128)} %get-tuple-element.80) | data formatting | bytes 3145728
  261.0 0.0 copy-done.2
  261.0 0.7 copy.30
  261.7 0.0 copy-done.3
  261.7 0.7 copy.31
  262.4 0.0 copy-done.1
  262.4 0.8 copy.32
  263.2 0.0 copy-done
  263.2 0.8 copy.33
  264.0 0.0 copy-done.4
  264.0 0.6 copy.34
Async XLA Ops:
  255.2 5.8 %copy-start.2 = (f32[1,48,1920]{2,1,0:T(8,128)S(1)}, f32[1,48,1920]{2,1,0:T(8,128)}, u32[]{:S(2)}) copy-start(f32[1,48,1920]{2,1,0:T(8,128)} %get-tuple-element.81) | copy-start | bytes 1105924
  255.2 6.5 %copy-start.3 = (f32[1,48,768]{2,1,0:T(8,128)S(1)}, f32[1,48,768]{2,1,0:T(8,128)}, u32[]{:S(2)}) copy-start(f32[1,48,768]{2,1,0:T(8,128)} %get-tuple-element.82) | copy-start | bytes 442372
  255.2 7.2 %copy-start.1 = (f32[1,48,3072]{2,1,0:T(8,128)S(1)}, f32[1,48,3072]{2,1,0:T(8,128)}, u32[]{:S(2)}) copy-start(f32[1,48,3072]{2,1,0:T(8,128)} %get-tuple-element.83) | copy-start | bytes 1769476
  255.2 8.0 %copy-start = (f32[1,192,768]{2,1,0:T(8,128)S(1)}, f32[1,192,768]{2,1,0:T(8,128)}, u32[]{:S(2)}) copy-start(f32[1,192,768]{2,1,0:T(8,128)} %get-tuple-element.85) | copy-start | bytes 1769476
  258.3 5.7 %copy-start.4 = (f32[48,384]{1,0:T(8,128)S(1)}, f32[48,384]{1,0:T(8,128)}, u32[]{:S(2)}) copy-start(f32[48,384]{1,0:T(8,128)} %get-tuple-element.86) | copy-start | bytes 221188

commit v4 on v3

--- a/solution.py
+++ b/solution.py
@@ -13,7 +13,7 @@
 MASKED = -1000000000.0
 F32 = jnp.float32
 BF16 = jnp.bfloat16
-VMEM_LIMIT = 63 * 2**20
+VMEM_LIMIT = 127 * 2**19
 
 
 def mm(left, right):
@@ -95,7 +95,8 @@
             outs.append(both[:, :128] / total)
             lses.append(top + jnp.log(total))
         o[l, rows, cols] = jnp.where(lane < 64, outs[0], outs[1]).astype(BF16)
-        lse[l, i, rows, :] = jnp.where(lane < 64, lses[0], lses[1])
+        old = jnp.where(lane == 2 * i, lses[0], lse[l, rows, :])
+        lse[l, rows, :] = jnp.where(lane == 2 * i + 1, lses[1], old)
         return carry
 
     lax.fori_loop(0, pairs, body, 0)
@@ -108,9 +109,9 @@
     return jnp.sum(spread, axis=1, keepdims=True).astype(jnp.int32)
 
 
-def forward_kernel(C, T, D, F, ends, segs, g1, b1, g2, b2, qkv, wo, fc, fcb, proj, shared,
+def forward_kernel(C, m, T, D, F, ends, segs, g1, b1, g2, b2, qkv, wo, fc, fcb, proj, shared,
                    xall_o, q_o, k_o, v_o, o_o, lse_o, r_o, hr_o, hh_o, gp_o, act_o, y_o, yb_o, gy_o, sm_o, watt_o, wfc_o, wproj_o,
-                   kseg_o,
+                   act_in_o, gm_in_o, kseg_o,
                    e, seg, sm, wqk, wv, wout, wfc, wproj, xall, q, k, v, o, lse, r, hr, hh, gp, act, y, yb, wvt, bias,
                    br_s, br_r, ml_s, ml_r, dma):
     core, dp, z = lax.axis_index(SECTION), lax.axis_index(DP), lax.axis_index(CTX)
@@ -124,6 +125,9 @@
     sems = Sems(dma)
     sib = (1 - core, dp, z)
     mirror = (core, dp, C - 1 - z)
+    top_bit = lax.div(dp, 1 << (m - 1))
+    across = (core, dp + (1 - 2 * top_bit) * (1 << (m - 1)), z)
+    owner = top_bit == core
     ahead = [(core, dp, base + lax.rem(z - base + n, N)) for n in range(1, N)]
     behind = [base + lax.rem(z - base + N - n, N) for n in range(1, N)]
     line = [(core, dp, lax.rem(z + n, C)) for n in range(1, C)]
@@ -172,7 +176,7 @@
     sm[core, 3:4, :D] = b2[...]
     sm[core, 4:5, :] = fcb[...]
 
-    greet([sib] + line)
+    greet([sib, across] + line)
 
     own_s, own_r = sems.one(), sems.one()
     own_push = push(ends.at[0, row], e.at[core, row], own_s, own_r, sib)
@@ -392,6 +396,8 @@
         save(hh.at[l], hh_o.at[l])
         save(gp.at[l], gp_o.at[l])
         save(act.at[l], act_o.at[l])
+        if l == 0:
+            when(jnp.logical_not(owner), act_push.start)
         for blk in range(2):
             rows = slice(blk * T, (blk + 1) * T)
             mlps[blk].wait_recv()
@@ -418,20 +424,17 @@
                 yb[rows, :] = out.astype(BF16)
         return sends + mlps
 
+    act_push = push(act.at[0], act_in_o, sems.one(), sems.one(), across)
+    gm_push = push(e.at[1], gm_in_o, sems.one(), sems.one(), across)
     finish_layer_inputs(0)
+
+    @pl.when(core == 1)
+    def _():
+        far_push.start()
+
     for cp in rest_push:
         cp.start()
     pair_sends = middle(0)
-
-    @pl.when(core == 1)
-    def _():
-        far_push.start()
-
-    finish_layer_inputs(1)
-    save(r, r_o)
-    pair_sends += middle(1)
-    save(y, y_o)
-    save(yb, yb_o)
 
     @pl.when(core == 1)
     def _():
@@ -439,11 +442,18 @@
         fwd_push.start()
         e_load.wait()
 
+    finish_layer_inputs(1)
+
     @pl.when(core == 0)
     def _():
         fwd_come.wait_recv()
         own_come.wait_recv()
 
+    when(jnp.logical_not(owner), gm_push.start)
+    save(r, r_o)
+    pair_sends += middle(1)
+    save(y, y_o)
+    save(yb, yb_o)
     save(e.at[1], gy_o)
     save(sm, sm_o)
     for l in range(2):
@@ -453,6 +463,16 @@
         save(wvt.at[l], watt_o.at[l, pl.ds(D + H, H)])
     save(wfc, wfc_o)
     save(wproj, wproj_o)
+    def crossed():
+        act_push.wait_recv()
+        gm_push.wait_recv()
+
+    def crossing():
+        act_push.wait_send()
+        gm_push.wait_send()
+
+    when(owner, crossed)
+    when(jnp.logical_not(owner), crossing)
     far_push.wait_send()
     fwd_push.wait_send()
     own_push.wait_send()
@@ -470,31 +490,66 @@
         cp.wait()
 
 
-def forward_pass(C, ends, segs, g1, b1, g2, b2, qkv, wo, fc, fcb, proj, shared):
+def forward_pass(C, m, ends, segs, g1, b1, g2, b2, qkv, wo, fc, fcb, proj, shared):
     T, D, F = ends.shape[2], ends.shape[3], fc.shape[2]
     N, L, H, FH = C // 2, C * T, D // 2, F // 2
     R, pairs = 2 * T, D // 256
     S = jax.ShapeDtypeStruct
     outs = [S((2, L, D), BF16), S((2, R, H), BF16), S((2, L, H), BF16), S((2, L, H), BF16), S((2, R, H), BF16),
-            S((2, pairs, R, 128), F32), S((2, R, D), BF16), S((2, R, D), F32), S((2, R, D), BF16), S((2, R, FH), BF16),
+            S((2, R, 128), F32), S((2, R, D), BF16), S((2, R, D), F32), S((2, R, D), BF16), S((2, R, FH), BF16),
             S((2, R, FH), BF16), S((R, D), F32), S((R, D), BF16), S((2, T, D), BF16), S((2, 8, F), F32), S((2, 2 * D, D), BF16),
-            S((2, D, FH), BF16), S((2, FH, D), BF16), S((1, L), jnp.int32)]
+            S((2, D, FH), BF16), S((2, FH, D), BF16), S((R, FH), BF16), S((2, T, D), BF16), S((1, L), jnp.int32)]
     V = pltpu.VMEM
     scratch = [V((2, 2, T, D), BF16), V((C, 1, T), jnp.int32), V((2, 8, F), F32), V((2, D, D), BF16), V((2, D, H), BF16),
                V((2, H, D), BF16), V((2, D, FH), BF16), V((2, FH, D), BF16), V((2, L, D), BF16), V((2, R, H), BF16),
-               V((2, L, H), BF16), V((2, L, H), BF16), V((2, R, H), BF16), V((2, pairs, R, 128), F32), V((2, R, D), BF16),
+               V((2, L, H), BF16), V((2, L, H), BF16), V((2, R, H), BF16), V((2, R, 128), F32), V((2, R, D), BF16),
                V((2, R, D), F32), V((2, R, D), BF16), V((2, R, FH), BF16), V((2, R, FH), BF16), V((R, D), F32),
                V((R, D), BF16), V((2, H, D), BF16), V((R, L), F32), V((2, R, D), BF16), V((2, R, D), BF16), V((2, R, D), BF16), V((2, R, D), BF16),
                pltpu.SemaphoreType.DMA((80 + 20 * N + 2 * C,))]
     return pl.pallas_call(
-        functools.partial(forward_kernel, C, T, D, F),
+        functools.partial(forward_kernel, C, m, T, D, F),
         in_specs=[HBM, HBM, VM, VM, VM, VM, HBM, HBM, HBM, VM, HBM, HBM],
-        out_specs=[HBM] * 18 + [VM],
+        out_specs=[HBM] * 20 + [VM],
         out_shape=outs,
         scratch_shapes=scratch,
         compiler_params=pltpu.CompilerParams(collective_id=0, has_side_effects=True, vmem_limit_bytes=VMEM_LIMIT),
         name="forward_pass",
     )(ends, segs, g1, b1, g2, b2, qkv, wo, fc, fcb, proj, shared)
+
+
+WHOLE, SIDED, SIDE_STEP = 0, 1, 2
+JOBS = ("P0", "P1", "P2", "F0", "F1", "F2", "O", "Q", "K", "V")
+POLLS = (
+    (),
+    (),
+    (),
+    (13,),
+    (),
+    (14, 13),
+    (15, 16),
+    (10, 11, 13, 14),
+    (12,),
+    (10, 15, 13, 11),
+    (16, 14),
+    (13,),
+    (),
+    (18, 17, 12, 10, 15, 19, 11),
+    (16, 14, 12, 15),
+    (18, 11, 10, 16),
+    (14, 12),
+    (15, 18, 16),
+    (19, 17, 3),
+    (18, 19, 17, 4, 3, 6),
+    (5,),
+    (0, 4, 18, 19, 17, 1),
+    (3, 5),
+    (2, 0),
+    (4, 19, 17, 3),
+    (6,),
+    (1, 3),
+    (8, 7, 5, 2, 0, 4, 6),
+)
+TAIL = (9, 1, 5, 2, 7, 8, 4, 0, 6, 9, 1, 5, 2, 7, 8, 6, 9, 7, 8, 9, 7, 8, 9)
 
 
 class Job:
@@ -505,7 +560,7 @@
         self.bits = list(range(env.m - 2 if sided else env.m - 1, -1, -1))
         self.fixed, self.z_done, self.steps, self.at = {}, False, [], 0
         self.used = 0
-        if sided:
+        if sided == SIDE_STEP:
             self.steps.append(("side", None, None))
         for item in order:
             if item == "z":
@@ -627,14 +682,13 @@
 def job_table(m):
     xs, ys = list(range(m)), list(range(m - 1, -1, -1))
     rest = list(range(m - 1))
+    xz, yz = xs + ["z"], ys + ["z"]
     return {
-        "P0": ("gproj", (0, 3), rest + ["z"], True), "P1": ("gproj", (1, 3), rest + ["z"], True),
-        "P2": ("gproj", (2, 3), rest + ["z"], True),
-        "F0": ("gfc", (0, 3), xs + ["z"], False), "F1": ("gfc", (1, 3), xs + ["z"], False),
-        "F2": ("gfc", (2, 3), ["z"] + xs, False),
-        "O": ("gout", (0, 1), rest + ["z"], True),
-        "Q": ("gq", (0, 1), xs + ["z"], False), "K": ("gk", (0, 1), ["z"] + xs, False),
-        "V": ("gv", (0, 1), ys + ["z"], False),
+        "P0": ("gproj", (0, 3), ["z"] + rest, SIDED), "P1": ("gproj", (1, 3), rest + ["z"], SIDED),
+        "P2": ("gproj", (2, 3), rest + ["z"], SIDED),
+        "F0": ("gfc", (0, 3), ["z"] + ys, WHOLE), "F1": ("gfc", (1, 3), xz, WHOLE), "F2": ("gfc", (2, 3), xz, WHOLE),
+        "O": ("gout", (0, 1), rest + ["z"], SIDE_STEP),
+        "Q": ("gq", (0, 1), xz, WHOLE), "K": ("gk", (0, 1), yz, WHOLE), "V": ("gv", (0, 1), xz, WHOLE),
     }
 
 
@@ -656,7 +710,7 @@
         tail = [shape[-2], shape[-1]]
         zdim = [C]
         steps = []
-        if sided:
+        if sided == SIDE_STEP:
             steps.append(tuple([2] * n + zdim + tail))
         for item in order:
             if item == "z":
@@ -696,8 +750,8 @@
             qh = jnp.where(sel, q2, jnp.zeros_like(q2))
             goh = jnp.where(sel, go2, jnp.zeros_like(go2))
             delta = jnp.sum(jnp.where(sel, prod, 0.0), axis=-1, keepdims=True)
-            s = mm_nt(qh, k2) + bias[rows, :keys]
-            prob = jnp.exp(s - lse[i, rows, 64 * h : 64 * h + 1])
+            s = mm_nt(qh, k2) + bias[rows, :keys].astype(F32)
+            prob = jnp.exp(s - lse[rows, 2 * i + h : 2 * i + h + 1])
             gp = mm_nt(goh, v2)
             gs = (prob * (gp - delta)).astype(BF16)
             dqs.append(mm(gs, k2))
@@ -755,8 +809,8 @@
         until.append((condition, cp))
         return cp
 
-    load("gy", 1, hbm["gy"].at[0], vm["gm"].at[slice(0, T)])
-    load("gy", 0, hbm["gy"].at[1], vm["gm"].at[slice(T, 2 * T)])
+    load("gy", 1, hbm["gy"].at[0], vm["gm"].at[0])
+    load("gy", 0, hbm["gy"].at[1], vm["gm"].at[1])
     load("wproj", 1, dst=vm["wa"])
     load("gp", 1)
     load("wfc", 1)
@@ -778,11 +832,19 @@
         for n in range(1, C):
             mine = jnp.where(pos(blk) == n, kseg[0:1, n * T : (n + 1) * T], mine)
         allowed = (kpos <= qpos) & (kseg[...] == column(mine))
-        vm["bias"][rows, :] = jnp.where(allowed, 0.0, MASKED)
+        vm["bias"][rows, :] = jnp.where(allowed, 0.0, MASKED).astype(BF16)
 
     greet([sib] + [env.line(lax.rem(z + n, C)) for n in range(1, C)] + [env.dp_xor(b) for b in range(m)])
 
     y_push = pushed(hbm["yb"].at[block(1 - row)], vm["far"], mirror, core == 1)
+    top = env.bit(m - 1) == core
+    aside = jnp.logical_not(top)
+    across = env.dp_xor(m - 1)
+    act_push = pushed(hbm["act"].at[1], vm["act_in"], across, aside)
+    gm_in_load = pltpu.make_async_copy(hbm["gm_in"], vm["gm_in"].at[1], sems.one())
+    act_in_load = pltpu.make_async_copy(hbm["act_in"], vm["act_in"], sems.one())
+    when(top, gm_in_load.start)
+    gm_push = push(vm["gm"], vm["gm_in"].at[0], sems.one(), sems.one(), across)
 
     table = job_table(m)
     jobs = {}
@@ -811,7 +873,13 @@
         shape = vm[buf].shape[1:-1] + (value.shape[-1],)
         vm[buf][(l,) + (slice(None),) * (len(shape) - 1) + (cols,)] = value.astype(BF16).reshape(shape)
 
-    def layer_back(l, poll):
+    polls = iter(POLLS)
+
+    def poll():
+        for code in next(polls):
+            adv(code // 10, JOBS[code % 10])
+
+    def layer_back(l):
         again = []
         need(("wproj", l), ("gp", l))
         bias_sum = None
@@ -819,13 +887,14 @@
             rows = slice(blk * T, (blk + 1) * T)
             if l == 1:
                 need(("gy", 1 - blk))
-                go[rows, :] = gm[rows, :].astype(F32)
-            gu = (gp[rows, :].astype(F32) * mm_nt(gm[rows, :], wa[...])).astype(BF16)
+                go[rows, :] = gm[blk].astype(F32)
+            gu = (gp[rows, :].astype(F32) * mm_nt(gm[blk], wa[...])).astype(BF16)
             gp[rows, :] = gu
             part = jnp.sum(gu.astype(F32), axis=0, keepdims=True)
             bias_sum = part if bias_sum is None else bias_sum + part
         sg[l, 4:5, :] = bias_sum
         load("watt", l, dst=wa)
+        poll()
         need(("wfc", l))
         shares = []
         for blk in range(2):
@@ -833,26 +902,17 @@
             part = mm_nt(gp[rows, :], wfc[...])
             ghh[rows, :] = part
             vm["a_s"][rows, :] = part.astype(BF16)
-            shares.append(pushed(vm["a_s"].at[rows, :], vm["a_r"].at[rows, :], sib, until=again))
+            shares.append(pushed(vm["a_s"].at[rows, :], vm["a_r"].at[rows, :], sib, until=[]))
         if l == 1:
             load("wfc", 0)
-        poll("up")
-        need(("act", l))
-        third = D // 3
-        for i in range(3):
-            cols = slice(i * third, (i + 1) * third)
-            put("gproj", l, cols, mm_tn(vm["act"][...], gm[:, cols]))
-            start("P%d" % i, l)
-        poll("proj")
-        if l == 1:
-            load("act", 0)
+        poll()
         need(("hh", l))
         third = FH // 3
-        for i in (2, 0, 1):
+        for i in (0, 1, 2):
             cols = slice(i * third, (i + 1) * third)
             put("gfc", l, cols, mm_tn(vm["hh"][...], gp[:, cols]))
             start("F%d" % i, l)
-        poll("fc")
+        poll()
         if l == 1:
             load("hh", 0)
             load("gp", 0)
@@ -868,22 +928,46 @@
             total = go[rows, :] + back
             go[rows, :] = total
             low = total.astype(BF16)
-            gm[rows, :] = low
+            vm["gb"][rows, :] = low
             vm["goa"][rows, :] = mm_nt(low, wa[D : D + H, :]).astype(BF16)
             sums = (gain_sum, bias_sum) if sums is None else (sums[0] + gain_sum, sums[1] + bias_sum)
         sg[l, 2:3, :D] = sums[0]
         sg[l, 3:4, :D] = sums[1]
+        poll()
         if l == 1:
             load("hr", 0)
         need(("o", l))
-        put("gout", l, slice(0, D), mm_tn(vm["o"][...], gm[...]))
+        put("gout", l, slice(0, D), mm_tn(vm["o"][...], vm["gb"][...]))
         start("O", l)
-        poll("norm")
+        poll()
         need(("q", l), ("k", l), ("v", l), ("lse", l))
         for i in range(pairs):
             attention_back_pair(i, T, L, vm["q"], vm["k"], vm["v"], vm["o"], vm["lse"], vm["goa"], vm["bias"], vm["dq"],
                                 vm["dk"], vm["dv"], l)
-            poll("pair%d" % i)
+            if i == 0:
+                def proj_grad():
+                    if l == 1:
+                        act_push.wait_recv()
+                        gm_in_load.wait()
+                    else:
+                        act_in_load.wait()
+                        gm_push.wait_recv()
+                    third = D // 3
+                    for n in range(3):
+                        cols = slice(n * third, (n + 1) * third)
+                        total = mm_tn(vm["act_in"][...], vm["gm_in"][l, :, :, cols].reshape(2 * T, third))
+                        for blk in range(2):
+                            total += mm_tn(vm["act"][blk * T : (blk + 1) * T, :], gm[blk, :, cols])
+                        put("gproj", l, cols, total)
+
+                need(("act", l))
+                when(top, proj_grad)
+                for n in range(3):
+                    start("P%d" % n, l)
+                if l == 1:
+                    load("act", 0)
+                    when(top, act_in_load.start)
+            poll()
         if l == 1:
             for name in ("o", "q", "k", "v", "lse"):
                 load(name, 0)
@@ -910,35 +994,40 @@
             dlo = node + row * (C - 1 - 2 * node)
             keep = key_part(dlo + core * (C - 1 - 2 * dlo))
             gives[n].wait_recv()
-            vm["fx_s"][l, n] = (keep + vm["fs_r"][n].astype(F32)).astype(BF16)
-            crossing.append(pushed(vm["fx_s"].at[l, n], vm["fx_r"].at[l, n], (core, dp, node)))
-        poll("cross")
+            vm["fx_s"][n] = (keep + vm["fs_r"][n].astype(F32)).astype(BF16)
+            crossing.append(pushed(vm["fx_s"].at[n], vm["fx_r"].at[l, n], (core, dp, node), until=again))
+        poll()
         for blk in range(2):
             rows = slice(blk * T, (blk + 1) * T)
             ghh[rows, :] = key_part(pos(blk)) + mm_nt(dq[rows, :], wa[:D, :H])
+        for cp in shares:
+            cp.wait_send()
         early = pl.ds(pl.multiple_of((1 - core) * T, T), T)
         late = pl.ds(pl.multiple_of(core * T, T), T)
-        vm["b_s"][early, :] = ghh[early, :].astype(BF16)
-        shares = [pushed(vm["b_s"].at[early, :], vm["b_r"].at[early, :], sib, until=again)]
+        vm["a_s"][early, :] = ghh[early, :].astype(BF16)
+        shares = [pushed(vm["a_s"].at[early, :], vm["b_r"].at[early, :], sib, until=again)]
         if l == 1:
             load("wproj", 0, dst=wa)
+        poll()
         need(("xall", l))
         xall = vm["xall"]
         put("gk", l, slice(0, H), mm_tn(xall[...], dk[...]))
         start("K", l)
+        poll()
         put("gq", l, slice(0, H), mm_tn(xall[block(lo), :], dq[:T, :]) + mm_tn(xall[block(hi), :], dq[T:, :]))
         start("Q", l)
+        poll()
         put("gv", l, slice(0, H), mm_tn(xall[...], dv[l]))
         start("V", l)
-        poll("qkv")
+        poll()
         if l == 1:
             load("xall", 0)
         need(("r", l))
         for n in range(N - 1):
             crossing[n].wait_recv()
             ghh[late, :] += vm["fx_r"][l, n].astype(F32)
-        vm["b_s"][late, :] = ghh[late, :].astype(BF16)
-        shares.append(pushed(vm["b_s"].at[late, :], vm["b_r"].at[late, :], sib, until=again))
+        vm["a_s"][late, :] = ghh[late, :].astype(BF16)
+        shares.append(pushed(vm["a_s"].at[late, :], vm["b_r"].at[late, :], sib, until=again))
         for cp in shares:
             cp.wait_recv()
         sums = None
@@ -949,46 +1038,25 @@
             total = go[rows, :] + back
             go[rows, :] = total
             if l == 1:
-                gm[rows, :] = total.astype(BF16)
+                gm[blk] = total.astype(BF16)
             sums = (gain_sum, bias_sum) if sums is None else (sums[0] + gain_sum, sums[1] + bias_sum)
         sg[l, 0:1, :D] = sums[0]
         sg[l, 1:2, :D] = sums[1]
+        poll()
         if l == 1:
             load("r", 0)
+            when(aside, gm_push.start)
+            sent.append((aside, gm_push))
         for condition, cp in again:
             when(condition, cp.wait_send)
 
-    def poll_first(where):
-        plan = {
-            "norm": ["F2"], "pair0": ["F2"], "pair2": ["F2"], "cross": ["F0", "F1", "F2"], "qkv": ["F2"],
-        }
-        adv(1, *plan.get(where, []))
-
-    def poll_second(where):
-        plan = {
-            "up": ["P0", "P1", "P2", "K", "F0", "F1"],
-            "proj": ["F0", "F1", "K", "O"],
-            "fc": ["F0", "F1", "K", "Q", "V", "P0", "P1", "P2"],
-            "norm": ["F0", "F1", "K", "Q", "V", "O"],
-            "pair0": ["P0", "P1", "P2", "K", "Q", "V", "O"],
-            "pair1": ["P0", "P1", "P2", "Q", "V", "O"],
-            "pair2": ["P0", "P1", "P2", "Q", "V", "O"],
-        }
-        adv(1, *plan.get(where, []))
-        if where in ("pair0", "pair1", "pair2"):
-            adv(0, "F2")
-        if where == "cross":
-            adv(0, "F0", "F1", "F2")
-        if where == "qkv":
-            adv(0, "F2", "F0", "F1")
-
-    layer_back(1, poll_first)
-    layer_back(0, poll_second)
+    layer_back(1)
+    layer_back(0)
 
     keep = pl.ds(pl.multiple_of(row * T, T), T)
     away = pl.ds(pl.multiple_of((1 - row) * T, T), T)
-    vm["far_s"][...] = go[away, :].astype(BF16)
-    x_push = pushed(vm["far_s"], vm["far"], mirror, core == 0)
+    vm["gb"][:T, :] = go[away, :].astype(BF16)
+    x_push = pushed(vm["gb"].at[pl.ds(0, T), :], vm["far"], mirror, core == 0)
     x_keep = pltpu.make_async_copy(go.at[keep, :], ends_o.at[0, row], sems.one())
     when(core == 0, x_keep.start)
 
@@ -1016,22 +1084,21 @@
     def finish_ends():
         when(core == 0, x_push.wait_recv)
         when(core == 1, y_push.wait_recv)
-        vm["far_f"][...] = vm["far"][...].astype(F32)
-        far_keep = pltpu.make_async_copy(vm["far_f"], ends_o.at[0, 1 - row], sems.one())
+        vm["ghh"][:T, :] = vm["far"][...].astype(F32)
+        far_keep = pltpu.make_async_copy(vm["ghh"].at[pl.ds(0, T), :], ends_o.at[0, 1 - row], sems.one())
         far_keep.start()
         far_keep.wait()
         when(core == 0, x_keep.wait)
         when(core == 1, y_keep.wait)
 
     if fused:
-        for name in ("P0", "F0", "P1", "F1", "P2", "F2", "K", "O", "Q", "V"):
-            for _ in range(len(jobs[(name, 1)].steps)):
-                adv(1, name)
-        order = ["F0", "F1", "F2", "K", "P0", "P1", "P2", "Q", "O", "V"]
-        while any(jobs[(name, 0)].at < len(jobs[(name, 0)].steps) for name in order):
-            adv(0, *order)
-            if small_at[0] < len(around):
+        for at, code in enumerate(TAIL):
+            adv(code // 10, JOBS[code % 10])
+            if at % 4 == 3 and small_at[0] < len(around):
                 small_step()
+        for job in jobs.values():
+            for _ in range(len(job.steps) - job.at):
+                job.advance()
     while small_at[0] < len(around):
         small_step()
     last = len(around)
@@ -1126,14 +1193,14 @@
         grads, land = flat, {}
     stages = m + C.bit_length() - 1
     vm = dict(
-        gm=V((R, D), BF16), gp=V((R, FH), BF16), act=V((R, FH), BF16), hh=V((R, D), BF16), hr=V((R, D), F32),
-        o=V((R, H), BF16), q=V((R, H), BF16), k=V((L, H), BF16), v=V((L, H), BF16), lse=V((pairs, R, 128), F32),
-        xall=V((L, D), BF16), r=V((R, D), BF16), sm=V((2, 8, F), F32), sg=V((2, 8, FH), F32), bias=V((R, L), F32),
+        gm=V((2, T, D), BF16), gb=V((R, D), BF16), gm_in=V((2, 2, T, D), BF16), act_in=V((R, FH), BF16), gp=V((R, FH), BF16), act=V((R, FH), BF16), hh=V((R, D), BF16), hr=V((R, D), F32),
+        o=V((R, H), BF16), q=V((R, H), BF16), k=V((L, H), BF16), v=V((L, H), BF16), lse=V((R, 128), F32),
+        xall=V((L, D), BF16), r=V((R, D), BF16), sm=V((2, 8, F), F32), sg=V((2, 8, FH), F32), bias=V((R, L), BF16),
         wa=V((2 * D, D), BF16), wfc=V((D, FH), BF16), go=V((R, D), F32), ghh=V((R, D), F32), a_s=V((R, D), BF16),
-        a_r=V((R, D), BF16), b_s=V((R, D), BF16), b_r=V((R, D), BF16), goa=V((R, H), BF16), dq=V((R, H), BF16),
+        a_r=V((R, D), BF16), b_r=V((R, D), BF16), goa=V((R, H), BF16), dq=V((R, H), BF16),
         dk=V((L, H), BF16), dv=V((2, L, H), BF16), fs_s=V((N - 1, T, D), BF16), fs_r=V((N - 1, T, D), BF16),
-        fx_s=V((2, N - 1, T, D), BF16), fx_r=V((2, N - 1, T, D), BF16), far=V((T, D), BF16), far_s=V((T, D), BF16),
-        far_f=V((T, D), F32), sv=V((stages + 1, 8, FH), F32), sv_r=V((stages, 8, FH), F32), fb_s=V((1, FH), F32),
+        fx_s=V((N - 1, T, D), BF16), fx_r=V((2, N - 1, T, D), BF16), far=V((T, D), BF16),
+        sv=V((stages + 1, 8, FH), F32), sv_r=V((stages, 8, FH), F32), fb_s=V((1, FH), F32),
         fin=dict(fc=V((D // J, FH), BF16), q=V((D // J, H), BF16), k=V((D // J, H), BF16), v=V((D // J, H), BF16),
                  out=V((D // J, D), BF16), proj=V((F // J, D), BF16), fb=V((1, FH), F32)),
         land=land, **{name: V((2,) + shape, BF16) for name, shape in grads.items()})
@@ -1190,9 +1257,9 @@
     micros, T, D = ends.shape[1:]
     F = fc_weight.shape[2]
     half, FH = D // 2, F // 2
-    names = ("xall", "q", "k", "v", "o", "lse", "r", "hr", "hh", "gp", "act", "y", "yb", "gy", "sm", "watt", "wfc", "wproj", "kseg")
+    names = ("xall", "q", "k", "v", "o", "lse", "r", "hr", "hh", "gp", "act", "y", "yb", "gy", "sm", "watt", "wfc", "wproj", "act_in", "gm_in", "kseg")
     kept = dict(zip(names, forward_pass(
-        C, ends, segment_ids.reshape(micros, 1, T), ln1_gain, ln1_bias, ln2_gain, ln2_bias, qkv_weight, out_weight,
+        C, m, ends, segment_ids.reshape(micros, 1, T), ln1_gain, ln1_bias, ln2_gain, ln2_bias, qkv_weight, out_weight,
         fc_weight, fc_bias, proj_weight, shared_weight)))
     block, small, *grads = backward_pass(C, m, T, D, F, kept)
     if len(grads) == 5:
@@ -1225,7 +1292,8 @@
     res = []
     for l in range(2):
         qkv = jnp.concatenate([gq[l], gk[l], gv[l]], axis=1)
-        res.append((scatter_sum(qkv, x_first), sided(gout[l]), scatter_sum(gfc[l], x_first), sided(gproj[l])))
+        res.append((scatter_sum(qkv, x_first), sided(gout[l]), scatter_sum(gfc[l], x_first),
+                    scatter_sum(gproj[l], y_first[1:], skip_first=True)))
     holder = jnp.where(lax.axis_index(DP) >= lax.axis_size(DP) // 2, 1, 0) == core
     mine = tuple(jnp.where(first, a, b) for a, b in zip(res[0], res[1]))
     got = tuple(swap(jnp.where(first, b, a)) for a, b in zip(res[0], res[1]))

time: 269 us -> 229 us (0.85)
  Pallas kernels: 253 us -> 213 us
    pallas_call x1, Pallas kernels: 180 us -> 139 us  [backward_pass(): pl.pallas_call(functools.partial(backward_kernel, C, m, T, D, F, fused, n...]
where the time goes in v4:
time: 229 us; the launch traced here: 225 us
  Pallas kernels  213 us (93%)
  local copies, waits for them, and re-layouts  9.03 us (4%)
    pallas_call x1, Pallas kernels, backward_pass(): pl.pallas_call(functools.partial(backward_kernel, C, m, T, D, F, fused, n...  139 us
    pallas_call x1, Pallas kernels, forward_pass(): pl.pallas_call(functools.partial(forward_kernel, C, m, T, D, F), in_specs...  74.5 us
    unnamed x16, local copies, waits for them, and re-layouts  6.37 us

profile of v4, /device:TPU:1, one launch (start us, length us, event | category | flops | bytes accessed | tf_op | source)
XLA Modules:
  0.0 225.0 jit_solution(9381518459187953581)
XLA Ops:
  0.6 1.3 reshape.31.segs
  1.9 74.5 %forward_pass.1 = (bf16[2,1024,768]{2,1,0:T(8,128)(2,1)}, bf16[2,512,384]{2,1,0:T(8,128)(2,1)}, bf16[2,1024,384]{2,1,0:T(8,128)(2,1)}, bf16[2,1024,384]{2,1,0:T(...) custom-call(bf16[1,2,256,768]{3,2,1,0:T(8,128)(2,1)} %ends.1, ...), custom_call_target="tpu_custom_call" | custom-call | tf_op jit(solution)/shard_map/forward_pass/pallas_call | solution.py:509
  76.4 139.0 %backward_pass.1 = (f32[1,2,256,768]{3,2,1,0:T(8,128)}, f32[8,1536]{1,0:T(8,128)}, f32[1,48,1920]{2,1,0:T(8,128)}, f32[1,48,768]{2,1,0:T(8,128)}, f32[1,48,3072]...) custom-call(bf16[2,1024,768]{2,1,0:T(8,128)(2,1)} %get-tuple-element.39.refs_0_, ...), custom_call_target="tpu_custom_call" | custom-call | tf_op jit(solution)/shard_map/backward_pass/pallas_call | solution.py:1210
  215.4 0.0 copy-start.2
  215.4 0.0 copy-start.3
  215.4 0.0 copy-start.1
  215.4 0.0 copy-start
  215.4 1.0 fusion.1
  216.4 0.7 fusion.2
  217.1 0.8 slice.27
  217.9 0.1 constant_dynamic-slice_fusion
  218.0 0.5 fusion.3
  218.5 0.0 copy-start.4
  218.5 2.7 %copy.29 = f32[1,2,256,768]{3,2,1,0:T(8,128)} copy(f32[1,2,256,768]{3,2,1,0:T(8,128)} %get-tuple-element.84) | data formatting | bytes 3145728
  221.2 0.0 copy-done.2
  221.2 0.7 copy.30
  221.9 0.0 copy-done.3
  221.9 0.7 copy.31
  222.6 0.0 copy-done.1
  222.6 0.8 copy.32
  223.4 0.0 copy-done
  223.4 0.8 copy.33
  224.2 0.0 copy-done.4
  224.2 0.6 copy.34
Async XLA Ops:
  215.4 5.8 %copy-start.2 = (f32[1,48,1920]{2,1,0:T(8,128)S(1)}, f32[1,48,1920]{2,1,0:T(8,128)}, u32[]{:S(2)}) copy-start(f32[1,48,1920]{2,1,0:T(8,128)} %get-tuple-element.85) | copy-start | bytes 1105924
  215.4 6.5 %copy-start.3 = (f32[1,48,768]{2,1,0:T(8,128)S(1)}, f32[1,48,768]{2,1,0:T(8,128)}, u32[]{:S(2)}) copy-start(f32[1,48,768]{2,1,0:T(8,128)} %get-tuple-element.86) | copy-start | bytes 442372
  215.4 7.2 %copy-start.1 = (f32[1,48,3072]{2,1,0:T(8,128)S(1)}, f32[1,48,3072]{2,1,0:T(8,128)}, u32[]{:S(2)}) copy-start(f32[1,48,3072]{2,1,0:T(8,128)} %get-tuple-element.87) | copy-start | bytes 1769476
  215.4 8.0 %copy-start = (f32[1,192,768]{2,1,0:T(8,128)S(1)}, f32[1,192,768]{2,1,0:T(8,128)}, u32[]{:S(2)}) copy-start(f32[1,192,768]{2,1,0:T(8,128)} %get-tuple-element.89) | copy-start | bytes 1769476
  218.5 5.7 %copy-start.4 = (f32[48,384]{1,0:T(8,128)S(1)}, f32[48,384]{1,0:T(8,128)}, u32[]{:S(2)}) copy-start(f32[48,384]{1,0:T(8,128)} %get-tuple-element.90) | copy-start | bytes 221188

commit v5 on v4

--- a/solution.py
+++ b/solution.py
@@ -112,7 +112,7 @@
 def forward_kernel(C, m, T, D, F, ends, segs, g1, b1, g2, b2, qkv, wo, fc, fcb, proj, shared,
                    xall_o, q_o, k_o, v_o, o_o, lse_o, r_o, hr_o, hh_o, gp_o, act_o, y_o, yb_o, gy_o, sm_o, watt_o, wfc_o, wproj_o,
                    act_in_o, gm_in_o, kseg_o,
-                   e, seg, sm, wqk, wv, wout, wfc, wproj, xall, q, k, v, o, lse, r, hr, hh, gp, act, y, yb, wvt, bias,
+                   e, seg, segv, sm, wqk, wv, wout, wfc, wproj, xall, q, k, v, o, lse, r, hr, hh, gp, act, y, yb, wvt, bias,
                    br_s, br_r, ml_s, ml_r, dma):
     core, dp, z = lax.axis_index(SECTION), lax.axis_index(DP), lax.axis_index(CTX)
     N, L, H, FH = C // 2, C * T, D // 2, F // 2
@@ -167,8 +167,9 @@
     def _():
         v_fresh.start()
 
-    seg_load = pltpu.make_async_copy(segs.at[row], seg.at[z], sems.one())
-    seg_load.start()
+    segv[0] = segs[0:1, :]
+    segv[1] = segs[1:2, :]
+    seg[z] = segv[row]
     sm[core] = jnp.zeros_like(sm[core])
     sm[core, 0:1, :D] = g1[...]
     sm[core, 1:2, :D] = b1[...]
@@ -181,26 +182,30 @@
     own_s, own_r = sems.one(), sems.one()
     own_push = push(ends.at[0, row], e.at[core, row], own_s, own_r, sib)
     own_come = push(ends.at[0, row], e.at[1 - core, row], own_s, own_r, sib)
-    far_s, far_r = sems.one(), sems.one()
-    far_push = push(ends.at[0, 1 - row], e.at[core, row], far_s, far_r, mirror)
-    far_come = push(ends.at[0, 1 - row], e.at[core, 1 - row], far_s, far_r, mirror)
-    fwd_s, fwd_r = sems.one(), sems.one()
-    fwd_push = push(e.at[core, 1 - row], e.at[core, 1 - row], fwd_s, fwd_r, sib)
-    fwd_come = push(e.at[1 - core, 1 - row], e.at[1 - core, 1 - row], fwd_s, fwd_r, sib)
+    seg_push = []
+    for n in range(1, C):
+        to = lax.rem(z + n, C)
+        cp = push(segv.at[lax.div(to, N)], seg.at[z], sems.one(), sems.one(), line[n - 1])
+        cp.start()
+        seg_push.append(cp)
+    far_push, far_come, fwd_push, fwd_come = [], [], [], []
+    for h in range(2):
+        part = pl.ds(h * T2, T2)
+        far_s, far_r, fwd_s, fwd_r = sems.one(), sems.one(), sems.one(), sems.one()
+        far_push.append(push(ends.at[0, 1 - row, part], e.at[core, row, part], far_s, far_r, mirror))
+        far_come.append(push(ends.at[0, 1 - row, part], e.at[core, 1 - row, part], far_s, far_r, mirror))
+        here, there = e.at[core, 1 - row, part], e.at[1 - core, 1 - row, part]
+        fwd_push.append(push(here, here, fwd_s, fwd_r, sib))
+        fwd_come.append(push(there, there, fwd_s, fwd_r, sib))
 
     @pl.when(core == 0)
     def _():
-        far_push.start()
+        for cp in far_push:
+            cp.start()
 
     own_push.start()
     sm_push = push(sm.at[core], sm.at[core], sems.one(), sems.one(), sib)
     sm_push.start()
-    seg_push = []
-    for n in range(1, C):
-        to = lax.rem(z + n, C)
-        cp = push(segs.at[to // N], seg.at[z], sems.one(), sems.one(), line[n - 1])
-        cp.start()
-        seg_push.append(cp)
     qk_push = [
         push(qkv.at[0, :, qo], wqk.at[core, :, pl.ds(0, H)], sems.one(), sems.one(), sib),
         push(qkv.at[0, :, ko], wqk.at[core, :, pl.ds(H, H)], sems.one(), sems.one(), sib),
@@ -219,7 +224,108 @@
         push(proj.at[0, pl.ds(pl.multiple_of((1 - core) * FH, FH), FH), :], wproj.at[core], sems.one(), sems.one(), sib),
     ]
 
-    seg_load.wait()
+    xh_sends = {}
+
+    def route_block(l, turn, blk):
+        p = pos(blk)
+        for n in range(N - 1):
+            part = xall.at[l, pl.ds(pl.multiple_of(p * T + core * T2, T2), T2), :]
+            s, rsem = sems.one(), sems.one()
+            cp = push(part, part, s, rsem, ahead[n])
+            src = behind[n]
+            slo = src + row * (C - 1 - 2 * src)
+            sp = slo + blk * (C - 1 - 2 * slo)
+            got = xall.at[l, pl.ds(pl.multiple_of(sp * T + core * T2, T2), T2), :]
+            other = xall.at[l, pl.ds(pl.multiple_of(sp * T + (1 - core) * T2, T2), T2), :]
+            come = push(got, got, s, rsem, ahead[n])
+            fs, fr = sems.one(), sems.one()
+            onward = push(got, got, fs, fr, sib)
+            arrive = push(other, other, fs, fr, sib)
+            xh_sends[(l, turn, n)] = (cp, come, onward, arrive, sp)
+
+    def leave(l, turn):
+        for n in range(N - 1):
+            xh_sends[(l, turn, n)][0].start()
+
+    def normed_block(l, turn, blk, values):
+        xall[l, rows_at(pos(blk)), :] = layer_norm(values, sm[l, 0:1, :D], sm[l, 1:2, :D]).astype(BF16)
+        route_block(l, turn, blk)
+        leave(l, turn)
+
+    def own_products(l, blk):
+        p = pos(blk)
+        xh = xall[l, rows_at(p), :]
+        both = mm(xh, wqk[l])
+        q[l, blk * T : (blk + 1) * T, :] = both[:, :H].astype(BF16)
+        k[l, rows_at(p), :] = both[:, H:].astype(BF16)
+
+    def value_products(l, p):
+        src = l * core
+        v[l, rows_at(p), :] = mm(xall[src, rows_at(p), :], wv[src]).astype(BF16)
+
+    def key_products(l, p):
+        k[l, rows_at(p), :] = mm(xall[l, rows_at(p), :], wqk[l, :, H:]).astype(BF16)
+
+    def arrivals(l, turn):
+        for n in range(N - 1):
+            cp, come, onward, arrive, sp = xh_sends[(l, turn, n)]
+            come.wait_recv()
+            onward.start()
+
+    def foreign_products(l, turn):
+        for n in range(N - 1):
+            cp, come, onward, arrive, sp = xh_sends[(l, turn, n)]
+            arrive.wait_recv()
+            key_products(l, sp)
+            value_products(l, sp)
+
+    act_push = [push(act.at[0, pl.ds(b * T, T), :], act_in_o.at[pl.ds(b * T, T), :], sems.one(), sems.one(), across) for b in range(2)]
+    gm_push = [push(e.at[1, b], gm_in_o.at[b], sems.one(), sems.one(), across) for b in (row, 1 - row)]
+
+    @pl.when(core == 0)
+    def _():
+        e_load.wait()
+
+    @pl.when(core == 1)
+    def _():
+        own_come.wait_recv()
+
+    sm_push.wait()
+    blk = row
+    r[0, pl.ds(pl.multiple_of(blk * T, T), T), :] = e[0, blk]
+    normed_block(0, 0, blk, e[0, blk].astype(F32))
+
+    @pl.when(core == 0)
+    def _():
+        loads[0].wait()
+        loads[1].wait()
+        v_shared.wait()
+
+    @pl.when(core == 1)
+    def _():
+        for cp in qk_push:
+            cp.wait_recv()
+        v_push.wait_recv()
+
+    def own_products_dynamic(l, blk):
+        p = pos(blk)
+        both = mm(xall[l, rows_at(p), :], wqk[l])
+        q[l, pl.ds(pl.multiple_of(blk * T, T), T), :] = both[:, :H].astype(BF16)
+        k[l, rows_at(p), :] = both[:, H:].astype(BF16)
+        value_products(l, p)
+
+    own_products_dynamic(0, blk)
+
+    @pl.when(core == 1)
+    def _():
+        e_load.wait()
+
+    @pl.when(core == 0)
+    def _():
+        own_come.wait_recv()
+
+    when(jnp.logical_not(owner), gm_push[0].start)
+
     for n, cp in enumerate(seg_push):
         cp.wait()
     kseg = jnp.concatenate([seg[n] for n in range(C)], axis=1)
@@ -231,252 +337,183 @@
         allowed = (kpos <= qpos) & (kseg == column(seg[pos(blk)]))
         bias[rows, :] = jnp.where(allowed, 0.0, MASKED)
 
-    xh_sends = {}
-
-    def normed_block(l, turn, blk, values):
-        p = pos(blk)
-        xall[l, rows_at(p), :] = layer_norm(values, sm[l, 0:1, :D], sm[l, 1:2, :D]).astype(BF16)
-        for n in range(N - 1):
-            part = xall.at[l, pl.ds(pl.multiple_of(p * T + core * T2, T2), T2), :]
-            s, rsem = sems.one(), sems.one()
-            cp = push(part, part, s, rsem, ahead[n])
-            cp.start()
-            src = behind[n]
-            slo = src + row * (C - 1 - 2 * src)
-            sp = slo + blk * (C - 1 - 2 * slo)
-            got = xall.at[l, pl.ds(pl.multiple_of(sp * T + core * T2, T2), T2), :]
-            other = xall.at[l, pl.ds(pl.multiple_of(sp * T + (1 - core) * T2, T2), T2), :]
-            come = push(got, got, s, rsem, ahead[n])
-            fs, fr = sems.one(), sems.one()
-            onward = push(got, got, fs, fr, sib)
-            arrive = push(other, other, fs, fr, sib)
-            xh_sends[(l, turn, n)] = (cp, come, onward, arrive, sp)
-
-    def own_products(l, blk):
-        p = pos(blk)
-        xh = xall[l, rows_at(p), :]
-        both = mm(xh, wqk[l])
-        q[l, blk * T : (blk + 1) * T, :] = both[:, :H].astype(BF16)
-        k[l, rows_at(p), :] = both[:, H:].astype(BF16)
-
-    def value_products(l, p):
-        src = l * core
-        v[l, rows_at(p), :] = mm(xall[src, rows_at(p), :], wv[src]).astype(BF16)
-
-    def key_products(l, p):
-        k[l, rows_at(p), :] = mm(xall[l, rows_at(p), :], wqk[l, :, H:]).astype(BF16)
-
-    @pl.when(core == 0)
-    def _():
-        e_load.wait()
+    blk = 1 - row
+
+    route_block(0, 1, blk)
+    for h in range(2):
+        @pl.when(core == 0)
+        def _():
+            far_come[h].wait_recv()
+            fwd_push[h].start()
+
+        @pl.when(core == 1)
+        def _():
+            fwd_come[h].wait_recv()
+
+        values = e[0, blk, h * T2 : (h + 1) * T2, :]
+        r[0, pl.ds(pl.multiple_of(blk * T + h * T2, T2), T2), :] = values
+        xall[0, pl.ds(pl.multiple_of(pos(blk) * T + h * T2, T2), T2), :] = layer_norm(
+            values.astype(F32), sm[0, 0:1, :D], sm[0, 1:2, :D]).astype(BF16)
+
+        @pl.when(core == h)
+        def _():
+            leave(0, 1)
 
     @pl.when(core == 1)
     def _():
-        own_come.wait_recv()
-
-    sm_push.wait()
-    blk = row
-    r[0, pl.ds(pl.multiple_of(blk * T, T), T), :] = e[0, blk]
-    normed_block(0, 0, blk, e[0, blk].astype(F32))
-
-    @pl.when(core == 0)
-    def _():
-        loads[0].wait()
-        loads[1].wait()
-        v_shared.wait()
-
-    @pl.when(core == 1)
-    def _():
-        for cp in qk_push:
-            cp.wait_recv()
-        v_push.wait_recv()
-
-    def own_products_dynamic(l, blk):
-        p = pos(blk)
-        both = mm(xall[l, rows_at(p), :], wqk[l])
-        q[l, pl.ds(pl.multiple_of(blk * T, T), T), :] = both[:, :H].astype(BF16)
-        k[l, rows_at(p), :] = both[:, H:].astype(BF16)
-        value_products(l, p)
+        for cp in far_push:
+            cp.start()
 
     own_products_dynamic(0, blk)
-    blk = 1 - row
-
-    @pl.when(core == 0)
-    def _():
-        far_come.wait_recv()
-        fwd_push.start()
-
-    @pl.when(core == 1)
-    def _():
-        fwd_come.wait_recv()
-
-    r[0, pl.ds(pl.multiple_of(blk * T, T), T), :] = e[0, blk]
-    normed_block(0, 1, blk, e[0, blk].astype(F32))
-    own_products_dynamic(0, blk)
-
-    def finish_layer_inputs(l):
-        for turn in range(2):
-            for n in range(N - 1):
-                cp, come, onward, arrive, sp = xh_sends[(l, turn, n)]
-                come.wait_recv()
-                onward.start()
-        for turn in range(2):
-            for n in range(N - 1):
-                cp, come, onward, arrive, sp = xh_sends[(l, turn, n)]
-                arrive.wait_recv()
-                key_products(l, sp)
-                value_products(l, sp)
+
+    def at_core(here, ours, theirs):
+        @pl.when(here)
+        def _():
+            for cp in ours:
+                cp.wait()
+
+        @pl.when(jnp.logical_not(here))
+        def _():
+            for cp in theirs:
+                cp.wait_recv()
+
+    def branch(l, blk):
+        rows = slice(blk * T, (blk + 1) * T)
+        part = mm(o[l, rows, :], wout[l])
+        hr[l, rows, :] = part
+        br_s[l, rows, :] = part.astype(BF16)
+        cp = push(br_s.at[l, rows, :], br_r.at[l, rows, :], sems.one(), sems.one(), sib)
+        cp.start()
+        return cp
+
+    def hidden_units(l, blk, come):
+        rows = slice(blk * T, (blk + 1) * T)
+        come.wait_recv()
+        hidden = r[l, rows, :].astype(F32) + hr[l, rows, :] + br_r[l, rows, :].astype(F32)
+        hr[l, rows, :] = hidden
+        normed2 = layer_norm(hidden, sm[l, 2:3, :D], sm[l, 3:4, :D]).astype(BF16)
+        hh[l, rows, :] = normed2
+        if l == 0 and blk == 0:
+            at_core(core == 0, loads[3:5], rest_push[1:3])
+        mine = pl.ds(pl.multiple_of(core * FH, 128), FH)
+        u = mm(normed2, wfc[l]) + sm[l, 4:5, mine]
+        a, slope = gelu_both(u)
+        gp[l, rows, :] = slope.astype(BF16)
+        act[l, rows, :] = a.astype(BF16)
+        if l == 0:
+            when(jnp.logical_not(owner), act_push[blk].start)
+
+    def feed_out(l, blk):
+        rows = slice(blk * T, (blk + 1) * T)
+        part = mm(act[l, rows, :], wproj[l])
+        y[rows, :] = part
+        ml_s[l, rows, :] = part.astype(BF16)
+        cp = push(ml_s.at[l, rows, :], ml_r.at[l, rows, :], sems.one(), sems.one(), sib)
+        cp.start()
+        return cp
+
+    def block_out(l, blk, come):
+        rows = slice(blk * T, (blk + 1) * T)
+        come.wait_recv()
+        out = hr[l, rows, :] + y[rows, :] + ml_r[l, rows, :].astype(F32)
+        if l == 0:
+            sent = out.astype(BF16)
+            r[1, rows, :] = sent
+            normed_block(1, blk, blk, sent.astype(F32))
+        else:
+            y[rows, :] = out
+            yb[rows, :] = out.astype(BF16)
+
+    def save_weights(l):
+        wvt[l] = jnp.transpose(wv[l * core])
+        save(wqk.at[l], watt_o.at[l, pl.ds(0, D)])
+        save(wout.at[l], watt_o.at[l, pl.ds(D, H)])
+        save(wvt.at[l], watt_o.at[l, pl.ds(D + H, H)])
+        save(wfc.at[l], wfc_o.at[l])
+        save(wproj.at[l], wproj_o.at[l])
 
     def middle(l):
-        sends = []
-        for blk in range(2):
-            rows = slice(blk * T, (blk + 1) * T)
-            attention_block(l, blk, T, L // 2 if blk == 0 else L, pairs, q, k, v, o, lse, bias)
-            if l == 0 and blk == 0:
-                @pl.when(core == 0)
-                def _():
-                    loads[2].wait()
-
-                @pl.when(core == 1)
-                def _():
-                    rest_push[0].wait_recv()
-            if l == 1 and blk == 0:
-                @pl.when(core == 1)
-                def _():
-                    loads[2].wait()
-
-                @pl.when(core == 0)
-                def _():
-                    rest_push[0].wait_recv()
-            part = mm(o[l, rows, :], wout[l])
-            hr[l, rows, :] = part
-            br_s[l, rows, :] = part.astype(BF16)
-            cp = push(br_s.at[l, rows, :], br_r.at[l, rows, :], sems.one(), sems.one(), sib)
-            cp.start()
-            sends.append(cp)
+        attention_block(l, 0, T, L // 2, pairs, q, k, v, o, lse, bias)
+        if l == 0:
+            at_core(core == 0, loads[2:3], rest_push[0:1])
+        else:
+            arrivals(1, 1)
+        sends = [branch(l, 0)]
+        if l == 1:
+            foreign_products(1, 1)
+        if l == 0:
+            @pl.when(core == 1)
+            def _():
+                for h in range(2):
+                    far_come[h].wait_recv()
+                    fwd_push[h].start()
+        attention_block(l, 1, T, L, pairs, q, k, v, o, lse, bias)
+        sends.append(branch(l, 1))
+        if l == 0:
+            @pl.when(core == 0)
+            def _():
+                for cp in fwd_come:
+                    cp.wait_recv()
+
+            when(jnp.logical_not(owner), gm_push[1].start)
         save(q.at[l], q_o.at[l])
         save(k.at[l], k_o.at[l])
         save(v.at[l], v_o.at[l])
         save(o.at[l], o_o.at[l])
         save(lse.at[l], lse_o.at[l])
         save(xall.at[l], xall_o.at[l])
-        mlps = []
-        for blk in range(2):
-            rows = slice(blk * T, (blk + 1) * T)
-            sends[blk].wait_recv()
-            hidden = r[l, rows, :].astype(F32) + hr[l, rows, :] + br_r[l, rows, :].astype(F32)
-            hr[l, rows, :] = hidden
-            normed2 = layer_norm(hidden, sm[l, 2:3, :D], sm[l, 3:4, :D]).astype(BF16)
-            hh[l, rows, :] = normed2
-            if blk == 0:
-                local = core == l
-
-                @pl.when(local)
-                def _():
-                    loads[3].wait()
-                    loads[4].wait()
-
-                @pl.when(jnp.logical_not(local))
-                def _():
-                    rest_push[1].wait_recv()
-                    rest_push[2].wait_recv()
-            mine = pl.ds(pl.multiple_of(core * FH, 128), FH)
-            u = mm(normed2, wfc[l]) + sm[l, 4:5, mine]
-            a, slope = gelu_both(u)
-            a = a.astype(BF16)
-            gp[l, rows, :] = slope.astype(BF16)
-            act[l, rows, :] = a
-            part = mm(a, wproj[l])
-            y[rows, :] = part
-            ml_s[l, rows, :] = part.astype(BF16)
-            cp = push(ml_s.at[l, rows, :], ml_r.at[l, rows, :], sems.one(), sems.one(), sib)
-            cp.start()
-            mlps.append(cp)
+        hidden_units(l, 0, sends[0])
+        mlps = [feed_out(l, 0)]
+        hidden_units(l, 1, sends[1])
         save(hr.at[l], hr_o.at[l])
         save(hh.at[l], hh_o.at[l])
         save(gp.at[l], gp_o.at[l])
         save(act.at[l], act_o.at[l])
+        block_out(l, 0, mlps[0])
+        mlps.append(feed_out(l, 1))
         if l == 0:
-            when(jnp.logical_not(owner), act_push.start)
-        for blk in range(2):
-            rows = slice(blk * T, (blk + 1) * T)
-            mlps[blk].wait_recv()
-            out = hr[l, rows, :] + y[rows, :] + ml_r[l, rows, :].astype(F32)
-            if l == 0:
-                sent = out.astype(BF16)
-                r[1, rows, :] = sent
-                normed_block(1, blk, blk, sent.astype(F32))
-                if blk == 0:
-                    @pl.when(core == 1)
-                    def _():
-                        loads[0].wait()
-                        loads[1].wait()
-                        v_fresh.wait()
-
-                    @pl.when(core == 0)
-                    def _():
-                        for cp in qk_push:
-                            cp.wait_recv()
-                own_products(1, blk)
-                value_products(1, pos(blk))
-            else:
-                y[rows, :] = out
-                yb[rows, :] = out.astype(BF16)
+            at_core(core == 1, loads[0:2] + [v_fresh], qk_push)
+            own_products(1, 0)
+            value_products(1, pos(0))
+        block_out(l, 1, mlps[1])
+        if l == 0:
+            own_products(1, 1)
+            value_products(1, pos(1))
+            at_core(core == 1, loads[2:5], rest_push)
+            save_weights(0)
+            save_weights(1)
         return sends + mlps
 
-    act_push = push(act.at[0], act_in_o, sems.one(), sems.one(), across)
-    gm_push = push(e.at[1], gm_in_o, sems.one(), sems.one(), across)
-    finish_layer_inputs(0)
-
-    @pl.when(core == 1)
-    def _():
-        far_push.start()
+    for turn in range(2):
+        arrivals(0, turn)
+    for turn in range(2):
+        foreign_products(0, turn)
 
     for cp in rest_push:
         cp.start()
     pair_sends = middle(0)
-
-    @pl.when(core == 1)
-    def _():
-        far_come.wait_recv()
-        fwd_push.start()
-        e_load.wait()
-
-    finish_layer_inputs(1)
-
-    @pl.when(core == 0)
-    def _():
-        fwd_come.wait_recv()
-        own_come.wait_recv()
-
-    when(jnp.logical_not(owner), gm_push.start)
     save(r, r_o)
+    arrivals(1, 0)
+    foreign_products(1, 0)
+
+    save(e.at[1], gy_o)
+    save(sm, sm_o)
     pair_sends += middle(1)
     save(y, y_o)
     save(yb, yb_o)
-    save(e.at[1], gy_o)
-    save(sm, sm_o)
-    for l in range(2):
-        wvt[l] = jnp.transpose(wv[l * core])
-        save(wqk.at[l], watt_o.at[l, pl.ds(0, D)])
-        save(wout.at[l], watt_o.at[l, pl.ds(D, H)])
-        save(wvt.at[l], watt_o.at[l, pl.ds(D + H, H)])
-    save(wfc, wfc_o)
-    save(wproj, wproj_o)
+
     def crossed():
-        act_push.wait_recv()
-        gm_push.wait_recv()
+        for cp in act_push + gm_push:
+            cp.wait_recv()
 
     def crossing():
-        act_push.wait_send()
-        gm_push.wait_send()
+        for cp in act_push + gm_push:
+            cp.wait_send()
 
     when(owner, crossed)
     when(jnp.logical_not(owner), crossing)
-    far_push.wait_send()
-    fwd_push.wait_send()
     own_push.wait_send()
-    for cp in qk_push + rest_push + pair_sends:
+    for cp in far_push + fwd_push + qk_push + rest_push + pair_sends:
         cp.wait_send()
 
     @pl.when(core == 0)
@@ -500,15 +537,15 @@
             S((2, R, FH), BF16), S((R, D), F32), S((R, D), BF16), S((2, T, D), BF16), S((2, 8, F), F32), S((2, 2 * D, D), BF16),
             S((2, D, FH), BF16), S((2, FH, D), BF16), S((R, FH), BF16), S((2, T, D), BF16), S((1, L), jnp.int32)]
     V = pltpu.VMEM
-    scratch = [V((2, 2, T, D), BF16), V((C, 1, T), jnp.int32), V((2, 8, F), F32), V((2, D, D), BF16), V((2, D, H), BF16),
+    scratch = [V((2, 2, T, D), BF16), V((C, 1, T), jnp.int32), V((2, 1, T), jnp.int32), V((2, 8, F), F32), V((2, D, D), BF16), V((2, D, H), BF16),
                V((2, H, D), BF16), V((2, D, FH), BF16), V((2, FH, D), BF16), V((2, L, D), BF16), V((2, R, H), BF16),
                V((2, L, H), BF16), V((2, L, H), BF16), V((2, R, H), BF16), V((2, R, 128), F32), V((2, R, D), BF16),
                V((2, R, D), F32), V((2, R, D), BF16), V((2, R, FH), BF16), V((2, R, FH), BF16), V((R, D), F32),
                V((R, D), BF16), V((2, H, D), BF16), V((R, L), F32), V((2, R, D), BF16), V((2, R, D), BF16), V((2, R, D), BF16), V((2, R, D), BF16),
-               pltpu.SemaphoreType.DMA((80 + 20 * N + 2 * C,))]
+               pltpu.SemaphoreType.DMA((90 + 16 * (N - 1) + 2 * (C - 1),))]
     return pl.pallas_call(
         functools.partial(forward_kernel, C, m, T, D, F),
-        in_specs=[HBM, HBM, VM, VM, VM, VM, HBM, HBM, HBM, VM, HBM, HBM],
+        in_specs=[HBM, VM, VM, VM, VM, VM, HBM, HBM, HBM, VM, HBM, HBM],
         out_specs=[HBM] * 20 + [VM],
         out_shape=outs,
         scratch_shapes=scratch,
@@ -519,47 +556,33 @@
 
 WHOLE, SIDED, SIDE_STEP = 0, 1, 2
 JOBS = ("P0", "P1", "P2", "F0", "F1", "F2", "O", "Q", "K", "V")
+PROJ_AT = (3, 3)
 POLLS = (
-    (),
-    (),
-    (),
-    (13,),
-    (),
-    (14, 13),
-    (15, 16),
-    (10, 11, 13, 14),
-    (12,),
-    (10, 15, 13, 11),
-    (16, 14),
-    (13,),
-    (),
-    (18, 17, 12, 10, 15, 19, 11),
-    (16, 14, 12, 15),
-    (18, 11, 10, 16),
-    (14, 12),
-    (15, 18, 16),
-    (19, 17, 3),
-    (18, 19, 17, 4, 3, 6),
-    (5,),
-    (0, 4, 18, 19, 17, 1),
-    (3, 5),
-    (2, 0),
-    (4, 19, 17, 3),
-    (6,),
-    (1, 3),
-    (8, 7, 5, 2, 0, 4, 6),
+    (), (), (113,), (), (), (), (), (114,), (), (13, 113, 115), (), (13,), (), (117,), (14, 113, 111, 114, 110),
+    (15, 112, 17, 13, 113, 14, 114), (10, 110), (11, 111, 115, 13), (14, 114), (), (113,),
+    (10, 103, 118, 110, 12, 112, 11), (14,), (13, 111, 114, 10, 15, 115), (12, 105, 112),
+    (11, 104, 111, 14, 15, 115, 18, 12, 112), (3, 116, 11), (15, 12), (118,), (), (5, 103, 101, 119, 115, 100, 4),
+    (18, 104, 102, 118, 3, 103, 16, 108, 15),
 )
-TAIL = (9, 1, 5, 2, 7, 8, 4, 0, 6, 9, 1, 5, 2, 7, 8, 6, 9, 7, 8, 9, 7, 8, 9)
+TAIL = (
+    19, 1, 0, 105, 18, 3, 4, 103, 116, 106, 2, 101, 104, 102, 5, 119, 118, 110, 105, 8,
+    108, 100, 3, 1, 4, 16, 101, 2, 103, 19, 107, 18, 109, 104, 5, 102, 10, 118, 0, 116,
+    6, 119, 105, 1, 8, 4, 3, 101, 2, 106, 104, 117, 18, 102, 16, 19, 116, 5, 7, 119,
+    105, 1, 4, 108, 100, 9, 109, 6, 2, 17, 107, 16, 116, 19, 5, 119, 8, 108, 117, 9,
+    106, 109, 7, 0, 100, 16, 19, 8, 108, 17, 117, 107, 0, 6, 106, 9, 109, 8, 17, 117,
+    7, 107, 6, 106, 9, 109, 17, 7, 107, 6, 9, 7,
+)
 
 
 class Job:
-    def __init__(self, env, buf, lead, cols, order, sided, land, credits, first_layer, active, earlier):
+    def __init__(self, env, buf, lead, cols, order, sided, land, credits, active, earlier, prior):
         self.env, self.buf, self.lead, self.cols = env, buf, lead, cols
-        self.sided, self.land, self.credits, self.first_layer, self.active = sided, land, credits, first_layer, active
+        self.sided, self.land, self.credits, self.active, self.prior = sided, land, credits, active, prior
+        self.copies = {}
         self.earlier = earlier
         self.bits = list(range(env.m - 2 if sided else env.m - 1, -1, -1))
-        self.fixed, self.z_done, self.steps, self.at = {}, False, [], 0
-        self.used = 0
+        self.fixed, self.z_done, self.steps, self.at, self.flying = {}, False, [], 0, False
+        self.used, self.own_sems = 0, []
         if sided == SIDE_STEP:
             self.steps.append(("side", None, None))
         for item in order:
@@ -606,45 +629,58 @@
     def bind(self, move, slot):
         send_if, src, to, recv_if, dst, source = move
         env = self.env
-        sem_s, sem_r = env.sems.one(), env.sems.one()
+        if self.prior is None:
+            sem_s, sem_r = env.sems.one(), env.sems.one()
+            self.own_sems.append((sem_s, sem_r))
+        else:
+            sem_s, sem_r = self.prior.own_sems[self.used]
         credit = self.credits.at[self.used]
         self.used += 1
         return send_if, src, to, recv_if, dst, source, slot, sem_s, sem_r, credit
 
     def send(self, i):
-        for send_if, src, to, recv_if, dst, source, slot, sem_s, sem_r, credit in self.plans[i]:
-            cp = push(self.buf.at[src], slot, sem_s, sem_r, to)
-
-            def go(cp=cp, credit=credit):
-                if not self.first_layer:
-                    when(self.earlier, lambda: pl.semaphore_wait(credit, 1))
+        for n, (send_if, src, to, recv_if, dst, source, slot, sem_s, sem_r, credit) in enumerate(self.plans[i]):
+            cp = self.copies[(i, n)] = push(self.buf.at[src], slot, sem_s, sem_r, to)
+
+            def go():
+                if self.prior is not None:
+                    def empty():
+                        pl.semaphore_wait(credit, 1)
+                        self.prior.copies[(i, n)].wait_send()
+
+                    when(self.earlier, empty)
                 cp.start()
 
             when(send_if, go)
-            self.env.sent.append((send_if, cp))
+            if self.prior is not None:
+                self.env.sent.append((send_if, cp))
 
     def take(self, i):
         for send_if, src, to, recv_if, dst, source, slot, sem_s, sem_r, credit in self.plans[i]:
             cp = push(slot, slot, sem_s, sem_r, to)
 
-            def got(cp=cp, dst=dst, slot=slot, credit=credit, source=source):
+            def got():
                 cp.wait_recv()
                 self.buf[dst] = self.buf[dst] + slot[...]
-                if self.first_layer:
+                if self.prior is None:
                     pl.semaphore_signal(credit, inc=1, device_id=source, device_id_type=MESH)
 
             when(recv_if, got)
 
-    def start(self):
-        self.send(0)
-
-    def advance(self):
-        if self.at >= len(self.steps):
-            return
-        self.take(self.at)
-        self.at += 1
-        if self.at < len(self.steps):
+    def send_next(self):
+        if not self.flying and self.at < len(self.steps):
             self.send(self.at)
+            self.flying = True
+
+    def take_next(self):
+        if self.flying:
+            self.take(self.at)
+            self.at, self.flying = self.at + 1, False
+
+    def finish(self):
+        while self.at < len(self.steps):
+            self.send_next()
+            self.take_next()
 
     def own(self):
         return self.view(self.fixed, self.env.z)
@@ -686,9 +722,9 @@
     return {
         "P0": ("gproj", (0, 3), ["z"] + rest, SIDED), "P1": ("gproj", (1, 3), rest + ["z"], SIDED),
         "P2": ("gproj", (2, 3), rest + ["z"], SIDED),
-        "F0": ("gfc", (0, 3), ["z"] + ys, WHOLE), "F1": ("gfc", (1, 3), xz, WHOLE), "F2": ("gfc", (2, 3), xz, WHOLE),
+        "F0": ("gfc", (0, 3), xs[:1] + ["z"] + xs[1:], WHOLE), "F1": ("gfc", (1, 3), xz, WHOLE), "F2": ("gfc", (2, 3), yz, WHOLE),
         "O": ("gout", (0, 1), rest + ["z"], SIDE_STEP),
-        "Q": ("gq", (0, 1), xz, WHOLE), "K": ("gk", (0, 1), yz, WHOLE), "V": ("gv", (0, 1), xz, WHOLE),
+        "Q": ("gq", (0, 1), xz, WHOLE), "K": ("gk", (0, 1), yz, WHOLE), "V": ("gv", (0, 1), yz, WHOLE),
     }
 
 
@@ -857,14 +893,12 @@
         earlier = True if name != "V" else core == 1
         active = True if l == 0 else earlier
         jobs[(name, l)] = Job(env, vm[buf], (l,), slice(at * width, (at + 1) * width), order, sided, vm["land"][name],
-                              credits[name], l == 1, active, earlier)
-        jobs[(name, l)].start()
-
-    def adv(l, *names):
-        if not fused:
-            return
-        for name in names:
-            jobs[(name, l)].advance()
+                              credits[name], active, earlier, jobs.get((name, 1)))
+
+    def move(code):
+        job = jobs.get((JOBS[code % 10], code // 10 % 10)) if fused else None
+        if job is not None:
+            job.send_next() if code >= 100 else job.take_next()
 
     gm, gp, go, ghh, wa, wfc = vm["gm"], vm["gp"], vm["go"], vm["ghh"], vm["wa"], vm["wfc"]
     sm, sg = vm["sm"], vm["sg"]
@@ -877,10 +911,35 @@
 
     def poll():
         for code in next(polls):
-            adv(code // 10, JOBS[code % 10])
+            move(code)
 
     def layer_back(l):
         again = []
+
+        def proj_phase():
+            def proj_grad():
+                if l == 1:
+                    act_push.wait_recv()
+                    gm_in_load.wait()
+                else:
+                    act_in_load.wait()
+                    gm_push.wait_recv()
+                third = D // 3
+                for n in range(3):
+                    cols = slice(n * third, (n + 1) * third)
+                    total = mm_tn(vm["act_in"][...], vm["gm_in"][l, :, :, cols].reshape(2 * T, third))
+                    for blk in range(2):
+                        total += mm_tn(vm["act"][blk * T : (blk + 1) * T, :], gm[blk, :, cols])
+                    put("gproj", l, cols, total)
+
+            need(("act", l))
+            when(top, proj_grad)
+            for n in range(3):
+                start("P%d" % n, l)
+            if l == 1:
+                load("act", 0)
+                when(top, act_in_load.start)
+
         need(("wproj", l), ("gp", l))
         bias_sum = None
         for blk in range(2):
@@ -912,7 +971,7 @@
             cols = slice(i * third, (i + 1) * third)
             put("gfc", l, cols, mm_tn(vm["hh"][...], gp[:, cols]))
             start("F%d" % i, l)
-        poll()
+            poll()
         if l == 1:
             load("hh", 0)
             load("gp", 0)
@@ -944,29 +1003,8 @@
         for i in range(pairs):
             attention_back_pair(i, T, L, vm["q"], vm["k"], vm["v"], vm["o"], vm["lse"], vm["goa"], vm["bias"], vm["dq"],
                                 vm["dk"], vm["dv"], l)
-            if i == 0:
-                def proj_grad():
-                    if l == 1:
-                        act_push.wait_recv()
-                        gm_in_load.wait()
-                    else:
-                        act_in_load.wait()
-                        gm_push.wait_recv()
-                    third = D // 3
-                    for n in range(3):
-                        cols = slice(n * third, (n + 1) * third)
-                        total = mm_tn(vm["act_in"][...], vm["gm_in"][l, :, :, cols].reshape(2 * T, third))
-                        for blk in range(2):
-                            total += mm_tn(vm["act"][blk * T : (blk + 1) * T, :], gm[blk, :, cols])
-                        put("gproj", l, cols, total)
-
-                need(("act", l))
-                when(top, proj_grad)
-                for n in range(3):
-                    start("P%d" % n, l)
-                if l == 1:
-                    load("act", 0)
-                    when(top, act_in_load.start)
+            if i == PROJ_AT[l]:
+                proj_phase()
             poll()
         if l == 1:
             for name in ("o", "q", "k", "v", "lse"):
@@ -1019,6 +1057,8 @@
         poll()
         put("gv", l, slice(0, H), mm_tn(xall[...], dv[l]))
         start("V", l)
+        if PROJ_AT[l] == 3:
+            proj_phase()
         poll()
         if l == 1:
             load("xall", 0)
@@ -1093,33 +1133,33 @@
 
     if fused:
         for at, code in enumerate(TAIL):
-            adv(code // 10, JOBS[code % 10])
-            if at % 4 == 3 and small_at[0] < len(around):
+            move(code)
+            if at % 8 == 7 and small_at[0] < len(around):
                 small_step()
         for job in jobs.values():
-            for _ in range(len(job.steps) - job.at):
-                job.advance()
+            job.finish()
     while small_at[0] < len(around):
         small_step()
     last = len(around)
-    small_o[...] = sv[last]
 
     if fused:
-        hand_over(core, sib, env, vm, jobs, m, D, H, FH, pushed, sv, last, outs)
+        hand_over(core, sib, env, vm, jobs, m, D, H, FH, pushed, sv, last)
+        results = list(zip(vm["stage"], outs[2:]))
     else:
-        leave = []
-        for name, out in zip(("gproj", "gfc", "gout", "gq", "gk", "gv"), outs[2:]):
-            leave.append(pltpu.make_async_copy(vm[name], out, sems.one()))
-            leave[-1].start()
-        for cp in leave:
-            cp.wait()
+        results = [(vm[name], out) for name, out in zip(("gproj", "gfc", "gout", "gq", "gk", "gv"), outs[2:])]
+    results.append((sv.at[last], small_o))
+    results = [pltpu.make_async_copy(src, dst, sems.one()) for src, dst in results]
+    for cp in results:
+        cp.start()
     finish_ends()
     for condition, cp in sent:
         when(condition, cp.wait_send)
-
-
-def hand_over(core, sib, env, vm, jobs, m, D, H, FH, pushed, sv, last, outs):
-    small_o, qkv_o, out_o, fc_o, proj_o, shared_o = outs[1:]
+    for cp in results:
+        cp.wait()
+
+
+def hand_over(core, sib, env, vm, jobs, m, D, H, FH, pushed, sv, last):
+    qkv_o, out_o, fc_o, proj_o, shared_o = vm["stage"]
     vm["fb_s"][...] = jnp.where(core == 0, sv[last, 5:6, :], sv[last, 4:5, :])
     fin = vm["fin"]
     top = env.bit(m - 1) == core
@@ -1172,7 +1212,7 @@
 
     when(core == 0, fresh_first)
     when(core == 1, fresh_second)
-    small_o[6:7, :] = fin["fb"][...]
+    sv[last, 6:7, :] = fin["fb"][...]
 
 
 def backward_pass(C, m, T, D, F, inputs):
@@ -1181,11 +1221,12 @@
     pairs = H // 128
     S, V = jax.ShapeDtypeStruct, pltpu.VMEM
     names = tuple(inputs)
-    outs = [S((1, 2, T, D), F32), S((8, FH), F32)]
+    outs, stage = [S((1, 2, T, D), F32), S((8, FH), F32)], []
     flat = {"gproj": (FH, D), "gfc": (D, FH), "gout": (H, D), "gq": (D, H), "gk": (D, H), "gv": (D, H)}
     if fused:
         outs += [S((1, D // J, 5 * H), F32), S((1, D // J, D), F32), S((1, D // J, F), F32), S((1, F // J, D), F32),
                  S((D // J, H), F32)]
+        stage = [V(out.shape, F32) for out in outs[2:]]
         grads = grad_shapes(C, m, D, F)
         land = {name: [V(shape, BF16) for shape in steps] for name, steps in landing_shapes(C, m, D, F).items()}
     else:
@@ -1203,16 +1244,17 @@
         sv=V((stages + 1, 8, FH), F32), sv_r=V((stages, 8, FH), F32), fb_s=V((1, FH), F32),
         fin=dict(fc=V((D // J, FH), BF16), q=V((D // J, H), BF16), k=V((D // J, H), BF16), v=V((D // J, H), BF16),
                  out=V((D // J, D), BF16), proj=V((F // J, D), BF16), fb=V((1, FH), F32)),
-        land=land, **{name: V((2,) + shape, BF16) for name, shape in grads.items()})
-    moves = 1 + m + 2 * (C - 1)
-    credits = {name: pltpu.SemaphoreType.REGULAR((moves,)) for name in job_table(m)} if fused else {}
+        land=land, stage=stage, **{name: V((2,) + shape, BF16) for name, shape in grads.items()})
+    moves = {name: len(order) - 1 + 2 * (C - 1) + (sided == SIDE_STEP) for name, (_, _, order, sided) in job_table(m).items()}
+    credits = {name: pltpu.SemaphoreType.REGULAR((n,)) for name, n in moves.items()} if fused else {}
+    semaphores = 60 + 2 * stages + 8 * (N - 1) + (20 + 2 * sum(moves.values()) if fused else 7)
     in_specs = [VM if name == "kseg" else HBM for name in names]
     return pl.pallas_call(
         functools.partial(backward_kernel, C, m, T, D, F, fused, names),
         in_specs=in_specs,
-        out_specs=[HBM, VM] + [VM if fused else HBM] * (len(outs) - 2),
+        out_specs=[HBM] * len(outs),
         out_shape=outs,
-        scratch_shapes=[vm, pltpu.SemaphoreType.DMA((120 + 40 * moves,)), credits],
+        scratch_shapes=[vm, pltpu.SemaphoreType.DMA((semaphores,)), credits],
         compiler_params=pltpu.CompilerParams(collective_id=1, has_side_effects=True, vmem_limit_bytes=VMEM_LIMIT),
         name="backward_pass",
     )(*inputs.values())
@@ -1259,21 +1301,65 @@
     half, FH = D // 2, F // 2
     names = ("xall", "q", "k", "v", "o", "lse", "r", "hr", "hh", "gp", "act", "y", "yb", "gy", "sm", "watt", "wfc", "wproj", "act_in", "gm_in", "kseg")
     kept = dict(zip(names, forward_pass(
-        C, m, ends, segment_ids.reshape(micros, 1, T), ln1_gain, ln1_bias, ln2_gain, ln2_bias, qkv_weight, out_weight,
+        C, m, ends, segment_ids, ln1_gain, ln1_bias, ln2_gain, ln2_bias, qkv_weight, out_weight,
         fc_weight, fc_bias, proj_weight, shared_weight)))
     block, small, *grads = backward_pass(C, m, T, D, F, kept)
-    if len(grads) == 5:
-        qkv_out, out_out, fc_out, proj_out, shared_out = grads
-        other_bias = small[6]
-    else:
-        qkv_out, out_out, fc_out, proj_out, shared_out = scattered(grads, core, m, half)
-        other_bias = swap(jnp.where(first, small[5], small[4]))
-    own_bias = jnp.where(first, small[4], small[5])
-    bias_grad = jnp.concatenate([jnp.where(first, own_bias, other_bias), jnp.where(first, other_bias, own_bias)])
+    if len(grads) != 5:
+        small = small.at[6].set(swap(jnp.where(first, small[5], small[4])))
+        grads = scattered(grads, core, m, half)
+    fcb_out, *ln, block, qkv_out, out_out, fc_out, proj_out, shared_out = assemble(small, J, C, D, F, [block, *grads])
+    return (block, qkv_out, out_out, fc_out, fcb_out, proj_out, shared_out, *ln)
+
+
+def assemble_kernel(J, C, D, F, small_in, *refs):
+    n = (len(refs) - 13) // 2
+    ins, small_outs, outs, bounce = refs[:n], refs[n : n + 5], refs[n + 5 : -8], refs[-8]
+    small, parts, dma = refs[-7], refs[-6:-1], refs[-1]
+    come = [pltpu.make_async_copy(a, b, dma.at[i]) for i, (a, b) in enumerate(zip(ins, bounce))]
+    first = pltpu.make_async_copy(small_in, small, dma.at[n])
+    for cp in [first] + come:
+        cp.start()
+    first.wait()
+    copies = []
+    core = lax.axis_index(SECTION)
     j = lax.axis_index(DP) * C + lax.axis_index(CTX)
-    fcb_out = lax.dynamic_slice_in_dim(bias_grad, j * (F // J), F // J, 0)
-    ln = lax.dynamic_slice_in_dim(small[:4], j * (D // J), D // J, 1)
-    return (block, qkv_out, out_out, fc_out, fcb_out[None], proj_out, shared_out, ln[0:1], ln[1:2], ln[2:3], ln[3:4])
+
+    def own_part(values):
+        width = values.shape[1] // J
+        at = lax.broadcasted_iota(jnp.int32, (values.shape[1], width), 0) - j * width
+        pick = (at == lax.broadcasted_iota(jnp.int32, (values.shape[1], width), 1)).astype(F32)
+        return jnp.dot(values, pick, precision=lax.Precision.HIGHEST, preferred_element_type=F32)
+
+    ours = jnp.where(core == 0, small[4:5, :], small[5:6, :])
+    theirs = small[6:7, :]
+    bias = jnp.concatenate([jnp.where(core == 0, ours, theirs), jnp.where(core == 0, theirs, ours)], axis=1)
+    parts[0][...] = own_part(jnp.broadcast_to(bias, (8, F)))[0:1, :]
+    norms = own_part(small[:, :D])
+    for i in range(4):
+        parts[1 + i][...] = norms[i : i + 1, :]
+    for i in range(5):
+        copies.append(pltpu.make_async_copy(parts[i], small_outs[i], dma.at[n + 1 + i]))
+        copies[-1].start()
+    for i in range(n):
+        come[i].wait()
+        copies.append(pltpu.make_async_copy(bounce[i], outs[i], dma.at[i]))
+        copies[-1].start()
+    for cp in copies:
+        cp.wait()
+
+
+def assemble(small, J, C, D, F, arrays):
+    S = jax.ShapeDtypeStruct
+    return pl.pallas_call(
+        functools.partial(assemble_kernel, J, C, D, F),
+        in_specs=[HBM] * (1 + len(arrays)),
+        out_specs=[HBM] * (5 + len(arrays)),
+        out_shape=[S((1, F // J), F32)] + [S((1, D // J), F32)] * 4 + [S(a.shape, a.dtype) for a in arrays],
+        scratch_shapes=[[pltpu.VMEM(a.shape, a.dtype) for a in arrays], pltpu.VMEM(small.shape, F32), pltpu.VMEM((1, F // J), F32)] + [pltpu.VMEM((1, D // J), F32)] * 4
+        + [pltpu.SemaphoreType.DMA((len(arrays) + 6,))],
+        compiler_params=pltpu.CompilerParams(vmem_limit_bytes=VMEM_LIMIT),
+        name="assemble",
+    )(small, *arrays)
 
 
 def scattered(grads, core, m, half):

time: 229 us -> 203 us (0.89)
  Pallas kernels: 213 us -> 198 us
  local copies, waits for them, and re-layouts: 9.03 us -> 0 us
    pallas_call x1, Pallas kernels: 74.5 us -> 64.1 us  [forward_pass(): pl.pallas_call(functools.partial(forward_kernel, C, m, T, D, F), in_specs...]
    pallas_call x1, Pallas kernels: 139 us -> 130 us  [backward_pass(): pl.pallas_call(functools.partial(backward_kernel, C, m, T, D, F, fused, n...]
    unnamed x16 -> x0, local copies, waits for them, and re-layouts: 6.37 us -> none
    pallas_call x0 -> x1, Pallas kernels: none -> 4.6 us  [assemble(): pl.pallas_call(functools.partial(assemble_kernel, J, C, D, F), in_specs=[...]
where the time goes in v5:
time: 203 us; the launch traced here: 199 us
  Pallas kernels  198 us (98%)
    pallas_call x1, Pallas kernels, backward_pass(): pl.pallas_call(functools.partial(backward_kernel, C, m, T, D, F, fused, n...  130 us
    pallas_call x1, Pallas kernels, forward_pass(): pl.pallas_call(functools.partial(forward_kernel, C, m, T, D, F), in_specs...  64.1 us
    pallas_call x1, Pallas kernels, assemble(): pl.pallas_call(functools.partial(assemble_kernel, J, C, D, F), in_specs=[...  4.6 us

profile of v5, /device:TPU:1, one launch (start us, length us, event | category | flops | bytes accessed | tf_op | source)
XLA Modules:
  0.0 199.3 jit_solution(16870907655003971384)
XLA Ops:
  0.6 64.1 %forward_pass.1 = (bf16[2,1024,768]{2,1,0:T(8,128)(2,1)}, bf16[2,512,384]{2,1,0:T(8,128)(2,1)}, bf16[2,1024,384]{2,1,0:T(8,128)(2,1)}, bf16[2,1024,384]{2,1,0:T(...) custom-call(bf16[1,2,256,768]{3,2,1,0:T(8,128)(2,1)} %ends.1, ...), custom_call_target="tpu_custom_call" | custom-call | tf_op jit(solution)/shard_map/forward_pass/pallas_call | solution.py:546
  64.7 129.8 %backward_pass.1 = (f32[1,2,256,768]{3,2,1,0:T(8,128)}, f32[8,1536]{1,0:T(8,128)}, f32[1,48,1920]{2,1,0:T(8,128)}, f32[1,48,768]{2,1,0:T(8,128)}, f32[1,48,3072]...) custom-call(bf16[2,1024,768]{2,1,0:T(8,128)(2,1)} %get-tuple-element.50.refs_0_, ...), custom_call_target="tpu_custom_call" | custom-call | tf_op jit(solution)/shard_map/backward_pass/pallas_call | solution.py:1252
  194.5 4.6 %assemble.1 = (f32[1,192]{1,0:T(1,128)}, f32[1,48]{1,0:T(1,128)}, f32[1,48]{1,0:T(1,128)}, f32[1,48]{1,0:T(1,128)}, f32[1,48]{1,0:T(1,128)}, /*index=5*/f32[1,2,...) custom-call(f32[8,1536]{1,0:T(8,128)} %get-tuple-element.71.small_in, ...), custom_call_target="tpu_custom_call" | custom-call | tf_op jit(solution)/shard_map/assemble/pallas_call | solution.py:1353

commit v6 on v5

--- a/solution.py
+++ b/solution.py
@@ -75,31 +75,53 @@
     pl.semaphore_wait(barrier, len(peers))
 
 
-def attention_block(l, blk, T, keys, pairs, q, k, v, o, lse, bias):
-    rows = slice(blk * T, (blk + 1) * T)
+def attention_unit(first, l, blk, key_blocks, T, pairs, q, k, v, bias, acc, top_of, sum_of):
+    rows = pl.ds(pl.multiple_of(blk * T, T), T)
     lane = lax.broadcasted_iota(jnp.int32, (T, 128), 1)
+    blocks = [pl.ds(pl.multiple_of(at * T, T), T) for at in key_blocks]
+    mask = jnp.concatenate([bias[rows, pl.ds(pl.multiple_of(at * T, 128), T)] for at in key_blocks], axis=1)
 
     def body(i, carry):
         cols = pl.ds(pl.multiple_of(i * 128, 128), 128)
         q2 = q[l, rows, cols] * jnp.asarray(HEAD**-0.5, BF16)
-        k2 = k[l, :keys, cols]
-        v2 = jnp.concatenate([v[l, :keys, cols], jnp.ones((keys, 128), BF16)], axis=1)
-        outs, lses = [], []
+        k2 = jnp.concatenate([k[l, at, cols] for at in blocks], axis=0)
+        v2 = jnp.concatenate([v[l, at, cols] for at in blocks], axis=0)
+        v2 = jnp.concatenate([v2, jnp.ones_like(v2)], axis=1)
+        sums, tops = [], []
         for h in range(2):
             qh = jnp.where((lane >= 64) == (h == 1), q2, jnp.zeros_like(q2))
-            s = mm_nt(qh, k2) + bias[rows, :keys]
+            s = mm_nt(qh, k2) + mask
             top = jnp.max(s, axis=-1, keepdims=True)
-            e = jnp.exp(s - top).astype(BF16)
-            both = mm(e, v2)
-            total = both[:, 128:]
-            outs.append(both[:, :128] / total)
-            lses.append(top + jnp.log(total))
-        o[l, rows, cols] = jnp.where(lane < 64, outs[0], outs[1]).astype(BF16)
-        old = jnp.where(lane == 2 * i, lses[0], lse[l, rows, :])
-        lse[l, rows, :] = jnp.where(lane == 2 * i + 1, lses[1], old)
+            sums.append(mm(jnp.exp(s - top).astype(BF16), v2))
+            tops.append(top)
+        top = jnp.where(lane < 64, tops[0], tops[1])
+        total = jnp.where(lane < 64, sums[0][:, 128:], sums[1][:, 128:])
+        part = jnp.where(lane < 64, sums[0][:, :128], sums[1][:, :128])
+        if not first:
+            old = top_of[i, rows, :]
+            new = jnp.maximum(old, top)
+            keep, add = jnp.exp(old - new), jnp.exp(top - new)
+            total = keep * sum_of[i, rows, :] + add * total
+            part = keep * acc[i, rows, :] + add * part
+            top = new
+        top_of[i, rows, :] = top
+        sum_of[i, rows, :] = total
+        acc[i, rows, :] = part
         return carry
 
     lax.fori_loop(0, pairs, body, 0)
+
+
+def attention_end(l, blk, T, pairs, o, lse, acc, top_of, sum_of):
+    rows = slice(blk * T, (blk + 1) * T)
+    lane = lax.broadcasted_iota(jnp.int32, (T, 128), 1)
+    logs = jnp.zeros((T, 128), F32)
+    for i in range(pairs):
+        total = sum_of[i, rows, :]
+        o[l, rows, i * 128 : (i + 1) * 128] = (acc[i, rows, :] / total).astype(BF16)
+        log = top_of[i, rows, :] + jnp.log(total)
+        logs = jnp.where(lane == 2 * i, log[:, 0:1], jnp.where(lane == 2 * i + 1, log[:, 64:65], logs))
+    lse[l, rows, :] = logs
 
 
 def column(row_values):
@@ -113,7 +135,7 @@
                    xall_o, q_o, k_o, v_o, o_o, lse_o, r_o, hr_o, hh_o, gp_o, act_o, y_o, yb_o, gy_o, sm_o, watt_o, wfc_o, wproj_o,
                    act_in_o, gm_in_o, kseg_o,
                    e, seg, segv, sm, wqk, wv, wout, wfc, wproj, xall, q, k, v, o, lse, r, hr, hh, gp, act, y, yb, wvt, bias,
-                   br_s, br_r, ml_s, ml_r, dma):
+                   acc, top_of, sum_of, br_s, br_r, ml_s, ml_r, dma):
     core, dp, z = lax.axis_index(SECTION), lax.axis_index(DP), lax.axis_index(CTX)
     N, L, H, FH = C // 2, C * T, D // 2, F // 2
     T2 = T // 2
@@ -432,22 +454,40 @@
         save(wfc.at[l], wfc_o.at[l])
         save(wproj.at[l], wproj_o.at[l])
 
+    def unit(first, l, blk, key_blocks):
+        attention_unit(first, l, blk, key_blocks, T, pairs, q, k, v, bias, acc, top_of, sum_of)
+
     def middle(l):
-        attention_block(l, 0, T, L // 2, pairs, q, k, v, o, lse, bias)
+        unit(True, l, 0, [lo])
+        arrivals(l, 0)
+        unit(True, l, 1, [lo, hi])
+        if l == 0:
+            arrivals(0, 1)
+            for cp in rest_push:
+                cp.start()
+        foreign_products(l, 0)
+        if l == 1:
+            arrivals(1, 1)
+        else:
+            foreign_products(0, 1)
+        order = [(slo, lax.div(lo - slo + N - 1, N)) for slo in [src + row * (C - 1 - 2 * src) for src in behind]]
+        for slo, above in order:
+            unit(False, l, 1, [slo])
+        if l == 1:
+            foreign_products(1, 1)
+        for slo, above in order:
+            unit(False, l, 1 - above, [slo + (1 - above) * (C - 1 - 2 * slo)])
+        attention_end(l, 0, T, pairs, o, lse, acc, top_of, sum_of)
         if l == 0:
             at_core(core == 0, loads[2:3], rest_push[0:1])
-        else:
-            arrivals(1, 1)
-        sends = [branch(l, 0)]
-        if l == 1:
-            foreign_products(1, 1)
-        if l == 0:
+
             @pl.when(core == 1)
             def _():
                 for h in range(2):
                     far_come[h].wait_recv()
                     fwd_push[h].start()
-        attention_block(l, 1, T, L, pairs, q, k, v, o, lse, bias)
+        sends = [branch(l, 0)]
+        attention_end(l, 1, T, pairs, o, lse, acc, top_of, sum_of)
         sends.append(branch(l, 1))
         if l == 0:
             @pl.when(core == 0)
@@ -484,17 +524,9 @@
             save_weights(1)
         return sends + mlps
 
-    for turn in range(2):
-        arrivals(0, turn)
-    for turn in range(2):
-        foreign_products(0, turn)
-
-    for cp in rest_push:
-        cp.start()
+
     pair_sends = middle(0)
     save(r, r_o)
-    arrivals(1, 0)
-    foreign_products(1, 0)
 
     save(e.at[1], gy_o)
     save(sm, sm_o)
@@ -541,7 +573,8 @@
                V((2, H, D), BF16), V((2, D, FH), BF16), V((2, FH, D), BF16), V((2, L, D), BF16), V((2, R, H), BF16),
                V((2, L, H), BF16), V((2, L, H), BF16), V((2, R, H), BF16), V((2, R, 128), F32), V((2, R, D), BF16),
                V((2, R, D), F32), V((2, R, D), BF16), V((2, R, FH), BF16), V((2, R, FH), BF16), V((R, D), F32),
-               V((R, D), BF16), V((2, H, D), BF16), V((R, L), F32), V((2, R, D), BF16), V((2, R, D), BF16), V((2, R, D), BF16), V((2, R, D), BF16),
+               V((R, D), BF16), V((2, H, D), BF16), V((R, L), F32), V((pairs, R, 128), F32), V((pairs, R, 128), F32),
+               V((pairs, R, 128), F32), V((2, R, D), BF16), V((2, R, D), BF16), V((2, R, D), BF16), V((2, R, D), BF16),
                pltpu.SemaphoreType.DMA((90 + 16 * (N - 1) + 2 * (C - 1),))]
     return pl.pallas_call(
         functools.partial(forward_kernel, C, m, T, D, F),
@@ -555,22 +588,24 @@
 
 
 WHOLE, SIDED, SIDE_STEP = 0, 1, 2
+SMALL = 200
 JOBS = ("P0", "P1", "P2", "F0", "F1", "F2", "O", "Q", "K", "V")
 PROJ_AT = (3, 3)
 POLLS = (
-    (), (), (113,), (), (), (), (), (114,), (), (13, 113, 115), (), (13,), (), (117,), (14, 113, 111, 114, 110),
-    (15, 112, 17, 13, 113, 14, 114), (10, 110), (11, 111, 115, 13), (14, 114), (), (113,),
-    (10, 103, 118, 110, 12, 112, 11), (14,), (13, 111, 114, 10, 15, 115), (12, 105, 112),
-    (11, 104, 111, 14, 15, 115, 18, 12, 112), (3, 116, 11), (15, 12), (118,), (), (5, 103, 101, 119, 115, 100, 4),
-    (18, 104, 102, 118, 3, 103, 16, 108, 15),
+    (), (), (113,), (), (), (), (), (), (), (115,), (), (), (), (13,), (113,), (), (116,), (), (), (), (15,),
+    (13, 117), (115, 112, 113), (), (13, 114, 113, 16, 17, 117), (110,), (), (), (13, 113), (15, 115),
+    (12, 112, 17, 117), (111,), (13,), (15, 115), (), (10, 110, 12, 112), (17, 116, 117), (), (15, 115, 14),
+    (10, 110, 114, 11, 111, 12, 112), (17, 118, 105, 15, 10, 110, 16, 116), (11, 111, 12, 10), (16, 116, 14, 114),
+    (11, 119), (), (16, 103, 14), (), (117,), (106,), (18, 111, 116, 5, 19, 114), (17, 118, 105), (11, 16),
+    (14, 119, 114), (),
 )
 TAIL = (
-    19, 1, 0, 105, 18, 3, 4, 103, 116, 106, 2, 101, 104, 102, 5, 119, 118, 110, 105, 8,
-    108, 100, 3, 1, 4, 16, 101, 2, 103, 19, 107, 18, 109, 104, 5, 102, 10, 118, 0, 116,
-    6, 119, 105, 1, 8, 4, 3, 101, 2, 106, 104, 117, 18, 102, 16, 19, 116, 5, 7, 119,
-    105, 1, 4, 108, 100, 9, 109, 6, 2, 17, 107, 16, 116, 19, 5, 119, 8, 108, 117, 9,
-    106, 109, 7, 0, 100, 16, 19, 8, 108, 17, 117, 107, 0, 6, 106, 9, 109, 8, 17, 117,
-    7, 107, 6, 106, 9, 109, 17, 7, 107, 6, 9, 7,
+    104, 3, 6, 14, 102, 18, 5, 118, 19, 119, 105, 200, 100, 19, 119, 103, 2, 102, 18, 118,
+    19, 119, 5, 105, 101, 2, 102, 4, 108, 18, 118, 0, 100, 19, 200, 5, 107, 105, 2, 18,
+    102, 3, 103, 0, 100, 200, 5, 109, 1, 101, 106, 2, 3, 103, 0, 100, 200, 7, 107, 104,
+    8, 1, 101, 3, 103, 0, 108, 6, 106, 7, 107, 9, 1, 101, 3, 109, 6, 106, 7, 107,
+    4, 104, 1, 6, 106, 8, 108, 7, 107, 4, 104, 9, 109, 6, 7, 8, 108, 4, 104, 9,
+    109, 8, 108, 4, 9, 109, 8, 9,
 )
 
 
@@ -589,6 +624,9 @@
             if item == "z":
                 for s in range(1, env.C):
                     self.steps.append(("z", s, dict(self.fixed)))
+                self.z_done = True
+            elif item == "d":
+                self.steps.append(("d", None, dict(self.fixed)))
                 self.z_done = True
             else:
                 self.steps.append(("bit", item, (dict(self.fixed), self.z_done)))
@@ -618,6 +656,11 @@
                           self.view({**fixed, what: mine}, zat), other))
             return [self.bind(move, self.land[i]) for move in moves]
         s, C, z = what, env.C, env.z
+        if kind == "d":
+            for n in range(1, C):
+                to, source = lax.rem(z + n, C), lax.rem(z + C - n, C)
+                moves.append((active, self.view(state, to), env.line(to), active, self.view(state, z), env.line(source)))
+            return [self.bind(move, self.land[i].at[n]) for n, move in enumerate(moves)]
         zm = C - 1 - z
         for side, (p, sign) in enumerate(((z, 1), (zm, -1))):
             out_at = z + sign * (C - s)
@@ -656,14 +699,20 @@
                 self.env.sent.append((send_if, cp))
 
     def take(self, i):
-        for send_if, src, to, recv_if, dst, source, slot, sem_s, sem_r, credit in self.plans[i]:
-            cp = push(slot, slot, sem_s, sem_r, to)
+        direct = self.steps[i][0] == "d"
+        groups = [self.plans[i]] if direct else [[plan] for plan in self.plans[i]]
+        for group in groups:
+            send_if, src, to, recv_if, dst = group[0][:5]
 
             def got():
-                cp.wait_recv()
-                self.buf[dst] = self.buf[dst] + slot[...]
+                total = self.buf[dst].astype(F32) if direct else self.buf[dst]
+                for _, _, to, _, _, source, slot, sem_s, sem_r, credit in group:
+                    push(slot, slot, sem_s, sem_r, to).wait_recv()
+                    total = total + slot[...].astype(total.dtype)
+                self.buf[dst] = total.astype(BF16)
                 if self.prior is None:
-                    pl.semaphore_signal(credit, inc=1, device_id=source, device_id_type=MESH)
+                    for _, _, _, _, _, source, _, _, _, credit in group:
+                        pl.semaphore_signal(credit, inc=1, device_id=source, device_id_type=MESH)
 
             when(recv_if, got)
 
@@ -720,11 +769,11 @@
     rest = list(range(m - 1))
     xz, yz = xs + ["z"], ys + ["z"]
     return {
-        "P0": ("gproj", (0, 3), ["z"] + rest, SIDED), "P1": ("gproj", (1, 3), rest + ["z"], SIDED),
+        "P0": ("gproj", (0, 3), rest + ["z"], SIDED), "P1": ("gproj", (1, 3), rest + ["z"], SIDED),
         "P2": ("gproj", (2, 3), rest + ["z"], SIDED),
-        "F0": ("gfc", (0, 3), xs[:1] + ["z"] + xs[1:], WHOLE), "F1": ("gfc", (1, 3), xz, WHOLE), "F2": ("gfc", (2, 3), yz, WHOLE),
+        "F0": ("gfc", (0, 3), xz, WHOLE), "F1": ("gfc", (1, 3), yz, WHOLE), "F2": ("gfc", (2, 3), xz, WHOLE),
         "O": ("gout", (0, 1), rest + ["z"], SIDE_STEP),
-        "Q": ("gq", (0, 1), xz, WHOLE), "K": ("gk", (0, 1), yz, WHOLE), "V": ("gv", (0, 1), yz, WHOLE),
+        "Q": ("gq", (0, 1), xs[:1] + ["z"] + xs[1:], WHOLE), "K": ("gk", (0, 1), yz, WHOLE), "V": ("gv", (0, 1), yz, WHOLE),
     }
 
 
@@ -753,6 +802,9 @@
                 zdim = []
                 for s in range(1, C):
                     steps.append(tuple([2] + [2] * len(lead) + tail))
+            elif item == "d":
+                zdim = []
+                steps.append(tuple([C - 1] + [2] * len(lead) + tail))
             else:
                 lead.pop(item)
                 steps.append(tuple([2] * len(lead) + zdim + tail))
@@ -951,9 +1003,18 @@
             gp[rows, :] = gu
             part = jnp.sum(gu.astype(F32), axis=0, keepdims=True)
             bias_sum = part if bias_sum is None else bias_sum + part
+            if blk == 0:
+                poll()
         sg[l, 4:5, :] = bias_sum
         load("watt", l, dst=wa)
         poll()
+        need(("hh", l))
+        third = FH // 3
+        for i in (0, 1, 2):
+            cols = slice(i * third, (i + 1) * third)
+            put("gfc", l, cols, mm_tn(vm["hh"][...], gp[:, cols]))
+            start("F%d" % i, l)
+            poll()
         need(("wfc", l))
         shares = []
         for blk in range(2):
@@ -962,16 +1023,10 @@
             ghh[rows, :] = part
             vm["a_s"][rows, :] = part.astype(BF16)
             shares.append(pushed(vm["a_s"].at[rows, :], vm["a_r"].at[rows, :], sib, until=[]))
+            poll()
         if l == 1:
             load("wfc", 0)
         poll()
-        need(("hh", l))
-        third = FH // 3
-        for i in (0, 1, 2):
-            cols = slice(i * third, (i + 1) * third)
-            put("gfc", l, cols, mm_tn(vm["hh"][...], gp[:, cols]))
-            start("F%d" % i, l)
-            poll()
         if l == 1:
             load("hh", 0)
             load("gp", 0)
@@ -989,6 +1044,7 @@
             low = total.astype(BF16)
             vm["gb"][rows, :] = low
             vm["goa"][rows, :] = mm_nt(low, wa[D : D + H, :]).astype(BF16)
+            poll()
             sums = (gain_sum, bias_sum) if sums is None else (sums[0] + gain_sum, sums[1] + bias_sum)
         sg[l, 2:3, :D] = sums[0]
         sg[l, 3:4, :D] = sums[1]
@@ -1028,6 +1084,7 @@
             dhi = C - 1 - dlo
             vm["fs_s"][n] = key_part(dlo + (1 - core) * (dhi - dlo)).astype(BF16)
             gives.append(pushed(vm["fs_s"].at[n], vm["fs_r"].at[n], sib, until=again))
+        poll()
         for n, node in enumerate(other_nodes):
             dlo = node + row * (C - 1 - 2 * node)
             keep = key_part(dlo + core * (C - 1 - 2 * dlo))
@@ -1038,6 +1095,7 @@
         for blk in range(2):
             rows = slice(blk * T, (blk + 1) * T)
             ghh[rows, :] = key_part(pos(blk)) + mm_nt(dq[rows, :], wa[:D, :H])
+            poll()
         for cp in shares:
             cp.wait_send()
         early = pl.ds(pl.multiple_of((1 - core) * T, T), T)
@@ -1068,6 +1126,7 @@
             ghh[late, :] += vm["fx_r"][l, n].astype(F32)
         vm["a_s"][late, :] = ghh[late, :].astype(BF16)
         shares.append(pushed(vm["a_s"].at[late, :], vm["b_r"].at[late, :], sib, until=again))
+        poll()
         for cp in shares:
             cp.wait_recv()
         sums = None
@@ -1079,6 +1138,7 @@
             go[rows, :] = total
             if l == 1:
                 gm[blk] = total.astype(BF16)
+            poll()
             sums = (gain_sum, bias_sum) if sums is None else (sums[0] + gain_sum, sums[1] + bias_sum)
         sg[l, 0:1, :D] = sums[0]
         sg[l, 1:2, :D] = sums[1]
@@ -1113,13 +1173,35 @@
     small_at = [0]
     small_cp = [pushed(sv.at[0], sv_r.at[0], around[0])]
 
+    last = len(around)
+
+    def bias_halves():
+        vm["fb_s"][...] = jnp.where(core == 0, sv[last, 5:6, :], sv[last, 4:5, :])
+        cp = pushed(vm["fb_s"], vm["fin"]["fb"], sib)
+        if not fused:
+            cp.wait_recv()
+            return
+        ours = jnp.where(core == 0, sv[last, 4:5, :], sv[last, 5:6, :])
+        j, J = dp * C + z, C << m
+        norms = own_part(sv[last, :, :D], j, J)
+        for i in range(4):
+            vm["parts"][1 + i][...] = norms[i : i + 1, :]
+        cp.wait_recv()
+        theirs = vm["fin"]["fb"][...]
+        bias = jnp.concatenate([jnp.where(core == 0, ours, theirs), jnp.where(core == 0, theirs, ours)], axis=1)
+        vm["parts"][0][...] = own_part(jnp.broadcast_to(bias, (8, F)), j, J)[0:1, :]
+
     def small_step():
         i = small_at[0]
+        if i == len(around):
+            return
         small_cp[0].wait_recv()
         sv[i + 1] = sv[i] + sv_r[i]
         small_at[0] += 1
         if i + 1 < len(around):
             small_cp[0] = pushed(sv.at[i + 1], sv_r.at[i + 1], around[i + 1])
+        else:
+            bias_halves()
 
     def finish_ends():
         when(core == 0, x_push.wait_recv)
@@ -1132,22 +1214,22 @@
         when(core == 1, y_keep.wait)
 
     if fused:
-        for at, code in enumerate(TAIL):
-            move(code)
-            if at % 8 == 7 and small_at[0] < len(around):
+        for code in TAIL:
+            if code == SMALL:
                 small_step()
+            else:
+                move(code)
         for job in jobs.values():
             job.finish()
     while small_at[0] < len(around):
         small_step()
-    last = len(around)
 
     if fused:
         hand_over(core, sib, env, vm, jobs, m, D, H, FH, pushed, sv, last)
-        results = list(zip(vm["stage"], outs[2:]))
+        results = list(zip(vm["stage"], outs[7:]))
     else:
-        results = [(vm[name], out) for name, out in zip(("gproj", "gfc", "gout", "gq", "gk", "gv"), outs[2:])]
-    results.append((sv.at[last], small_o))
+        results = [(vm[name], out) for name, out in zip(("gproj", "gfc", "gout", "gq", "gk", "gv"), outs[7:])]
+    results += [(sv.at[last], small_o)] + list(zip(vm["parts"], outs[2:7]))
     results = [pltpu.make_async_copy(src, dst, sems.one()) for src, dst in results]
     for cp in results:
         cp.start()
@@ -1160,7 +1242,6 @@
 
 def hand_over(core, sib, env, vm, jobs, m, D, H, FH, pushed, sv, last):
     qkv_o, out_o, fc_o, proj_o, shared_o = vm["stage"]
-    vm["fb_s"][...] = jnp.where(core == 0, sv[last, 5:6, :], sv[last, 4:5, :])
     fin = vm["fin"]
     top = env.bit(m - 1) == core
     own = lambda name, l: (l,) + jobs[(name, 0)].own()[1:]
@@ -1169,7 +1250,6 @@
         pushed(vm["gq"].at[own("Q", 1 - core)], fin["q"], sib),
         pushed(vm["gk"].at[own("K", 1 - core)], fin["k"], sib),
         pushed(vm["gv"].at[own("V", 0)], fin["v"], sib),
-        pushed(vm["fb_s"], fin["fb"], sib),
     ]
     out_push = pushed(vm["gout"].at[own("O", 1 - core)], fin["out"], sib, top)
     proj_push = pushed(vm["gproj"].at[own("P0", 1 - core)[:-1]], fin["proj"], sib, top)
@@ -1212,7 +1292,6 @@
 
     when(core == 0, fresh_first)
     when(core == 1, fresh_second)
-    sv[last, 6:7, :] = fin["fb"][...]
 
 
 def backward_pass(C, m, T, D, F, inputs):
@@ -1221,12 +1300,12 @@
     pairs = H // 128
     S, V = jax.ShapeDtypeStruct, pltpu.VMEM
     names = tuple(inputs)
-    outs, stage = [S((1, 2, T, D), F32), S((8, FH), F32)], []
+    outs, stage = [S((1, 2, T, D), F32), S((8, FH), F32), S((1, F // J), F32)] + [S((1, D // J), F32)] * 4, []
     flat = {"gproj": (FH, D), "gfc": (D, FH), "gout": (H, D), "gq": (D, H), "gk": (D, H), "gv": (D, H)}
     if fused:
         outs += [S((1, D // J, 5 * H), F32), S((1, D // J, D), F32), S((1, D // J, F), F32), S((1, F // J, D), F32),
                  S((D // J, H), F32)]
-        stage = [V(out.shape, F32) for out in outs[2:]]
+        stage = [V(out.shape, F32) for out in outs[7:]]
         grads = grad_shapes(C, m, D, F)
         land = {name: [V(shape, BF16) for shape in steps] for name, steps in landing_shapes(C, m, D, F).items()}
     else:
@@ -1244,10 +1323,10 @@
         sv=V((stages + 1, 8, FH), F32), sv_r=V((stages, 8, FH), F32), fb_s=V((1, FH), F32),
         fin=dict(fc=V((D // J, FH), BF16), q=V((D // J, H), BF16), k=V((D // J, H), BF16), v=V((D // J, H), BF16),
                  out=V((D // J, D), BF16), proj=V((F // J, D), BF16), fb=V((1, FH), F32)),
-        land=land, stage=stage, **{name: V((2,) + shape, BF16) for name, shape in grads.items()})
-    moves = {name: len(order) - 1 + 2 * (C - 1) + (sided == SIDE_STEP) for name, (_, _, order, sided) in job_table(m).items()}
+        land=land, stage=stage, parts=[V(out.shape, F32) for out in outs[2:7]], **{name: V((2,) + shape, BF16) for name, shape in grads.items()})
+    moves = {name: len(order) - 1 + ("z" in order) * (C - 1) + C - 1 + (sided == SIDE_STEP) for name, (_, _, order, sided) in job_table(m).items()}
     credits = {name: pltpu.SemaphoreType.REGULAR((n,)) for name, n in moves.items()} if fused else {}
-    semaphores = 60 + 2 * stages + 8 * (N - 1) + (20 + 2 * sum(moves.values()) if fused else 7)
+    semaphores = 60 + 2 * stages + 8 * (N - 1) + (25 + 2 * sum(moves.values()) if fused else 14)
     in_specs = [VM if name == "kseg" else HBM for name in names]
     return pl.pallas_call(
         functools.partial(backward_kernel, C, m, T, D, F, fused, names),
@@ -1303,43 +1382,35 @@
     kept = dict(zip(names, forward_pass(
         C, m, ends, segment_ids, ln1_gain, ln1_bias, ln2_gain, ln2_bias, qkv_weight, out_weight,
         fc_weight, fc_bias, proj_weight, shared_weight)))
-    block, small, *grads = backward_pass(C, m, T, D, F, kept)
+    block, small, fcb_out, *rest = backward_pass(C, m, T, D, F, kept)
+    ln, grads = rest[:4], rest[4:]
     if len(grads) != 5:
-        small = small.at[6].set(swap(jnp.where(first, small[5], small[4])))
+        theirs = swap(jnp.where(first, small[5], small[4]))
+        ours = jnp.where(first, small[4], small[5])
+        bias = jnp.where(first, jnp.concatenate([ours, theirs]), jnp.concatenate([theirs, ours]))
+        j = lax.axis_index(DP) * C + lax.axis_index(CTX)
+        fcb_out = lax.dynamic_slice_in_dim(bias, j * (F // J), F // J, 0)[None]
+        ln = [lax.dynamic_slice_in_dim(small[i : i + 1, :D], j * (D // J), D // J, 1) for i in range(4)]
         grads = scattered(grads, core, m, half)
-    fcb_out, *ln, block, qkv_out, out_out, fc_out, proj_out, shared_out = assemble(small, J, C, D, F, [block, *grads])
+    block, fcb_out, *rest = assemble([block, fcb_out, *ln, *grads])
+    ln, (qkv_out, out_out, fc_out, proj_out, shared_out) = rest[:4], rest[4:]
     return (block, qkv_out, out_out, fc_out, fcb_out, proj_out, shared_out, *ln)
 
 
-def assemble_kernel(J, C, D, F, small_in, *refs):
-    n = (len(refs) - 13) // 2
-    ins, small_outs, outs, bounce = refs[:n], refs[n : n + 5], refs[n + 5 : -8], refs[-8]
-    small, parts, dma = refs[-7], refs[-6:-1], refs[-1]
+def own_part(values, j, J):
+    width = values.shape[1] // J
+    at = lax.broadcasted_iota(jnp.int32, (values.shape[1], width), 0) - j * width
+    pick = (at == lax.broadcasted_iota(jnp.int32, (values.shape[1], width), 1)).astype(F32)
+    return jnp.dot(values, pick, precision=lax.Precision.HIGHEST, preferred_element_type=F32)
+
+
+def assemble_kernel(*refs):
+    n = (len(refs) - 2) // 2
+    ins, outs, bounce, dma = refs[:n], refs[n:-2], refs[-2], refs[-1]
     come = [pltpu.make_async_copy(a, b, dma.at[i]) for i, (a, b) in enumerate(zip(ins, bounce))]
-    first = pltpu.make_async_copy(small_in, small, dma.at[n])
-    for cp in [first] + come:
+    for cp in come:
         cp.start()
-    first.wait()
     copies = []
-    core = lax.axis_index(SECTION)
-    j = lax.axis_index(DP) * C + lax.axis_index(CTX)
-
-    def own_part(values):
-        width = values.shape[1] // J
-        at = lax.broadcasted_iota(jnp.int32, (values.shape[1], width), 0) - j * width
-        pick = (at == lax.broadcasted_iota(jnp.int32, (values.shape[1], width), 1)).astype(F32)
-        return jnp.dot(values, pick, precision=lax.Precision.HIGHEST, preferred_element_type=F32)
-
-    ours = jnp.where(core == 0, small[4:5, :], small[5:6, :])
-    theirs = small[6:7, :]
-    bias = jnp.concatenate([jnp.where(core == 0, ours, theirs), jnp.where(core == 0, theirs, ours)], axis=1)
-    parts[0][...] = own_part(jnp.broadcast_to(bias, (8, F)))[0:1, :]
-    norms = own_part(small[:, :D])
-    for i in range(4):
-        parts[1 + i][...] = norms[i : i + 1, :]
-    for i in range(5):
-        copies.append(pltpu.make_async_copy(parts[i], small_outs[i], dma.at[n + 1 + i]))
-        copies[-1].start()
     for i in range(n):
         come[i].wait()
         copies.append(pltpu.make_async_copy(bounce[i], outs[i], dma.at[i]))
@@ -1348,18 +1419,16 @@
         cp.wait()
 
 
-def assemble(small, J, C, D, F, arrays):
-    S = jax.ShapeDtypeStruct
+def assemble(arrays):
     return pl.pallas_call(
-        functools.partial(assemble_kernel, J, C, D, F),
-        in_specs=[HBM] * (1 + len(arrays)),
-        out_specs=[HBM] * (5 + len(arrays)),
-        out_shape=[S((1, F // J), F32)] + [S((1, D // J), F32)] * 4 + [S(a.shape, a.dtype) for a in arrays],
-        scratch_shapes=[[pltpu.VMEM(a.shape, a.dtype) for a in arrays], pltpu.VMEM(small.shape, F32), pltpu.VMEM((1, F // J), F32)] + [pltpu.VMEM((1, D // J), F32)] * 4
-        + [pltpu.SemaphoreType.DMA((len(arrays) + 6,))],
+        assemble_kernel,
+        in_specs=[HBM] * len(arrays),
+        out_specs=[HBM] * len(arrays),
+        out_shape=[jax.ShapeDtypeStruct(a.shape, a.dtype) for a in arrays],
+        scratch_shapes=[[pltpu.VMEM(a.shape, a.dtype) for a in arrays], pltpu.SemaphoreType.DMA((len(arrays),))],
         compiler_params=pltpu.CompilerParams(vmem_limit_bytes=VMEM_LIMIT),
         name="assemble",
-    )(small, *arrays)
+    )(*arrays)
 
 
 def scattered(grads, core, m, half):

time: 203 us -> 201 us (level)
  no operation moved by 1% of the time
where the time goes in v6:
time: 201 us; the launch traced here: 199 us
  Pallas kernels  198 us (99%)
    pallas_call x1, Pallas kernels, backward_pass(): pl.pallas_call(functools.partial(backward_kernel, C, m, T, D, F, fused, n...  132 us
    pallas_call x1, Pallas kernels, forward_pass(): pl.pallas_call(functools.partial(forward_kernel, C, m, T, D, F), in_specs...  62.9 us

profile of v6, /device:TPU:1, one launch (start us, length us, event | category | flops | bytes accessed | tf_op | source)
XLA Modules:
  0.0 198.6 jit_solution(5104326601799012246)
XLA Ops:
  0.6 62.9 %forward_pass.1 = (bf16[2,1024,768]{2,1,0:T(8,128)(2,1)}, bf16[2,512,384]{2,1,0:T(8,128)(2,1)}, bf16[2,1024,384]{2,1,0:T(8,128)(2,1)}, bf16[2,1024,384]{2,1,0:T(...) custom-call(bf16[1,2,256,768]{3,2,1,0:T(8,128)(2,1)} %ends.1, ...), custom_call_target="tpu_custom_call" | custom-call | tf_op jit(solution)/shard_map/forward_pass/pallas_call | solution.py:579
  63.5 131.7 %backward_pass.1 = (f32[1,2,256,768]{3,2,1,0:T(8,128)}, f32[8,1536]{1,0:T(8,128)}, f32[1,192]{1,0:T(1,128)}, f32[1,48]{1,0:T(1,128)}, f32[1,48]{1,0:T(1,128)}, /...) custom-call(bf16[2,1024,768]{2,1,0:T(8,128)(2,1)} %get-tuple-element, ...), custom_call_target="tpu_custom_call" | custom-call | tf_op jit(solution)/shard_map/backward_pass/pallas_call | solution.py:1331
  195.2 3.2 %assemble.1 = (f32[1,2,256,768]{3,2,1,0:T(8,128)}, f32[1,192]{1,0:T(1,128)}, f32[1,48]{1,0:T(1,128)}, f32[1,48]{1,0:T(1,128)}, f32[1,48]{1,0:T(1,128)}, /*index=...) custom-call(f32[1,2,256,768]{3,2,1,0:T(8,128)} %get-tuple-element.75, ...), custom_call_target="tpu_custom_call" | custom-call | tf_op jit(solution)/shard_map/assemble/pallas_call | solution.py:1423

commit v7 on v6

--- a/solution.py
+++ b/solution.py
@@ -459,9 +459,12 @@
 
     def middle(l):
         unit(True, l, 0, [lo])
-        arrivals(l, 0)
+        if l == 0:
+            arrivals(0, 0)
         unit(True, l, 1, [lo, hi])
-        if l == 0:
+        if l == 1:
+            arrivals(1, 0)
+        else:
             arrivals(0, 1)
             for cp in rest_push:
                 cp.start()

time: 201 us -> 201 us (level)
  no operation moved by 1% of the time
where the time goes in v7:
time: 201 us; the launch traced here: 199 us
  Pallas kernels  198 us (99%)
    pallas_call x1, Pallas kernels, backward_pass(): pl.pallas_call(functools.partial(backward_kernel, C, m, T, D, F, fused, n...  132 us
    pallas_call x1, Pallas kernels, forward_pass(): pl.pallas_call(functools.partial(forward_kernel, C, m, T, D, F), in_specs...  62.9 us

profile of v7, /device:TPU:1, one launch (start us, length us, event | category | flops | bytes accessed | tf_op | source)
XLA Modules:
  0.0 198.6 jit_solution(17764459744557499689)
XLA Ops:
  0.6 62.9 %forward_pass.1 = (bf16[2,1024,768]{2,1,0:T(8,128)(2,1)}, bf16[2,512,384]{2,1,0:T(8,128)(2,1)}, bf16[2,1024,384]{2,1,0:T(8,128)(2,1)}, bf16[2,1024,384]{2,1,0:T(...) custom-call(bf16[1,2,256,768]{3,2,1,0:T(8,128)(2,1)} %ends.1, ...), custom_call_target="tpu_custom_call" | custom-call | tf_op jit(solution)/shard_map/forward_pass/pallas_call | solution.py:582
  63.5 131.7 %backward_pass.1 = (f32[1,2,256,768]{3,2,1,0:T(8,128)}, f32[8,1536]{1,0:T(8,128)}, f32[1,192]{1,0:T(1,128)}, f32[1,48]{1,0:T(1,128)}, f32[1,48]{1,0:T(1,128)}, /...) custom-call(bf16[2,1024,768]{2,1,0:T(8,128)(2,1)} %get-tuple-element, ...), custom_call_target="tpu_custom_call" | custom-call | tf_op jit(solution)/shard_map/backward_pass/pallas_call | solution.py:1334
  195.2 3.2 %assemble.1 = (f32[1,2,256,768]{3,2,1,0:T(8,128)}, f32[1,192]{1,0:T(1,128)}, f32[1,48]{1,0:T(1,128)}, f32[1,48]{1,0:T(1,128)}, f32[1,48]{1,0:T(1,128)}, /*index=...) custom-call(f32[1,2,256,768]{3,2,1,0:T(8,128)} %get-tuple-element.75, ...), custom_call_target="tpu_custom_call" | custom-call | tf_op jit(solution)/shard_map/assemble/pallas_call | solution.py:1426
